TPU v7x, 256 devices: a whole 4x4x8 slice. The times are simulated.
256 devices in a mesh: wide: 32 (over z, x), narrow: 8 (over y, core).
Axes of the slice: x: 4, y: 4, z: 8, core: 2. Of those that a mesh axis runs over, the one named last changes fastest.
Arguments:
- integrals: bfloat16 [32, 64, 64, 8192], P('wide', None, None, 'narrow'), may hold values from -6 to 6
- occupied_coeffs: bfloat16 [4, 20480], P(None, 'wide'), may hold values from -0.75 to 0.75
- metric: bfloat16 [8192, 8192], P('narrow', 'wide'), may hold values from -0.125 to 0.125
- mu_block: int32 [32], P('wide'), may hold values from 0 to 319
- pair_count: int32 [32], P('wide'), may hold values from 8 to 64
- destination: int32 [1024], P('wide'), may hold values from 0 to 31, as said below
Outputs:
- placed: bfloat16 [2048, 8, 8192], P('wide', None, 'narrow')
Inputs may be any that keep to these rules, and one draw needn't show every extreme that they name: Among the 32 items of one wide device at most 2 name the same destination; in every draw one destination receives exactly 2 items from every wide device.
All inputs are finite; a program needn't handle non-finite values.
Results may differ from a plain program's by a relative error of at most 0.017.
Values may be sent and summed in bfloat16 or wider, within the bound.
No kernel may reach another device: no remote copies, remote signals or barrier semaphores. Data moves between devices by JAX's collectives and lax.ppermute only.
A program may use at most 128 MiB of HBM per device.

v0:
```python
import jax
import jax.numpy as jnp
from jax import lax
from jax.sharding import PartitionSpec as P


def transform_block(block_tile, coeff_all, first_block, live_count):
    block_width = block_tile.shape[0]
    coeff_block = lax.dynamic_slice_in_dim(coeff_all, first_block * block_width, block_width, 1)
    keep_mask = (jnp.arange(block_tile.shape[1], dtype=jnp.int32) < live_count)[None, :, None]
    block_tile = jnp.where(keep_mask, block_tile, jnp.zeros_like(block_tile))
    return jnp.einsum(
        "im,mnp->nip", coeff_block, block_tile, preferred_element_type=jnp.float32
    ).astype(jnp.bfloat16)


def slot_table(destination, peer_count, capacity):
    item_count = destination.shape[0]
    same_dest = destination[:, None] == destination[None, :]
    earlier = jnp.arange(item_count)[:, None] > jnp.arange(item_count)[None, :]
    slot_rank = jnp.sum((same_dest & earlier).astype(jnp.int32), axis=1)
    target = destination * capacity + slot_rank
    return (target[None, :] == jnp.arange(peer_count * capacity, dtype=jnp.int32)[:, None]).astype(
        jnp.bfloat16
    )


def per_device(integrals, occupied_coeffs, metric, mu_block, pair_count, destination):
    peer_count = lax.axis_size("wide")
    item_count = destination.shape[0]
    capacity = max(2, (2 * item_count + peer_count - 1) // peer_count)
    p_local = integrals.shape[3]
    coeff_all = lax.all_gather(occupied_coeffs, "wide", axis=1, tiled=True)
    halves = jax.vmap(transform_block, in_axes=(0, None, 0, 0))(
        integrals, coeff_all, mu_block, pair_count
    )
    item_rows = halves.shape[0] * halves.shape[1] * halves.shape[2] // item_count
    flat_items = halves.reshape(item_count, item_rows * p_local)
    placing = slot_table(destination, peer_count, capacity)
    metric_rows = lax.all_gather(metric, "wide", axis=1, tiled=True)
    outgoing = jnp.dot(placing, flat_items, preferred_element_type=jnp.float32).astype(jnp.bfloat16)
    arrived = lax.all_to_all(outgoing, "wide", split_axis=0, concat_axis=0, tiled=True)
    partial_terms = jnp.dot(
        arrived.reshape(-1, p_local), metric_rows, preferred_element_type=jnp.float32
    )
    summed = lax.psum_scatter(
        partial_terms.astype(jnp.bfloat16), "narrow", scatter_dimension=1, tiled=True
    )
    return summed.reshape(peer_count * capacity, item_rows, summed.shape[1])


def solution(mesh):
    placed = (
        P("wide", None, None, "narrow"),
        P(None, "wide"),
        P("narrow", "wide"),
        P("wide"),
        P("wide"),
        P("wide"),
    )
    return jax.shard_map(
        per_device, mesh=mesh, in_specs=placed, out_specs=P("wide", None, "narrow"), check_vma=False
    )
```

profile of v0, /device:TPU:18, one launch (start us, length us, event | category | flops | bytes accessed | tf_op | source)
XLA Modules:
  0.0 259.6 jit_solution(6116760855263988130)
XLA Ops:
  6.5 0.0 all-gather.2.cloned.1.call-start
  6.5 0.7 all-gather.2.cloned.1.call-update
  7.3 0.0 reduce-scatter.2.cloned.1.call-start
  8.6 49.3 %all_gather.6 = bf16[4,20480]{1,0:T(4,128)(2,1)S(1)} all-gather(bf16[4,640]{1,0:T(4,128)(2,1)} %param.7), channel_id=1, replica_groups=mesh['wide'=32,'narrow'=8] {'wide'}, dimensions={1}, use_global_device_ids=true | all-gather | bytes 168960 | tf_op jit(solution)/shard_map/all_gather | solution.py:33
  57.9 7.3 %select_bitcast_fusion = bf16[64,64,1024]{2,1,0:T(8,128)(2,1)} fusion(bf16[1,64,64,1024]{3,2,1,0:T(8,128)(2,1)} %param.6, pred[64]{0:T(512)(128)(4,1)S(1)} %iota_compare_fusion.3), kind=kLoop, calls=%fused_computation.4 | loop fusion | flops 4194304 | bytes 16777280 | tf_op jit(solution)/shard_map/reshape.2
  65.2 0.0 copy-start
  65.2 8.0 %fusion.5 = bf16[1,64,4,1024]{3,2,1,0:T(4,128)(2,1)S(1)} fusion(bf16[64,64,1024]{2,1,0:T(8,128)(2,1)} %select_bitcast_fusion, bf16[4,20480]{1,0:T(4,128)(2,1)S(1)} %all_gather.6, s32[]{:T(128)} %bitcast.2), kind=kOutput, calls=%fused_computation.6 | convolution fusion | flops 33816576 | bytes 8913924 | tf_op jit(solution)/shard_map/vmap(im,mnp->nip)/dot_general | solution.py:12
  73.2 0.4 reshape.36
  73.6 0.0 copy-done
  73.6 0.2 convert_reduce_fusion
  73.8 0.4 convolution_convert_fusion.1
  74.2 0.7 all_to_all.6
  74.9 36.3 %all_to_all.9 = bf16[32,2,8192]{2,1,0:T(2,128)(2,1)S(1)} all-to-all(bf16[32,2,8192]{2,1,0:T(2,128)(2,1)S(1)} %all_to_all.6), channel_id=1, replica_groups=mesh['wide'=32,'narrow'=8] {'wide'}, dimensions={0} | all-to-all | bytes 2097152 | tf_op jit(solution)/shard_map/all_to_all | solution.py:42
  111.2 0.8 reshape.37
  112.0 72.7 %all-gather.2.cloned.1.call-done = bf16[1024,8192]{1,0:T(8,128)(2,1)} async-done(((bf16[1024,256]{1,0:T(8,128)(2,1)}), bf16[1024,8192]{1,0:T(8,128)(2,1)}) %all-gather.2.cloned.1.call-update) | async-done | bytes 16777232 | tf_op jit(solution)/shard_map/all_gather | solution.py:40
  184.7 16.8 %convolution_convert_fusion = bf16[512,8192]{1,0:T(8,128)(2,1)} fusion(bf16[512,1024]{1,0:T(8,128)(2,1)S(1)} %reshape.37, bf16[1024,8192]{1,0:T(8,128)(2,1)} %all-gather.2.cloned.1.call-done), kind=kOutput, calls=%fused_computation | convolution fusion | flops 8594128896 | bytes 26214400 | tf_op jit(solution)/shard_map/dot_general | solution.py:43
  201.4 0.0 reduce-scatter.2.cloned.1.call-update
  201.5 51.3 %reduce-scatter.2.cloned.1.call-done = bf16[512,1024]{1,0:T(8,128)(2,1)} async-done(((bf16[512,8192]{1,0:T(8,128)(2,1)}), bf16[512,1024]{1,0:T(8,128)(2,1)}) %reduce-scatter.2.cloned.1.call-update) | async-done | bytes 1048592 | tf_op jit(solution)/shard_map/reduce_scatter | solution.py:46
  (2 shorter events, 0.0 us)
Async XLA Ops:
  6.5 178.1 %all-gather.2.cloned.1.call-start = ((), (), s32[]{:S(2)}) async-start(), calls=%async_computation.2 | async-start | bytes 17301504 | tf_op jit(solution)/shard_map/all_gather | solution.py:40
  7.3 245.5 %reduce-scatter.2.cloned.1.call-start = ((), (), s32[]{:S(2)}) async-start(), calls=%async_computation.3 | async-start | bytes 9437184 | tf_op jit(solution)/shard_map/reduce_scatter | solution.py:46
  65.2 8.4 %copy-start = (s32[32]{0:T(128)S(1)}, s32[32]{0:T(128)}, u32[]{:S(2)}) copy-start(s32[32]{0:T(128)} %param.11) | copy-start | bytes 388
Sparse Core Ops, SparseCore 0:
  9.8 174.8 all-gather.1
  201.6 51.1 reduce-scatter.1
where the time goes:
time: 263 us; the launch traced here: 260 us
  waiting for transfers between devices  125 us (48%)
  blocking collectives  85.6 us (33%)
  matrix products  25.2 us (10%)
  between operations  14.7 us (6%)
  other arithmetic  7.48 us (3%)
    all_gather x1, waiting for transfers between devices, per_device(): metric_rows = lax.all_gather(metric, 'wide', axis=1, tiled=True)  72.7 us
    reduce_scatter x1, waiting for transfers between devices, per_device(): lax.psum_scatter(partial_terms.astype(jnp.bfloat16), 'narrow', scatter_di...  51.3 us
    all_gather x1, blocking collectives, per_device(): coeff_all = lax.all_gather(occupied_coeffs, 'wide', axis=1, tiled=True)  49.3 us
    all_to_all x1, blocking collectives, per_device(): lax.all_to_all(outgoing, 'wide', split_axis=0, concat_axis=0, tiled=True)  36.3 us
    dot_general x1, matrix products, per_device(): jnp.dot(arrived.reshape(-1, p_local), metric_rows, preferred_element_type...  16.8 us
    dot_general x1, matrix products, transform_block(): jnp.einsum('im,mnp->nip', coeff_block, block_tile, preferred_element_type...  8.01 us
    another operation x1, other arithmetic  7.29 us
  transfers between devices with their start and end apart: 2, of which 2 were waited for; matrix products, arithmetic and copies ran while one was open for 7% of the time, Pallas kernels for 0%

commit v1 on v0

v1 whole, which is shorter than its diff:
```python
import jax
import jax.numpy as jnp
from jax import lax
from jax.sharding import Mesh, PartitionSpec as P


def small_gather(occupied_coeffs, destination):
    rows = occupied_coeffs.shape[0]
    packed = jnp.concatenate(
        [occupied_coeffs, destination.astype(jnp.bfloat16).reshape(rows, -1)], axis=1
    )
    gathered = lax.all_gather(packed, ("z", "x"), axis=0)
    width = occupied_coeffs.shape[1]
    coeffs = gathered[:, :, :width]
    dests = gathered[:, :, width:].reshape(gathered.shape[0], -1).astype(jnp.int32)
    return coeffs, dests


def half_transform(block, coeff_block, live_count):
    mu, nu, p = block.shape
    i = coeff_block.shape[0]
    ids = jnp.arange(nu, dtype=jnp.int32)
    same = (ids[:, None] == ids[None, :]) & (ids[:, None] < live_count)
    weights = jnp.where(
        same[:, None, None, :], coeff_block[None, :, :, None], jnp.zeros((), jnp.bfloat16)
    ).reshape(nu * i, mu * nu)
    return jnp.dot(
        weights, block.reshape(mu * nu, p), preferred_element_type=jnp.float32
    ).astype(jnp.bfloat16)


def per_device(integrals, occupied_coeffs, metric, mu_block, pair_count, destination):
    nz, nx = lax.axis_size("z"), lax.axis_size("x")
    peers = nz * nx
    item_count = destination.shape[0]
    cap = max(2, (2 * item_count + peers - 1) // peers)
    _, mu_width, nu, p_local = integrals.shape
    orbitals = occupied_coeffs.shape[0]
    item_rows = nu * orbitals // item_count

    metric_z = lax.all_gather(metric, "z", axis=0)
    coeffs, dests = small_gather(occupied_coeffs, destination)
    blocks_per = occupied_coeffs.shape[1] // mu_width
    first = mu_block[0]
    coeff_block = lax.dynamic_slice(
        coeffs, (first // blocks_per, 0, (first % blocks_per) * mu_width), (1, orbitals, mu_width)
    )[0]
    halves = half_transform(integrals[0], coeff_block, pair_count[0])
    items = lax.all_gather(halves, "x", axis=0, tiled=True)
    partial = jnp.einsum("rp,zpq->zrq", items, metric_z, preferred_element_type=jnp.float32).astype(
        jnp.bfloat16
    )
    summed = lax.psum_scatter(partial, ("y", "core"), scatter_dimension=0, tiled=False)
    q = summed.shape[-1]

    my_dests = lax.dynamic_slice_in_dim(dests, lax.axis_index("z") * nx, nx, 0)
    same = my_dests[:, :, None] == my_dests[:, None, :]
    ids = jnp.arange(item_count)
    rank = jnp.sum((same & (ids[:, None] > ids[None, :])).astype(jnp.int32), axis=2)
    target = my_dests * cap + rank
    placing = (
        target[:, None, :] == jnp.arange(peers * cap, dtype=jnp.int32)[None, :, None]
    ).astype(jnp.bfloat16)
    outgoing = jnp.einsum(
        "xsj,xjc->sxc",
        placing,
        summed.reshape(nx, item_count, item_rows * q),
        preferred_element_type=jnp.float32,
    ).astype(jnp.bfloat16)
    outgoing = outgoing.reshape(peers, cap, nx, item_rows, q)
    arrived = lax.all_to_all(outgoing, ("z", "x"), split_axis=0, concat_axis=0, tiled=True)
    arrived = arrived.reshape(nz, nx, cap, nx, item_rows, q).transpose(0, 3, 2, 4, 1, 5)
    return arrived.reshape(peers * cap, item_rows, nx * q)


def solution(mesh):
    n_narrow = mesh.shape["narrow"]
    grid = mesh.devices.reshape(8, 4, n_narrow // 2, 2)
    fine = Mesh(grid, ("z", "x", "y", "core"))
    wide, narrow = ("z", "x"), ("y", "core")
    placed = (
        P(wide, None, None, narrow),
        P(None, wide),
        P(narrow, wide),
        P(wide),
        P(wide),
        P(wide),
    )
    return jax.shard_map(
        per_device, mesh=fine, in_specs=placed, out_specs=P(wide, None, narrow), check_vma=False
    )
```

time: 263 us -> 257 us (0.977)
  matrix products: 25.2 us -> 16.3 us
  local copies, waits for them, and re-layouts: 1.91 us -> 8.9 us
  other arithmetic: 7.48 us -> 4.07 us
    reduce_scatter x1, waiting for transfers between devices: 51.3 us -> 34 us  [per_device(): lax.psum_scatter(partial, ('y', 'core'), scatter_dimension=0, tiled=False)]
    all_gather x1 -> x2, waiting for transfers between devices: 72.7 us -> 88.3 us  [the longest x1 57.6 us: per_device(): metric_z = lax.all_gather(metric, 'z', axis=0)]
    dot_general x3, matrix products: 25.2 us -> 16.3 us  [the longest x1 9.26 us: per_device(): jnp.einsum('rp,zpq->zrq', items, metric_z, preferred_element_type=jnp.flo...]
    another operation x1 -> x0, other arithmetic: 7.29 us -> none
    select_n x0 -> x1, local copies, waits for them, and re-layouts: none -> 5.66 us  [half_transform(): jnp.where(same[:, None, None, :], coeff_block[None, :, :, None], jnp.zero...]
  transfers between devices with their start and end apart: 2 -> 3, of which waited for: 2 -> 3; matrix products, arithmetic and copies ran while one was open for 7% -> 0% of each run, Pallas kernels for 0% -> 0%
where the time goes in v1:
time: 257 us; the launch traced here: 255 us
  waiting for transfers between devices  123 us (48%)
  blocking collectives  88 us (34%)
  matrix products  16.3 us (6%)
  between operations  14.5 us (6%)
  local copies, waits for them, and re-layouts  8.9 us (3%)
  other arithmetic  4.07 us (2%)
    all_gather x1, waiting for transfers between devices, per_device(): metric_z = lax.all_gather(metric, 'z', axis=0)  57.6 us
    all_gather x1, blocking collectives, small_gather(): gathered = lax.all_gather(packed, ('z', 'x'), axis=0)  49.3 us
    all_to_all x1, blocking collectives, per_device(): lax.all_to_all(outgoing, ('z', 'x'), split_axis=0, concat_axis=0, tiled=T...  38.7 us
    reduce_scatter x1, waiting for transfers between devices, per_device(): lax.psum_scatter(partial, ('y', 'core'), scatter_dimension=0, tiled=False)  34 us
    all_gather x1, waiting for transfers between devices, per_device(): items = lax.all_gather(halves, 'x', axis=0, tiled=True)  30.6 us
    dot_general x1, matrix products, per_device(): jnp.einsum('rp,zpq->zrq', items, metric_z, preferred_element_type=jnp.flo...  9.26 us
    dot_general x1, matrix products, half_transform(): jnp.dot(weights, block.reshape(mu * nu, p), preferred_element_type=jnp.fl...  6.5 us
    select_n x1, local copies, waits for them, and re-layouts, half_transform(): jnp.where(same[:, None, None, :], coeff_block[None, :, :, None], jnp.zero...  5.66 us
  transfers between devices with their start and end apart: 3, of which 3 were waited for; matrix products, arithmetic and copies ran while one was open for 0% of the time, Pallas kernels for 0%

profile of v1, /device:TPU:18, one launch (start us, length us, event | category | flops | bytes accessed | tf_op | source)
XLA Modules:
  0.0 254.9 jit_solution(3528279683402469364)
XLA Ops:
  7.9 0.7 convert_element_type.28
  8.5 0.1 reshape.79
  8.6 0.1 fusion.2
  8.7 0.7 maximum_bitcast_fusion
  9.4 49.3 %all-gather.2 = bf16[32,4,648]{2,1,0:T(4,128)(2,1)S(1)} all-gather(bf16[1,4,648]{2,1,0:T(4,128)(2,1)S(1)} %maximum_bitcast_fusion), channel_id=2, replica_groups=mesh['z'=8,'x'=4,'y'=4,'core'=2] {'z','x'}, dimensions={0}, use_global_device_ids=true | all-gather | bytes 171072 | tf_op jit(solution)/shard_map/all_gather | solution.py:12
  58.8 0.1 dynamic-slice_bitcast_fusion
  58.8 2.3 broadcast_select_fusion
  61.2 5.7 %select_n.39 = bf16[256,4096]{1,0:T(8,128)(2,1)S(1)} reshape(bf16[64,4,64,64]{3,2,1,0:T(8,128)(2,1)} %broadcast_select_fusion) | data formatting | bytes 4194304 | tf_op jit(solution)/shard_map/jit(_where)/select_n | solution.py:24
  66.8 6.5 %convolution_convert_fusion.1 = bf16[256,1024]{1,0:T(8,128)(2,1)} fusion(bf16[256,4096]{1,0:T(8,128)(2,1)S(1)} %select_n.39, bf16[4096,1024]{1,0:T(8,128)(2,1)} %bitcast.39), kind=kOutput, calls=%fused_computation.4 | convolution fusion | flops 2147745792 | bytes 11010048 | tf_op jit(solution)/shard_map/dot_general | solution.py:27
  73.4 0.7 all-gather.8.cloned.1.call-update
  74.2 30.6 %all-gather.6.cloned.1.call-done = bf16[1024,1024]{1,0:T(8,128)(2,1)} async-done(((bf16[256,1024]{1,0:T(8,128)(2,1)}), bf16[1024,1024]{1,0:T(8,128)(2,1)}) %all-gather.6.cloned.1.call-update) | async-done | bytes 2097168 | tf_op jit(solution)/shard_map/all_gather | solution.py:49
  104.8 57.6 %all-gather.8.cloned.1.call-done = bf16[8192,256]{1,0:T(8,128)(2,1)} async-done(((bf16[1024,256]{1,0:T(8,128)(2,1)}), bf16[8192,256]{1,0:T(8,128)(2,1)}) %all-gather.8.cloned.1.call-update) | async-done | bytes 4194320 | tf_op jit(solution)/shard_map/all_gather | solution.py:41
  162.4 9.3 %convert_bitcast_fusion = bf16[8,1024,256]{2,1,0:T(8,128)(2,1)} fusion(bf16[8,1024,256]{2,1,0:T(8,128)(2,1)} %bitcast.40, bf16[1024,1024]{1,0:T(8,128)(2,1)} %all-gather.6.cloned.1.call-done), kind=kOutput, calls=%fused_computation | convolution fusion | flops 4297064448 | bytes 10485760 | tf_op jit(solution)/shard_map/rp,zpq->zrq/dot_general | solution.py:50
  171.7 0.1 copy.27
  171.8 0.1 dynamic-slice_convert_fusion
  171.9 0.1 copy.28
  172.0 0.2 convert_reduce_fusion
  172.2 34.0 %reduce-scatter.2.cloned.1.call-done = bf16[1,1024,256]{2,1,0:T(8,128)(2,1)} async-done(((bf16[8,1024,256]{2,1,0:T(8,128)(2,1)}), bf16[1,1024,256]{2,1,0:T(8,128)(2,1)}) %reduce-scatter.2.cloned.1.call-update) | async-done | bytes 524304 | tf_op jit(solution)/shard_map/reduce_scatter | solution.py:53
  206.2 1.3 reshape_reduce_scatter.3
  207.5 0.6 convolution_convert_fusion
  208.1 0.3 copy.29
  208.4 0.1 copy.25
  208.5 38.7 %all_to_all.5 = bf16[32,2,4,8,256]{4,3,1,2,0:T(8,128)(2,1)S(1)} all-to-all(bf16[32,2,4,8,256]{4,3,1,2,0:T(8,128)(2,1)S(1)} %copy.25), channel_id=1, replica_groups=mesh['z'=8,'x'=4,'y'=4,'core'=2] {'z','x'}, dimensions={0} | all-to-all | bytes 2097152 | tf_op jit(solution)/shard_map/all_to_all | solution.py:71
  247.2 1.1 copy.26
  (10 shorter events, 0.2 us)
Async XLA Ops:
  6.5 98.2 %all-gather.6.cloned.1.call-start = ((), (), s32[]{:S(2)}) async-start(), calls=%async_computation.2 | async-start | bytes 2621440 | tf_op jit(solution)/shard_map/all_gather | solution.py:49
  73.4 89.1 %all-gather.8.cloned.1.call-start = ((), (), s32[]{:S(2)}) async-start(), calls=%async_computation.4 | async-start | bytes 4718592 | tf_op jit(solution)/shard_map/all_gather | solution.py:41
  74.1 132.1 %reduce-scatter.2.cloned.1.call-start = ((), (), s32[]{:S(2)}) async-start(), calls=%async_computation.3 | async-start | bytes 4718592 | tf_op jit(solution)/shard_map/reduce_scatter | solution.py:53
Sparse Core Ops, SparseCore 0:
  73.5 31.2 all-gather.5
  106.6 55.8 all-gather.7
  171.8 34.3 reduce-scatter.1

commit v2 on v0

v2 whole, which is shorter than its diff:
```python
import functools

import jax
import jax.numpy as jnp
from jax import lax
from jax.experimental import pallas as pl
from jax.experimental.pallas import tpu as pltpu
from jax.sharding import Mesh, PartitionSpec as P

BF = jnp.bfloat16
F32 = jnp.float32
VMEM_LIMIT = 48 * 1024 * 1024


def shift(size, step):
    return [(i, (i + step) % size) for i in range(size)]


def params():
    return pltpu.CompilerParams(vmem_limit_bytes=VMEM_LIMIT)


def halves_kernel(where, packed_ref, block_ref, out_ref, weight, *, nu, orbitals):
    width, group, p = block_ref.shape
    rows, depth = group * orbitals, width * group
    lanes, packs = packed_ref.shape[2], packed_ref.shape[1]

    def iota(shape, dim):
        return lax.broadcasted_iota(jnp.int32, shape, dim)

    def dot(left, right):
        return jnp.dot(left, right, preferred_element_type=F32)

    pick = iota((lanes, width), 0) == where[1] * width + iota((lanes, width), 1)
    chosen = dot(packed_ref[0], pick.astype(BF)).astype(BF)
    repeat = lax.rem(iota((rows, packs), 0), orbitals) == iota((rows, packs), 1)
    coeff = dot(repeat.astype(BF), chosen).astype(BF)
    spread = iota((width, depth), 0) == iota((width, depth), 1) // group
    wide = dot(coeff, spread.astype(BF))
    row_nu = iota((rows, depth), 0) // orbitals
    col_nu = lax.rem(iota((rows, depth), 1), group)
    live = pl.program_id(0) * group + row_nu < where[2]
    weight[...] = jnp.where((row_nu == col_nu) & live, wide, 0.0).astype(BF)
    out_ref[...] = dot(weight[...], block_ref[...].reshape(depth, p)).astype(BF)


def half_transform(where, packed, block, orbitals):
    mu, nu, p = block.shape
    group = 32
    rows = group * orbitals
    return pl.pallas_call(
        functools.partial(halves_kernel, nu=nu, orbitals=orbitals),
        grid_spec=pltpu.PrefetchScalarGridSpec(
            num_scalar_prefetch=1,
            grid=(nu // group,),
            in_specs=[
                pl.BlockSpec((1,) + packed.shape[1:], lambda s, w: (w[0], 0, 0)),
                pl.BlockSpec((mu, group, p), lambda s, w: (0, s, 0)),
            ],
            out_specs=pl.BlockSpec((rows, p), lambda s, w: (s, 0)),
            scratch_shapes=[pltpu.VMEM((rows, mu * group), BF)],
        ),
        out_shape=jax.ShapeDtypeStruct((nu * orbitals, p), BF),
        compiler_params=params(),
        cost_estimate=pl.CostEstimate(
            flops=2 * rows * mu * nu * p, bytes_accessed=2 * mu * nu * p, transcendentals=0
        ),
        name="halves",
    )(where, packed, block)


def product_kernel(order, *refs, items, pieces, steps, with_arrived):
    refs = list(refs)
    rows = [refs.pop(0) for _ in range(items)]
    blocks = [[refs.pop(0) for _ in range(n)] for n in pieces]
    arrived = [refs.pop(0) for _ in range(steps)] if with_arrived else None
    outs = [refs.pop(0) for _ in range(steps)]
    held, sems = refs

    def copies(step, block):
        at = 0
        for part, ref in enumerate(block):
            depth = ref.shape[0]
            yield pltpu.make_async_copy(ref, held.at[step, pl.ds(at, depth)], sems.at[step, part])
            at += depth

    for step in range(steps):
        for d, block in enumerate(blocks):

            @pl.when(order[step] == d)
            def _(step=step, block=block):
                for copy in copies(step, block):
                    copy.start()

    for step in range(steps):
        for d, block in enumerate(blocks):

            @pl.when(order[step] == d)
            def _(step=step, block=block):
                for copy in copies(step, block):
                    copy.wait()

        at = 0
        for piece in rows:
            count = piece.shape[0]
            value = jnp.dot(piece[...], held[step], preferred_element_type=F32)
            if with_arrived:
                value = value + arrived[step][at : at + count].astype(F32)
            outs[step][at : at + count] = value.astype(BF)
            at += count


def product(order, items, pieces, arrived, steps):
    rows = sum(piece.shape[0] for piece in items)
    depth, q = pieces[0][0].shape
    flat = [part for block in pieces for part in block]
    extra = list(arrived) if arrived is not None else []
    vmem = pl.BlockSpec(memory_space=pltpu.VMEM)
    return pl.pallas_call(
        functools.partial(
            product_kernel,
            items=len(items),
            pieces=tuple(len(block) for block in pieces),
            steps=steps,
            with_arrived=arrived is not None,
        ),
        in_specs=[pl.BlockSpec(memory_space=pltpu.SMEM)]
        + [vmem] * len(items)
        + [pl.BlockSpec(memory_space=pl.ANY)] * len(flat)
        + [vmem] * len(extra),
        out_specs=[vmem] * steps,
        out_shape=[jax.ShapeDtypeStruct((rows, q), BF)] * steps,
        scratch_shapes=[
            pltpu.VMEM((steps, depth, q), BF),
            pltpu.SemaphoreType.DMA((steps, 2)),
        ],
        compiler_params=pltpu.CompilerParams(vmem_limit_bytes=24 * 1024 * 1024),
        cost_estimate=pl.CostEstimate(
            flops=2 * rows * depth * q * steps,
            bytes_accessed=2 * (rows * depth + steps * (depth * q + rows * q)),
            transcendentals=0,
        ),
        name="product",
    )(order, *items, *flat, *extra)


def place_kernel(dests, *refs, sources, count, cap):
    *terms, out, total, used = refs
    value = terms[0][...].astype(F32)
    for term in terms[1:]:
        value = value + term[...].astype(F32)
    total[...] = value
    out[...] = jnp.zeros_like(out)
    peers = out.shape[0]
    rows = out.shape[2]
    for s in range(sources):

        @pl.loop(0, peers)
        def _(d):
            used[d] = 0

        @pl.loop(0, count)
        def _(j, s=s):
            d = dests[s * count + j]
            rank = used[d]
            used[d] = rank + 1
            start = pl.multiple_of((s * count + j) * rows, rows)
            out[d, s * cap + rank] = total[pl.ds(start, rows), :].astype(BF)


def place(dests, terms, peers, sources, count, cap, rows):
    q = terms[0].shape[1]
    shape = (peers, sources * cap, rows, q)
    return pl.pallas_call(
        functools.partial(place_kernel, sources=sources, count=count, cap=cap),
        grid_spec=pltpu.PrefetchScalarGridSpec(
            num_scalar_prefetch=1,
            grid=(1,),
            in_specs=[pl.BlockSpec(t.shape, lambda s, o: (0, 0)) for t in terms],
            out_specs=pl.BlockSpec(shape, lambda s, o: (0, 0, 0, 0)),
            scratch_shapes=[pltpu.VMEM(terms[0].shape, F32), pltpu.SMEM((peers,), jnp.int32)],
        ),
        out_shape=jax.ShapeDtypeStruct(shape, BF),
        compiler_params=params(),
        cost_estimate=pl.CostEstimate(
            flops=8 * terms[0].size, bytes_accessed=2 * (4 * terms[0].size + 2 * terms[0].size), transcendentals=0
        ),
        name="place",
    )(dests, *terms)


def final_kernel(*refs, offsets, cap):
    *parts, out = refs
    nx = parts[0].shape[0]
    q = parts[0].shape[3]
    for part, steps in zip(parts, offsets):
        for at, d in enumerate(steps):
            for x in range(nx):
                slot = ((x - d) % nx) * cap
                out[slot : slot + cap, :, x * q : (x + 1) * q] = part[x, at * cap : (at + 1) * cap]


def finish(parts, offsets, nz, nx, cap):
    peers, slots, rows, q = parts[0].shape
    return pl.pallas_call(
        functools.partial(final_kernel, offsets=offsets, cap=cap),
        grid=(nz,),
        in_specs=[pl.BlockSpec((nx, slots, rows, q), lambda s: (s, 0, 0, 0))] * len(parts),
        out_specs=pl.BlockSpec((nx * cap, rows, nx * q), lambda s: (s, 0, 0)),
        out_shape=jax.ShapeDtypeStruct((peers * cap, rows, nx * q), BF),
        compiler_params=params(),
        name="finish",
    )(*parts)


def per_device(integrals, occupied_coeffs, metric, mu_block, pair_count, destination):
    nz, nx, ny = lax.axis_size("z"), lax.axis_size("x"), lax.axis_size("y")
    peers = nz * nx
    count = destination.shape[0]
    cap = max(2, (2 * count + peers - 1) // peers)
    _, mu_width, nu, p_local = integrals.shape
    orbitals, local_width = occupied_coeffs.shape
    item_rows = nu * orbitals // count

    def hop(value, axis, size, step):
        return lax.ppermute(value, axis, shift(size, step))

    def after(value, *others):
        return lax.optimization_barrier((value,) + others)[0]

    mid = metric.shape[0] // 2
    up, down = [metric], [metric]
    for _ in range(nz // 2 - 1):
        up.append(hop(up[-1], "z", nz, 1))
        down.append(hop(down[-1], "z", nz, -1))
    far = (hop(up[-1][:mid], "z", nz, 1), hop(down[-1][mid:], "z", nz, -1))
    pieces = [(block,) for block in up] + [far] + [(block,) for block in down[:0:-1]]

    dest_row = jnp.pad(destination.astype(BF)[None], ((0, 8 - orbitals - 1), (0, local_width - count)))
    packed = jnp.concatenate([occupied_coeffs, dest_row], axis=0)
    packed = lax.all_to_all(
        jnp.broadcast_to(packed[None], (peers,) + packed.shape), ("z", "x"), 0, 0, tiled=True
    )
    blocks_per = local_width // mu_width
    where = jnp.stack([mu_block[0] // blocks_per, mu_block[0] % blocks_per, pair_count[0]])
    halves = half_transform(where, packed, integrals[0], orbitals)

    half = halves.shape[0] // 2
    ahead = hop(halves, "x", nx, 1)
    behind = hop(halves, "x", nx, -1)
    far_low = hop(ahead[:half], "x", nx, 1)
    far_high = hop(behind[half:], "x", nx, -1)
    items = (halves, ahead, behind, far_low, far_high)
    offsets = (0, 1, 3, 2)

    z, x, y, core = (lax.axis_index(name) for name in ("z", "x", "y", "core"))
    dests = packed[:, orbitals, :count].astype(jnp.int32)
    rows_of = jnp.concatenate(
        [lax.dynamic_index_in_dim(dests, z * nx + (x - d) % nx, 0, False) for d in offsets]
    )
    turns = ((2, 1), (3, 0))

    def order_of(turn, owner_core):
        return jnp.stack([(z - 2 * ((y + k) % ny) - owner_core) % nz for k in turn]).astype(jnp.int32)

    swap = [(0, 1), (1, 0)]
    swapped = []
    for turn in turns:
        other = product(order_of(turn, 1 - core), items, pieces, None, len(turn))
        swapped.append([lax.ppermute(value, "core", swap) for value in other])
    terms = {}
    for turn, arrived in zip(turns, swapped):
        own = product(order_of(turn, core), items, pieces, arrived, len(turn))
        for k, value in zip(turn, own):
            terms[k] = hop(value, "y", ny, k) if k else value
    outgoing = place(
        rows_of, [terms[k] for k in range(ny)], peers, len(offsets), count, cap, item_rows
    )
    arrived = lax.all_to_all(outgoing, ("z", "x"), 0, 0, tiled=True)
    return finish([arrived], [offsets], nz, nx, cap)


def solution(mesh):
    grid = mesh.devices.reshape(8, 4, mesh.shape["narrow"] // 2, 2)
    fine = Mesh(grid, ("z", "x", "y", "core"))
    wide, narrow = ("z", "x"), ("y", "core")
    placed = (
        P(wide, None, None, narrow),
        P(None, wide),
        P(narrow, wide),
        P(wide),
        P(wide),
        P(wide),
    )
    return jax.shard_map(
        per_device, mesh=fine, in_specs=placed, out_specs=P(wide, None, narrow), check_vma=False
    )
```

time: 263 us -> 156 us (0.59)
  waiting for transfers between devices: 125 us -> 42 us
  blocking collectives: 85.6 us -> 35.9 us
  starting transfers between devices: 0.04 us -> 30.7 us
  Pallas kernels: 0 us -> 27.4 us
  matrix products: 25.2 us -> 0 us
  between operations: 14.7 us -> 1.46 us
  local copies, waits for them, and re-layouts: 1.91 us -> 13.2 us
  other arithmetic: 7.48 us -> 2.61 us
    all_gather x1 -> x0, waiting for transfers between devices: 72.7 us -> none  [per_device(): metric_rows = lax.all_gather(metric, 'wide', axis=1, tiled=True)]
    reduce_scatter x1 -> x0, waiting for transfers between devices: 51.3 us -> none  [per_device(): lax.psum_scatter(partial_terms.astype(jnp.bfloat16), 'narrow', scatter_di...]
    all_gather x1 -> x0, blocking collectives: 49.3 us -> none  [per_device(): coeff_all = lax.all_gather(occupied_coeffs, 'wide', axis=1, tiled=True)]
    ppermute x0 -> x19, waiting for transfers between devices: none -> 39 us  [the longest x15 39 us: hop(): return lax.ppermute(value, axis, shift(size, step))]
    pallas_call x0 -> x7, Pallas kernels: none -> 27.4 us  [the longest x4 15.5 us: product(): pl.pallas_call(functools.partial(product_kernel, items=len(items), pieces...]
    dot_general x3 -> x0, matrix products: 25.2 us -> none  [the longest x1 16.8 us: per_device(): jnp.dot(arrived.reshape(-1, p_local), metric_rows, preferred_element_type...]
    ppermute x0 -> x19, starting transfers between devices: none -> 22.9 us  [the longest x15 21 us: hop(): return lax.ppermute(value, axis, shift(size, step))]
    unnamed x2 -> x26, local copies, waits for them, and re-layouts: 0.01 us -> 9.58 us
  transfers between devices with their start and end apart: 2 -> 20, of which waited for: 2 -> 10; matrix products, arithmetic and copies ran while one was open for 7% -> 4% of each run, Pallas kernels for 0% -> 11%
where the time goes in v2:
time: 156 us; the launch traced here: 153 us
  waiting for transfers between devices  42 us (27%)
  blocking collectives  35.9 us (23%)
  starting transfers between devices  30.7 us (20%)
  Pallas kernels  27.4 us (18%)
  local copies, waits for them, and re-layouts  13.2 us (8%)
  other arithmetic  2.61 us (2%)
    ppermute x15, waiting for transfers between devices, hop(): return lax.ppermute(value, axis, shift(size, step))  39 us
    all_to_all x1, blocking collectives, per_device(): arrived = lax.all_to_all(outgoing, ('z', 'x'), 0, 0, tiled=True)  35.9 us
    ppermute x15, starting transfers between devices, hop(): return lax.ppermute(value, axis, shift(size, step))  21 us
    pallas_call x4, Pallas kernels, product(): pl.pallas_call(functools.partial(product_kernel, items=len(items), pieces...  15.5 us
    unnamed x26, local copies, waits for them, and re-layouts  9.58 us
    all_to_all x1, starting transfers between devices, per_device(): lax.all_to_all(jnp.broadcast_to(packed[None], (peers,) + packed.shape), (...  7.78 us
    pallas_call x1, Pallas kernels, half_transform(): pl.pallas_call(functools.partial(halves_kernel, nu=nu, orbitals=orbitals)...  5.15 us
    pallas_call x1, Pallas kernels, place(): pl.pallas_call(functools.partial(place_kernel, sources=sources, count=cou...  4.08 us
  transfers between devices with their start and end apart: 20, of which 10 were waited for; matrix products, arithmetic and copies ran while one was open for 4% of the time, Pallas kernels for 11%

profile of v2, /device:TPU:18, one launch (start us, length us, event | category | flops | bytes accessed | tf_op | source)
XLA Modules:
  0.0 153.3 jit_solution(12501006415091632509)
XLA Ops:
  0.0 5.9 %collective-permute-start.8 = (bf16[1024,256]{1,0:T(8,128)(2,1)}, bf16[1024,256]{1,0:T(8,128)(2,1)S(1)}, u32[]{:S(2)}, u32[]{:S(2)}) collective-permute-start(bf16[1024,256]{1,0:T(8,128)(2,1)} %refs_5_.7), channel_id=1, source_target_pairs={{0,224},{32,0},{64,32},{96,64},{128,96},{160,128},{192,160},{224,1... | collective-permute-start | bytes 1572872 | tf_op jit(solution)/shard_map/ppermute | solution.py:226
  8.0 7.8 %all-to-all-start = ((bf16[32,8,640]{2,1,0:T(8,128)(2,1)}), bf16[32,8,640]{2,1,0:T(8,128)(2,1)S(1)}, u32[]{:S(2)}, u32[]{:S(2)}) async-start(bf16[32,8,640]{2,1,0:T(8,128)(2,1)} %broadcast_in_dim.10), calls=%async_computation | async-start | bytes 655360 | tf_op jit(solution)/shard_map/all_to_all | solution.py:241
  15.8 5.5 %collective-permute-done.8.refs_13_ = bf16[1024,256]{1,0:T(8,128)(2,1)S(1)} collective-permute-done((bf16[1024,256]{1,0:T(8,128)(2,1)}, bf16[1024,256]{1,0:T(8,128)(2,1)S(1)}, u32[]{:S(2)}, u32[]{:S(2)}) %collective-permute-start.8) | collective-permute-done | bytes 524320 | tf_op jit(solution)/shard_map/ppermute | solution.py:226
  21.2 3.9 %collective-permute-start.9 = (bf16[1024,256]{1,0:T(8,128)(2,1)S(1)}, bf16[1024,256]{1,0:T(8,128)(2,1)}, u32[]{:S(2)}, u32[]{:S(2)}) collective-permute-start(bf16[1024,256]{1,0:T(8,128)(2,1)S(1)} %collective-permute-done.8.refs_13_), channel_id=1, source_target_pairs={{0,224},{32,0},{64,32},{96,64},{128,96},{160,128},{192,160},{224,1... | collective-permute-start | bytes 1572872 | tf_op jit(solution)/shard_map/ppermute | solution.py:226
  27.0 3.0 %all-to-all-done.packed_ref = bf16[32,8,640]{2,1,0:T(8,128)(2,1)S(1)} async-done(((bf16[32,8,640]{2,1,0:T(8,128)(2,1)}), bf16[32,8,640]{2,1,0:T(8,128)(2,1)S(1)}, u32[]{:S(2)}, u32[]{:S(2)}) %all-to-all-start) | async-done | bytes 327712 | tf_op jit(solution)/shard_map/all_to_all | solution.py:241
  30.1 5.1 %halves.1.refs_0_ = bf16[256,1024]{1,0:T(8,128)(2,1)S(1)} custom-call(s32[3]{0:T(128)S(1)} %pad_add_fusion.2.where, bf16[32,8,640]{2,1,0:T(8,128)(2,1)S(1)} %all-to-all-done.packed_ref, bf16[64,64,1024]{2,1,0:T(8,128)(2,1)} %bitcast.24), custom_call_target="tpu_custom_call" | custom-call | flops 1073741824 | bytes 8388608 | tf_op jit(solution)/shard_map/halves/pallas_call | solution.py:51
  36.8 1.2 collective-permute-start
  38.0 1.3 collective-permute-start.10
  40.0 7.1 %collective-permute-done.1.refs_2_ = bf16[256,1024]{1,0:T(8,128)(2,1)S(1)} collective-permute-done((bf16[256,1024]{1,0:T(8,128)(2,1)S(1)}, bf16[256,1024]{1,0:T(8,128)(2,1)S(1)}, u32[]{:S(2)}, u32[]{:S(2)}) %collective-permute-start.1) | collective-permute-done | bytes 524320 | tf_op jit(solution)/shard_map/ppermute | solution.py:226
  49.4 1.2 collective-permute-start.2
  51.3 2.1 %collective-permute-start.11 = (bf16[512,256]{1,0:T(8,128)(2,1)}, bf16[512,256]{1,0:T(8,128)(2,1)}, u32[]{:S(2)}, u32[]{:S(2)}) collective-permute-start(bf16[512,256]{1,0:T(8,128)(2,1)} %slice.24), channel_id=1, source_target_pairs={{0,224},{32,0},{64,32},{96,64},{128,96},{160,128},{192,160},{224,1... | collective-permute-start | bytes 786440 | tf_op jit(solution)/shard_map/ppermute | solution.py:226
  54.4 1.7 %collective-permute-done.2.refs_3_ = bf16[128,1024]{1,0:T(8,128)(2,1)} collective-permute-done((bf16[128,1024]{1,0:T(8,128)(2,1)}, bf16[128,1024]{1,0:T(8,128)(2,1)}, u32[]{:S(2)}, u32[]{:S(2)}) %collective-permute-start.2) | collective-permute-done | bytes 262176 | tf_op jit(solution)/shard_map/ppermute | solution.py:226
  56.1 1.9 %collective-permute-done.11.refs_10_ = bf16[512,256]{1,0:T(8,128)(2,1)} collective-permute-done((bf16[512,256]{1,0:T(8,128)(2,1)}, bf16[512,256]{1,0:T(8,128)(2,1)}, u32[]{:S(2)}, u32[]{:S(2)}) %collective-permute-start.11) | collective-permute-done | bytes 262176 | tf_op jit(solution)/shard_map/ppermute | solution.py:226
  58.0 4.1 %collective-permute-done.7.refs_9_ = bf16[512,256]{1,0:T(8,128)(2,1)} collective-permute-done((bf16[512,256]{1,0:T(8,128)(2,1)}, bf16[512,256]{1,0:T(8,128)(2,1)}, u32[]{:S(2)}, u32[]{:S(2)}) %collective-permute-start.7) | collective-permute-done | bytes 262176 | tf_op jit(solution)/shard_map/ppermute | solution.py:226
  64.2 3.5 %product.6 = (bf16[1024,256]{1,0:T(8,128)(2,1)}, bf16[1024,256]{1,0:T(8,128)(2,1)}) custom-call(s32[2]{0:T(128)S(1)} %get-tuple-element.26.order, bf16[256,1024]{1,0:T(8,128)(2,1)S(1)} %halves.1.refs_0_, bf16[256,1024]{1,0:T(8,128)(2,1)S(1)} %collective-permute-done.refs_1_, bf16[256,1024]{1,0:T(8,128)(2,1)S(1)} %collective-permute-done.1.refs_2_, ...), custom_call_target="tpu_custom_call" | custom-call | flops 1073741824 | bytes 4194304 | tf_op jit(solution)/shard_map/product/pallas_call | solution.py:119
  69.5 3.5 %product.4 = (bf16[1024,256]{1,0:T(8,128)(2,1)}, bf16[1024,256]{1,0:T(8,128)(2,1)}) custom-call(s32[2]{0:T(128)S(1)} %get-tuple-element.25.order, bf16[256,1024]{1,0:T(8,128)(2,1)S(1)} %halves.1.refs_0_, bf16[256,1024]{1,0:T(8,128)(2,1)S(1)} %collective-permute-done.refs_1_, bf16[256,1024]{1,0:T(8,128)(2,1)S(1)} %collective-permute-done.1.refs_2_, ...), custom_call_target="tpu_custom_call" | custom-call | flops 1073741824 | bytes 4194304 | tf_op jit(solution)/shard_map/product/pallas_call | solution.py:119
  76.4 4.0 %product.7 = (bf16[1024,256]{1,0:T(8,128)(2,1)}, bf16[1024,256]{1,0:T(8,128)(2,1)}) custom-call(s32[2]{0:T(128)S(1)} %pad_add_fusion.4.order, bf16[256,1024]{1,0:T(8,128)(2,1)S(1)} %halves.1.refs_0_, bf16[256,1024]{1,0:T(8,128)(2,1)S(1)} %collective-permute-done.refs_1_, bf16[256,1024]{1,0:T(8,128)(2,1)S(1)} %collective-permute-done.1.refs_2_, ...), custom_call_target="tpu_custom_call" | custom-call | flops 1073741824 | bytes 4194304 | tf_op jit(solution)/shard_map/product/pallas_call | solution.py:119
  80.4 2.0 %collective-permute-start.16 = (bf16[1024,256]{1,0:T(8,128)(2,1)}, bf16[1024,256]{1,0:T(8,128)(2,1)}, u32[]{:S(2)}, u32[]{:S(2)}) collective-permute-start(bf16[1024,256]{1,0:T(8,128)(2,1)} %get-tuple-element.18), channel_id=1, source_target_pairs={{0,2},{2,4},{4,6},{6,0},{1,3},{3,5},{5,7},{7,1},{8,10},{10,12},{12... | collective-permute-start | bytes 1572872 | tf_op jit(solution)/shard_map/ppermute | solution.py:226
  82.5 4.5 %product.5 = (bf16[1024,256]{1,0:T(8,128)(2,1)}, bf16[1024,256]{1,0:T(8,128)(2,1)S(1)}) custom-call(s32[2]{0:T(128)S(1)} %pad_add_fusion.1.order, bf16[256,1024]{1,0:T(8,128)(2,1)S(1)} %halves.1.refs_0_, bf16[256,1024]{1,0:T(8,128)(2,1)S(1)} %collective-permute-done.refs_1_, bf16[256,1024]{1,0:T(8,128)(2,1)S(1)} %collective-permute-done.1.refs_2_, ...), custom_call_target="tpu_custom_call" | custom-call | flops 1073741824 | bytes 4194304 | tf_op jit(solution)/shard_map/product/pallas_call | solution.py:119
  89.7 16.3 %collective-permute-done.16.refs_1_ = bf16[1024,256]{1,0:T(8,128)(2,1)} collective-permute-done((bf16[1024,256]{1,0:T(8,128)(2,1)}, bf16[1024,256]{1,0:T(8,128)(2,1)}, u32[]{:S(2)}, u32[]{:S(2)}) %collective-permute-start.16) | collective-permute-done | bytes 524320 | tf_op jit(solution)/shard_map/ppermute | solution.py:226
  106.1 1.7 %collective-permute-done.18.refs_3_ = bf16[1024,256]{1,0:T(8,128)(2,1)S(1)} collective-permute-done((bf16[1024,256]{1,0:T(8,128)(2,1)}, bf16[1024,256]{1,0:T(8,128)(2,1)S(1)}, u32[]{:S(2)}, u32[]{:S(2)}) %collective-permute-start.18) | collective-permute-done | bytes 524320 | tf_op jit(solution)/shard_map/ppermute | solution.py:226
  110.7 4.1 %place.1 = bf16[32,8,8,256]{3,2,1,0:T(8,128)(2,1)S(1)} custom-call(s32[128]{0:T(128)S(1)} %pad_add_fusion.dests, bf16[1024,256]{1,0:T(8,128)(2,1)S(1)} %copy-done.10, bf16[1024,256]{1,0:T(8,128)(2,1)} %collective-permute-done.16.refs_1_, bf16[1024,256]{1,0:T(8,128)(2,1)} %collective-permute-done.17.refs_2_, bf16[1024,256]{1,0:T(8,128)(2,1)S(1)} %copy-done.12), custom_call_target="tpu_custom_call" | custom-call | flops 2097152 | bytes 3145728 | tf_op jit(solution)/shard_map/place/pallas_call | solution.py:174
  114.8 35.9 %all_to_all.10.refs_0_ = bf16[32,8,8,256]{3,2,1,0:T(8,128)(2,1)S(1)} all-to-all(bf16[32,8,8,256]{3,2,1,0:T(8,128)(2,1)S(1)} %place.1), channel_id=1, replica_groups=mesh['z'=8,'x'=4,'y'=4,'core'=2] {'z','x'}, dimensions={0} | all-to-all | bytes 2097152 | tf_op jit(solution)/shard_map/all_to_all | solution.py:279
  150.6 2.7 %finish.1 = bf16[64,8,1024]{2,1,0:T(8,128)(2,1)} custom-call(bf16[32,8,8,256]{3,2,1,0:T(8,128)(2,1)S(1)} %all_to_all.10.refs_0_), custom_call_target="tpu_custom_call" | custom-call | tf_op jit(solution)/shard_map/finish/pallas_call | solution.py:205
  (64 shorter events, 22.0 us)
Async XLA Ops:
  0.0 62.1 %copy-start = (bf16[1024,256]{1,0:T(8,128)(2,1)S(1)}, bf16[1024,256]{1,0:T(8,128)(2,1)}, u32[]{:S(2)}) copy-start(bf16[1024,256]{1,0:T(8,128)(2,1)} %refs_5_.7) | copy-start | bytes 1572868
  0.0 21.2 %collective-permute-start.8 = (bf16[1024,256]{1,0:T(8,128)(2,1)}, bf16[1024,256]{1,0:T(8,128)(2,1)S(1)}, u32[]{:S(2)}, u32[]{:S(2)}) collective-permute-start(bf16[1024,256]{1,0:T(8,128)(2,1)} %refs_5_.7), channel_id=1, source_target_pairs={{0,224},{32,0},{64,32},{96,64},{128,96},{160,128},{192,160},{224,1... | collective-permute-start | bytes 1572872 | tf_op jit(solution)/shard_map/ppermute | solution.py:226
  5.9 19.8 %collective-permute-start.4 = (bf16[1024,256]{1,0:T(8,128)(2,1)}, bf16[1024,256]{1,0:T(8,128)(2,1)S(1)}, u32[]{:S(2)}, u32[]{:S(2)}) collective-permute-start(bf16[1024,256]{1,0:T(8,128)(2,1)} %refs_5_.7), channel_id=1, source_target_pairs={{0,32},{32,64},{64,96},{96,128},{128,160},{160,192},{192,224},{224... | collective-permute-start | bytes 1572872 | tf_op jit(solution)/shard_map/ppermute | solution.py:226
  8.0 22.1 %all-to-all-start = ((bf16[32,8,640]{2,1,0:T(8,128)(2,1)}), bf16[32,8,640]{2,1,0:T(8,128)(2,1)S(1)}, u32[]{:S(2)}, u32[]{:S(2)}) async-start(bf16[32,8,640]{2,1,0:T(8,128)(2,1)} %broadcast_in_dim.10), calls=%async_computation | async-start | bytes 655360 | tf_op jit(solution)/shard_map/all_to_all | solution.py:241
  21.2 16.8 %copy-start.1 = (bf16[1024,256]{1,0:T(8,128)(2,1)}, bf16[1024,256]{1,0:T(8,128)(2,1)S(1)}, u32[]{:S(2)}) copy-start(bf16[1024,256]{1,0:T(8,128)(2,1)S(1)} %collective-permute-done.8.refs_13_) | copy-start | bytes 1572868
  21.2 16.8 %collective-permute-start.9 = (bf16[1024,256]{1,0:T(8,128)(2,1)S(1)}, bf16[1024,256]{1,0:T(8,128)(2,1)}, u32[]{:S(2)}, u32[]{:S(2)}) collective-permute-start(bf16[1024,256]{1,0:T(8,128)(2,1)S(1)} %collective-permute-done.8.refs_13_), channel_id=1, source_target_pairs={{0,224},{32,0},{64,32},{96,64},{128,96},{160,128},{192,160},{224,1... | collective-permute-start | bytes 1572872 | tf_op jit(solution)/shard_map/ppermute | solution.py:226
  25.6 13.7 %copy-start.5 = (bf16[1024,256]{1,0:T(8,128)(2,1)}, bf16[1024,256]{1,0:T(8,128)(2,1)S(1)}, u32[]{:S(2)}) copy-start(bf16[1024,256]{1,0:T(8,128)(2,1)S(1)} %collective-permute-done.4.refs_6_) | copy-start | bytes 1572868
  25.6 13.7 %collective-permute-start.5 = (bf16[1024,256]{1,0:T(8,128)(2,1)S(1)}, bf16[1024,256]{1,0:T(8,128)(2,1)}, u32[]{:S(2)}, u32[]{:S(2)}) collective-permute-start(bf16[1024,256]{1,0:T(8,128)(2,1)S(1)} %collective-permute-done.4.refs_6_), channel_id=1, source_target_pairs={{0,32},{32,64},{64,96},{96,128},{128,160},{160,192},{192,224},{224... | collective-permute-start | bytes 1572872 | tf_op jit(solution)/shard_map/ppermute | solution.py:226
  36.0 11.2 %collective-permute-start.1 = (bf16[256,1024]{1,0:T(8,128)(2,1)S(1)}, bf16[256,1024]{1,0:T(8,128)(2,1)S(1)}, u32[]{:S(2)}, u32[]{:S(2)}) collective-permute-start(bf16[256,1024]{1,0:T(8,128)(2,1)S(1)} %halves.1.refs_0_), channel_id=1, source_target_pairs={{0,24},{8,0},{16,8},{24,16},{1,25},{9,1},{17,9},{25,17},{2,26},{10... | collective-permute-start | bytes 1572872 | tf_op jit(solution)/shard_map/ppermute | solution.py:226
  36.8 11.9 %collective-permute-start = (bf16[256,1024]{1,0:T(8,128)(2,1)S(1)}, bf16[256,1024]{1,0:T(8,128)(2,1)S(1)}, u32[]{:S(2)}, u32[]{:S(2)}) collective-permute-start(bf16[256,1024]{1,0:T(8,128)(2,1)S(1)} %halves.1.refs_0_), channel_id=1, source_target_pairs={{0,8},{8,16},{16,24},{24,0},{1,9},{9,17},{17,25},{25,1},{2,10},{10... | collective-permute-start | bytes 1572872 | tf_op jit(solution)/shard_map/ppermute | solution.py:226
  38.0 12.6 %collective-permute-start.10 = (bf16[1024,256]{1,0:T(8,128)(2,1)}, bf16[1024,256]{1,0:T(8,128)(2,1)S(1)}, u32[]{:S(2)}, u32[]{:S(2)}) collective-permute-start(bf16[1024,256]{1,0:T(8,128)(2,1)} %collective-permute-done.9.refs_12_), channel_id=1, source_target_pairs={{0,224},{32,0},{64,32},{96,64},{128,96},{160,128},{192,160},{224,1... | collective-permute-start | bytes 1572872 | tf_op jit(solution)/shard_map/ppermute | solution.py:226
  39.3 14.1 %collective-permute-start.6 = (bf16[1024,256]{1,0:T(8,128)(2,1)}, bf16[1024,256]{1,0:T(8,128)(2,1)S(1)}, u32[]{:S(2)}, u32[]{:S(2)}) collective-permute-start(bf16[1024,256]{1,0:T(8,128)(2,1)} %collective-permute-done.5.refs_7_), channel_id=1, source_target_pairs={{0,32},{32,64},{64,96},{96,128},{128,160},{160,192},{192,224},{224... | collective-permute-start | bytes 1572872 | tf_op jit(solution)/shard_map/ppermute | solution.py:226
  47.8 6.6 %collective-permute-start.3 = (bf16[128,1024]{1,0:T(8,128)(2,1)}, bf16[128,1024]{1,0:T(8,128)(2,1)S(1)}, u32[]{:S(2)}, u32[]{:S(2)}) collective-permute-start(bf16[128,1024]{1,0:T(8,128)(2,1)} %slice.22), channel_id=1, source_target_pairs={{0,24},{8,0},{16,8},{24,16},{1,25},{9,1},{17,9},{25,17},{2,26},{10... | collective-permute-start | bytes 786440 | tf_op jit(solution)/shard_map/ppermute | solution.py:226
  49.4 6.7 %collective-permute-start.2 = (bf16[128,1024]{1,0:T(8,128)(2,1)}, bf16[128,1024]{1,0:T(8,128)(2,1)}, u32[]{:S(2)}, u32[]{:S(2)}) collective-permute-start(bf16[128,1024]{1,0:T(8,128)(2,1)} %slice.21), channel_id=1, source_target_pairs={{0,8},{8,16},{16,24},{24,0},{1,9},{9,17},{17,25},{25,1},{2,10},{10... | collective-permute-start | bytes 786440 | tf_op jit(solution)/shard_map/ppermute | solution.py:226
  51.3 6.7 %collective-permute-start.11 = (bf16[512,256]{1,0:T(8,128)(2,1)}, bf16[512,256]{1,0:T(8,128)(2,1)}, u32[]{:S(2)}, u32[]{:S(2)}) collective-permute-start(bf16[512,256]{1,0:T(8,128)(2,1)} %slice.24), channel_id=1, source_target_pairs={{0,224},{32,0},{64,32},{96,64},{128,96},{160,128},{192,160},{224,1... | collective-permute-start | bytes 786440 | tf_op jit(solution)/shard_map/ppermute | solution.py:226
  54.2 7.9 %collective-permute-start.7 = (bf16[512,256]{1,0:T(8,128)(2,1)}, bf16[512,256]{1,0:T(8,128)(2,1)}, u32[]{:S(2)}, u32[]{:S(2)}) collective-permute-start(bf16[512,256]{1,0:T(8,128)(2,1)} %slice.23), channel_id=1, source_target_pairs={{0,32},{32,64},{64,96},{96,128},{128,160},{160,192},{192,224},{224... | collective-permute-start | bytes 786440 | tf_op jit(solution)/shard_map/ppermute | solution.py:226
  67.7 6.6 %collective-permute-start.14 = (bf16[1024,256]{1,0:T(8,128)(2,1)}, bf16[1024,256]{1,0:T(8,128)(2,1)}, u32[]{:S(2)}, u32[]{:S(2)}) collective-permute-start(bf16[1024,256]{1,0:T(8,128)(2,1)} %get-tuple-element.16), channel_id=1, source_target_pairs={{0,1},{1,0},{2,3},{3,2},{4,5},{5,4},{6,7},{7,6},{8,9},{9,8},{10,11... | collective-permute-start | bytes 1572872 | tf_op jit(solution)/shard_map/ppermute | solution.py:270
  67.9 6.4 %collective-permute-start.15 = (bf16[1024,256]{1,0:T(8,128)(2,1)}, bf16[1024,256]{1,0:T(8,128)(2,1)}, u32[]{:S(2)}, u32[]{:S(2)}) collective-permute-start(bf16[1024,256]{1,0:T(8,128)(2,1)} %get-tuple-element.17), channel_id=1, source_target_pairs={{0,1},{1,0},{2,3},{3,2},{4,5},{5,4},{6,7},{7,6},{8,9},{9,8},{10,11... | collective-permute-start | bytes 1572872 | tf_op jit(solution)/shard_map/ppermute | solution.py:270
  73.0 9.5 %collective-permute-start.12 = (bf16[1024,256]{1,0:T(8,128)(2,1)}, bf16[1024,256]{1,0:T(8,128)(2,1)}, u32[]{:S(2)}, u32[]{:S(2)}) collective-permute-start(bf16[1024,256]{1,0:T(8,128)(2,1)} %get-tuple-element.13), channel_id=1, source_target_pairs={{0,1},{1,0},{2,3},{3,2},{4,5},{5,4},{6,7},{7,6},{8,9},{9,8},{10,11... | collective-permute-start | bytes 1572872 | tf_op jit(solution)/shard_map/ppermute | solution.py:270
  74.0 8.5 %collective-permute-start.13 = (bf16[1024,256]{1,0:T(8,128)(2,1)}, bf16[1024,256]{1,0:T(8,128)(2,1)}, u32[]{:S(2)}, u32[]{:S(2)}) collective-permute-start(bf16[1024,256]{1,0:T(8,128)(2,1)} %get-tuple-element.14), channel_id=1, source_target_pairs={{0,1},{1,0},{2,3},{3,2},{4,5},{5,4},{6,7},{7,6},{8,9},{9,8},{10,11... | collective-permute-start | bytes 1572872 | tf_op jit(solution)/shard_map/ppermute | solution.py:270
  74.3 1.0 copy-start.4
  80.4 25.7 %collective-permute-start.16 = (bf16[1024,256]{1,0:T(8,128)(2,1)}, bf16[1024,256]{1,0:T(8,128)(2,1)}, u32[]{:S(2)}, u32[]{:S(2)}) collective-permute-start(bf16[1024,256]{1,0:T(8,128)(2,1)} %get-tuple-element.18), channel_id=1, source_target_pairs={{0,2},{2,4},{4,6},{6,0},{1,3},{3,5},{5,7},{7,1},{8,10},{10,12},{12... | collective-permute-start | bytes 1572872 | tf_op jit(solution)/shard_map/ppermute | solution.py:226
  82.4 23.6 %collective-permute-start.17 = (bf16[1024,256]{1,0:T(8,128)(2,1)}, bf16[1024,256]{1,0:T(8,128)(2,1)}, u32[]{:S(2)}, u32[]{:S(2)}) collective-permute-start(bf16[1024,256]{1,0:T(8,128)(2,1)} %get-tuple-element.19), channel_id=1, source_target_pairs={{0,4},{2,6},{4,0},{6,2},{1,5},{3,7},{5,1},{7,3},{8,12},{10,14},{12... | collective-permute-start | bytes 1572872 | tf_op jit(solution)/shard_map/ppermute | solution.py:226
  87.8 20.0 %collective-permute-start.18 = (bf16[1024,256]{1,0:T(8,128)(2,1)}, bf16[1024,256]{1,0:T(8,128)(2,1)S(1)}, u32[]{:S(2)}, u32[]{:S(2)}) collective-permute-start(bf16[1024,256]{1,0:T(8,128)(2,1)} %get-tuple-element.20), channel_id=1, source_target_pairs={{0,6},{2,0},{4,2},{6,4},{1,7},{3,1},{5,3},{7,5},{8,14},{10,8},{12,... | collective-permute-start | bytes 1572872 | tf_op jit(solution)/shard_map/ppermute | solution.py:226
  (9 other events, 8.6 us)

commit v3 on v2

--- a/solution.py
+++ b/solution.py
@@ -10,17 +10,18 @@
 BF = jnp.bfloat16
 F32 = jnp.float32
 VMEM_LIMIT = 48 * 1024 * 1024
+SMALL_LIMIT = 24 * 1024 * 1024
 
 
 def shift(size, step):
     return [(i, (i + step) % size) for i in range(size)]
 
 
-def params():
-    return pltpu.CompilerParams(vmem_limit_bytes=VMEM_LIMIT)
-
-
-def halves_kernel(where, packed_ref, block_ref, out_ref, weight, *, nu, orbitals):
+def params(limit=VMEM_LIMIT):
+    return pltpu.CompilerParams(vmem_limit_bytes=limit)
+
+
+def halves_kernel(where, packed_ref, block_ref, out_ref, weight, *, orbitals):
     width, group, p = block_ref.shape
     rows, depth = group * orbitals, width * group
     lanes, packs = packed_ref.shape[2], packed_ref.shape[1]
@@ -49,7 +50,7 @@
     group = 32
     rows = group * orbitals
     return pl.pallas_call(
-        functools.partial(halves_kernel, nu=nu, orbitals=orbitals),
+        functools.partial(halves_kernel, orbitals=orbitals),
         grid_spec=pltpu.PrefetchScalarGridSpec(
             num_scalar_prefetch=1,
             grid=(nu // group,),
@@ -69,13 +70,13 @@
     )(where, packed, block)
 
 
-def product_kernel(order, *refs, items, pieces, steps, with_arrived):
+def product_kernel(order, *refs, items, pieces, steps, adds, outs):
     refs = list(refs)
     rows = [refs.pop(0) for _ in range(items)]
     blocks = [[refs.pop(0) for _ in range(n)] for n in pieces]
-    arrived = [refs.pop(0) for _ in range(steps)] if with_arrived else None
-    outs = [refs.pop(0) for _ in range(steps)]
-    held, sems = refs
+    terms = [refs.pop(0) for _ in adds]
+    results = [refs.pop(0) for _ in outs]
+    held, sems, added, added_sems = refs
 
     def copies(step, block):
         at = 0
@@ -84,73 +85,104 @@
             yield pltpu.make_async_copy(ref, held.at[step, pl.ds(at, depth)], sems.at[step, part])
             at += depth
 
+    def each(step, act):
+        for d, block in enumerate(blocks):
+
+            @pl.when(order[step] == d)
+            def _(block=block):
+                for copy in copies(step, block):
+                    act(copy)
+
+    def added_copy(slot):
+        term = terms[slot] if adds[slot][0] is None else terms[slot].at[adds[slot][0]]
+        spot = added.at[slot, pl.ds(0, term.shape[0])]
+        return pltpu.make_async_copy(term, spot, added_sems.at[slot])
+
     for step in range(steps):
-        for d, block in enumerate(blocks):
-
-            @pl.when(order[step] == d)
-            def _(step=step, block=block):
-                for copy in copies(step, block):
-                    copy.start()
+        each(step, lambda copy: copy.start())
+        for slot, (_, wanted, _) in enumerate(adds):
+            if wanted == step:
+                added_copy(slot).start()
 
     for step in range(steps):
-        for d, block in enumerate(blocks):
-
-            @pl.when(order[step] == d)
-            def _(step=step, block=block):
-                for copy in copies(step, block):
-                    copy.wait()
-
+        each(step, lambda copy: copy.wait())
+        for slot, (_, wanted, _) in enumerate(adds):
+            if wanted == step:
+                added_copy(slot).wait()
         at = 0
         for piece in rows:
             count = piece.shape[0]
             value = jnp.dot(piece[...], held[step], preferred_element_type=F32)
-            if with_arrived:
-                value = value + arrived[step][at : at + count].astype(F32)
-            outs[step][at : at + count] = value.astype(BF)
+            for slot, (_, wanted, first) in enumerate(adds):
+                size = terms[slot].shape[-2]
+                if wanted == step and first <= at < first + size:
+                    value = value + added[slot, at - first : at - first + count].astype(F32)
+            for ref, places in zip(results, outs):
+                for wanted, lead, first in places:
+                    size = ref.shape[-2]
+                    if wanted == step and first <= at < first + size:
+                        spot = slice(at - first, at - first + count)
+                        if lead is None:
+                            ref[spot] = value.astype(BF)
+                        else:
+                            ref[lead, spot] = value.astype(BF)
             at += count
 
 
-def product(order, items, pieces, arrived, steps):
+def product(order, items, pieces, terms, shapes, outs):
     rows = sum(piece.shape[0] for piece in items)
     depth, q = pieces[0][0].shape
-    flat = [part for block in pieces for part in block]
-    extra = list(arrived) if arrived is not None else []
+    steps = order.shape[0]
+    flat = [
+        pltpu.with_memory_space_constraint(part, pltpu.HBM) for block in pieces for part in block
+    ]
+    hbm = pl.BlockSpec(memory_space=pltpu.HBM)
     vmem = pl.BlockSpec(memory_space=pltpu.VMEM)
+    slots = max(1, len(terms))
     return pl.pallas_call(
         functools.partial(
             product_kernel,
             items=len(items),
             pieces=tuple(len(block) for block in pieces),
             steps=steps,
-            with_arrived=arrived is not None,
+            adds=tuple(term[1:] for term in terms),
+            outs=outs,
         ),
         in_specs=[pl.BlockSpec(memory_space=pltpu.SMEM)]
         + [vmem] * len(items)
-        + [pl.BlockSpec(memory_space=pl.ANY)] * len(flat)
-        + [vmem] * len(extra),
-        out_specs=[vmem] * steps,
-        out_shape=[jax.ShapeDtypeStruct((rows, q), BF)] * steps,
+        + [hbm] * (len(flat) + len(terms)),
+        out_specs=[vmem] * len(shapes),
+        out_shape=[jax.ShapeDtypeStruct(shape, BF) for shape in shapes],
         scratch_shapes=[
             pltpu.VMEM((steps, depth, q), BF),
             pltpu.SemaphoreType.DMA((steps, 2)),
+            pltpu.VMEM((slots, rows if terms else 16, q), BF),
+            pltpu.SemaphoreType.DMA((slots,)),
         ],
-        compiler_params=pltpu.CompilerParams(vmem_limit_bytes=24 * 1024 * 1024),
+        compiler_params=params(SMALL_LIMIT),
         cost_estimate=pl.CostEstimate(
             flops=2 * rows * depth * q * steps,
             bytes_accessed=2 * (rows * depth + steps * (depth * q + rows * q)),
             transcendentals=0,
         ),
         name="product",
-    )(order, *items, *flat, *extra)
+    )(order, *items, *flat, *[term[0] for term in terms])
 
 
 def place_kernel(dests, *refs, sources, count, cap):
-    *terms, out, total, used = refs
-    value = terms[0][...].astype(F32)
-    for term in terms[1:]:
-        value = value + term[...].astype(F32)
+    *terms, out, total, used, held, sems = refs
+    copies = [
+        pltpu.make_async_copy(term, held.at[at], sems.at[at]) for at, term in enumerate(terms)
+    ]
+    for copy in copies:
+        copy.start()
+    out[...] = jnp.zeros_like(out)
+    for copy in copies:
+        copy.wait()
+    value = held[0].astype(F32)
+    for at in range(1, len(terms)):
+        value = value + held[at].astype(F32)
     total[...] = value
-    out[...] = jnp.zeros_like(out)
     peers = out.shape[0]
     rows = out.shape[2]
     for s in range(sources):
@@ -176,12 +208,17 @@
         grid_spec=pltpu.PrefetchScalarGridSpec(
             num_scalar_prefetch=1,
             grid=(1,),
-            in_specs=[pl.BlockSpec(t.shape, lambda s, o: (0, 0)) for t in terms],
+            in_specs=[pl.BlockSpec(memory_space=pltpu.HBM)] * len(terms),
             out_specs=pl.BlockSpec(shape, lambda s, o: (0, 0, 0, 0)),
-            scratch_shapes=[pltpu.VMEM(terms[0].shape, F32), pltpu.SMEM((peers,), jnp.int32)],
+            scratch_shapes=[
+                pltpu.VMEM(terms[0].shape, F32),
+                pltpu.SMEM((peers,), jnp.int32),
+                pltpu.VMEM((len(terms),) + terms[0].shape, BF),
+                pltpu.SemaphoreType.DMA((len(terms),)),
+            ],
         ),
         out_shape=jax.ShapeDtypeStruct(shape, BF),
-        compiler_params=params(),
+        compiler_params=params(SMALL_LIMIT),
         cost_estimate=pl.CostEstimate(
             flops=8 * terms[0].size, bytes_accessed=2 * (4 * terms[0].size + 2 * terms[0].size), transcendentals=0
         ),
@@ -189,28 +226,29 @@
     )(dests, *terms)
 
 
-def final_kernel(*refs, offsets, cap):
-    *parts, out = refs
-    nx = parts[0].shape[0]
-    q = parts[0].shape[3]
-    for part, steps in zip(parts, offsets):
-        for at, d in enumerate(steps):
+def final_kernel(part, out, *, offsets, nx, cap):
+    q = part.shape[3]
+    for z in range(part.shape[0] // nx):
+        for at, d in enumerate(offsets):
             for x in range(nx):
-                slot = ((x - d) % nx) * cap
-                out[slot : slot + cap, :, x * q : (x + 1) * q] = part[x, at * cap : (at + 1) * cap]
-
-
-def finish(parts, offsets, nz, nx, cap):
-    peers, slots, rows, q = parts[0].shape
+                slot = (z * nx + (x - d) % nx) * cap
+                out[slot : slot + cap, :, x * q : (x + 1) * q] = part[
+                    z * nx + x, at * cap : (at + 1) * cap
+                ]
+
+
+def finish(arrived, offsets, nx, cap):
+    peers, slots, rows, q = arrived.shape
+    steps = 2
     return pl.pallas_call(
-        functools.partial(final_kernel, offsets=offsets, cap=cap),
-        grid=(nz,),
-        in_specs=[pl.BlockSpec((nx, slots, rows, q), lambda s: (s, 0, 0, 0))] * len(parts),
-        out_specs=pl.BlockSpec((nx * cap, rows, nx * q), lambda s: (s, 0, 0)),
+        functools.partial(final_kernel, offsets=offsets, nx=nx, cap=cap),
+        grid=(steps,),
+        in_specs=[pl.BlockSpec((peers // steps, slots, rows, q), lambda s: (s, 0, 0, 0))],
+        out_specs=pl.BlockSpec((peers * cap // steps, rows, nx * q), lambda s: (s, 0, 0)),
         out_shape=jax.ShapeDtypeStruct((peers * cap, rows, nx * q), BF),
-        compiler_params=params(),
+        compiler_params=params(SMALL_LIMIT),
         name="finish",
-    )(*parts)
+    )(arrived)
 
 
 def per_device(integrals, occupied_coeffs, metric, mu_block, pair_count, destination):
@@ -225,9 +263,6 @@
     def hop(value, axis, size, step):
         return lax.ppermute(value, axis, shift(size, step))
 
-    def after(value, *others):
-        return lax.optimization_barrier((value,) + others)[0]
-
     mid = metric.shape[0] // 2
     up, down = [metric], [metric]
     for _ in range(nz // 2 - 1):
@@ -258,26 +293,53 @@
     rows_of = jnp.concatenate(
         [lax.dynamic_index_in_dim(dests, z * nx + (x - d) % nx, 0, False) for d in offsets]
     )
-    turns = ((2, 1), (3, 0))
-
     def order_of(turn, owner_core):
         return jnp.stack([(z - 2 * ((y + k) % ny) - owner_core) % nz for k in turn]).astype(jnp.int32)
 
+    rows, q = halves.shape[0] * nx, metric.shape[1]
+    near = rows // 2
     swap = [(0, 1), (1, 0)]
-    swapped = []
-    for turn in turns:
-        other = product(order_of(turn, 1 - core), items, pieces, None, len(turn))
-        swapped.append([lax.ppermute(value, "core", swap) for value in other])
-    terms = {}
-    for turn, arrived in zip(turns, swapped):
-        own = product(order_of(turn, core), items, pieces, arrived, len(turn))
-        for k, value in zip(turn, own):
-            terms[k] = hop(value, "y", ny, k) if k else value
+    first, second = product(
+        order_of((2, 0, 1, 3), 1 - core),
+        items,
+        pieces,
+        (),
+        ((2, rows, q), (2, rows, q)),
+        (((0, 0, 0), (1, 1, 0)), ((2, 0, 0), (3, 1, 0))),
+    )
+    first = lax.ppermute(first, "core", swap)
+    second = lax.ppermute(second, "core", swap)
+    low, high = product(
+        order_of((2,), core),
+        items,
+        pieces,
+        ((first, 0, 0, 0),),
+        ((near, q), (near, q)),
+        (((0, None, 0),), ((0, None, near),)),
+    )
+    low, high = hop(low, "y", ny, -1), hop(high, "y", ny, 1)
+    right, left = product(
+        order_of((1, 3), core),
+        items,
+        pieces,
+        ((second, 0, 0, 0), (second, 1, 1, 0), (high, None, 0, near), (low, None, 1, 0)),
+        ((rows, q), (rows, q)),
+        (((0, None, 0),), ((1, None, 0),)),
+    )
+    (kept,) = product(
+        order_of((0,), core),
+        items,
+        pieces,
+        ((first, 1, 0, 0),),
+        ((rows, q),),
+        (((0, None, 0),),),
+    )
+    terms = [kept, hop(right, "y", ny, 1), hop(left, "y", ny, -1)]
     outgoing = place(
-        rows_of, [terms[k] for k in range(ny)], peers, len(offsets), count, cap, item_rows
+        rows_of, terms, peers, len(offsets), count, cap, item_rows
     )
     arrived = lax.all_to_all(outgoing, ("z", "x"), 0, 0, tiled=True)
-    return finish([arrived], [offsets], nz, nx, cap)
+    return finish(arrived, offsets, nx, cap)
 
 
 def solution(mesh):

time: 156 us -> 143 us (0.917)
  local copies, waits for them, and re-layouts: 13.2 us -> 4.5 us
  Pallas kernels: 27.4 us -> 23.6 us
  waiting for transfers between devices: 42 us -> 44.9 us
  blocking collectives: 35.9 us -> 34.3 us
    unnamed x26 -> x10, local copies, waits for them, and re-layouts: 9.58 us -> 0.81 us
    ppermute x4 -> x2, waiting for transfers between devices: 0.01 us -> 2.97 us  [the longest x1 2.97 us: per_device(): first = lax.ppermute(first, 'core', swap)]
    ppermute x15 -> x16, starting transfers between devices: 21 us -> 22.9 us  [hop(): return lax.ppermute(value, axis, shift(size, step))]
    pallas_call x2, Pallas kernels: 7.84 us -> 6.14 us  [the longest x1 5.14 us: half_transform(): pl.pallas_call(functools.partial(halves_kernel, orbitals=orbitals), grid_...]
    ppermute x15 -> x16, waiting for transfers between devices: 39 us -> 38.9 us  [hop(): return lax.ppermute(value, axis, shift(size, step))]
  transfers between devices with their start and end apart: 20 -> 19, of which waited for: 10 -> 12; matrix products, arithmetic and copies ran while one was open for 4% -> 4% of each run, Pallas kernels for 11% -> 7%
where the time goes in v3:
time: 143 us; the launch traced here: 142 us
  waiting for transfers between devices  44.9 us (31%)
  blocking collectives  34.3 us (24%)
  starting transfers between devices  31.2 us (22%)
  Pallas kernels  23.6 us (17%)
  local copies, waits for them, and re-layouts  4.5 us (3%)
  other arithmetic  1.7 us (1%)
  between operations  1.43 us (1%)
    ppermute x16, waiting for transfers between devices, hop(): return lax.ppermute(value, axis, shift(size, step))  38.9 us
    all_to_all x1, blocking collectives, per_device(): arrived = lax.all_to_all(outgoing, ('z', 'x'), 0, 0, tiled=True)  34.3 us
    ppermute x16, starting transfers between devices, hop(): return lax.ppermute(value, axis, shift(size, step))  22.9 us
    pallas_call x4, Pallas kernels, product(): pl.pallas_call(functools.partial(product_kernel, items=len(items), pieces...  14.5 us
    all_to_all x1, starting transfers between devices, per_device(): lax.all_to_all(jnp.broadcast_to(packed[None], (peers,) + packed.shape), (...  7.78 us
    pallas_call x1, Pallas kernels, half_transform(): pl.pallas_call(functools.partial(halves_kernel, orbitals=orbitals), grid_...  5.14 us
    all_to_all x1, waiting for transfers between devices, per_device(): lax.all_to_all(jnp.broadcast_to(packed[None], (peers,) + packed.shape), (...  3.03 us
    ppermute x1, waiting for transfers between devices, per_device(): first = lax.ppermute(first, 'core', swap)  2.97 us
  transfers between devices with their start and end apart: 19, of which 12 were waited for; matrix products, arithmetic and copies ran while one was open for 4% of the time, Pallas kernels for 7%

profile of v3, /device:TPU:18, one launch (start us, length us, event | category | flops | bytes accessed | tf_op | source)
XLA Modules:
  0.0 141.7 jit_solution(7068929041054994067)
XLA Ops:
  0.0 5.9 %collective-permute-start.8 = (bf16[1024,256]{1,0:T(8,128)(2,1)}, bf16[1024,256]{1,0:T(8,128)(2,1)S(1)}, u32[]{:S(2)}, u32[]{:S(2)}) collective-permute-start(bf16[1024,256]{1,0:T(8,128)(2,1)} %refs_5_.7), channel_id=1, source_target_pairs={{0,224},{32,0},{64,32},{96,64},{128,96},{160,128},{192,160},{224,1... | collective-permute-start | bytes 1572872 | tf_op jit(solution)/shard_map/ppermute | solution.py:264
  8.0 7.8 %all-to-all-start = ((bf16[32,8,640]{2,1,0:T(8,128)(2,1)}), bf16[32,8,640]{2,1,0:T(8,128)(2,1)S(1)}, u32[]{:S(2)}, u32[]{:S(2)}) async-start(bf16[32,8,640]{2,1,0:T(8,128)(2,1)} %broadcast_in_dim.10), calls=%async_computation | async-start | bytes 655360 | tf_op jit(solution)/shard_map/all_to_all | solution.py:276
  15.8 5.4 %collective-permute-done.8.refs_13_ = bf16[1024,256]{1,0:T(8,128)(2,1)S(1)} collective-permute-done((bf16[1024,256]{1,0:T(8,128)(2,1)}, bf16[1024,256]{1,0:T(8,128)(2,1)S(1)}, u32[]{:S(2)}, u32[]{:S(2)}) %collective-permute-start.8) | collective-permute-done | bytes 524320 | tf_op jit(solution)/shard_map/ppermute | solution.py:264
  21.2 3.9 %collective-permute-start.9 = (bf16[1024,256]{1,0:T(8,128)(2,1)S(1)}, bf16[1024,256]{1,0:T(8,128)(2,1)}, u32[]{:S(2)}, u32[]{:S(2)}) collective-permute-start(bf16[1024,256]{1,0:T(8,128)(2,1)S(1)} %collective-permute-done.8.refs_13_), channel_id=1, source_target_pairs={{0,224},{32,0},{64,32},{96,64},{128,96},{160,128},{192,160},{224,1... | collective-permute-start | bytes 1572872 | tf_op jit(solution)/shard_map/ppermute | solution.py:264
  27.0 3.0 %all-to-all-done.packed_ref = bf16[32,8,640]{2,1,0:T(8,128)(2,1)S(1)} async-done(((bf16[32,8,640]{2,1,0:T(8,128)(2,1)}), bf16[32,8,640]{2,1,0:T(8,128)(2,1)S(1)}, u32[]{:S(2)}, u32[]{:S(2)}) %all-to-all-start) | async-done | bytes 327712 | tf_op jit(solution)/shard_map/all_to_all | solution.py:276
  30.1 5.1 %halves.1.refs_0_ = bf16[256,1024]{1,0:T(8,128)(2,1)S(1)} custom-call(s32[3]{0:T(128)S(1)} %pad_add_fusion.1.where, bf16[32,8,640]{2,1,0:T(8,128)(2,1)S(1)} %all-to-all-done.packed_ref, bf16[64,64,1024]{2,1,0:T(8,128)(2,1)} %bitcast.24), custom_call_target="tpu_custom_call" | custom-call | flops 1073741824 | bytes 8388608 | tf_op jit(solution)/shard_map/halves/pallas_call | solution.py:52
  37.3 2.0 %collective-permute-start.10 = (bf16[1024,256]{1,0:T(8,128)(2,1)}, bf16[1024,256]{1,0:T(8,128)(2,1)S(1)}, u32[]{:S(2)}, u32[]{:S(2)}) collective-permute-start(bf16[1024,256]{1,0:T(8,128)(2,1)} %collective-permute-done.9.refs_12_), channel_id=1, source_target_pairs={{0,224},{32,0},{64,32},{96,64},{128,96},{160,128},{192,160},{224,1... | collective-permute-start | bytes 1572872 | tf_op jit(solution)/shard_map/ppermute | solution.py:264
  39.4 7.1 %collective-permute-done.1.refs_2_ = bf16[256,1024]{1,0:T(8,128)(2,1)S(1)} collective-permute-done((bf16[256,1024]{1,0:T(8,128)(2,1)S(1)}, bf16[256,1024]{1,0:T(8,128)(2,1)S(1)}, u32[]{:S(2)}, u32[]{:S(2)}) %collective-permute-start.1) | collective-permute-done | bytes 524320 | tf_op jit(solution)/shard_map/ppermute | solution.py:264
  48.8 1.2 collective-permute-start.2
  50.7 2.8 %collective-permute-start.11 = (bf16[512,256]{1,0:T(8,128)(2,1)}, bf16[512,256]{1,0:T(8,128)(2,1)S(1)}, u32[]{:S(2)}, u32[]{:S(2)}) collective-permute-start(bf16[512,256]{1,0:T(8,128)(2,1)} %slice.24), channel_id=1, source_target_pairs={{0,224},{32,0},{64,32},{96,64},{128,96},{160,128},{192,160},{224,1... | collective-permute-start | bytes 786440 | tf_op jit(solution)/shard_map/ppermute | solution.py:264
  55.4 2.3 %collective-permute-done.11.refs_10_ = bf16[512,256]{1,0:T(8,128)(2,1)S(1)} collective-permute-done((bf16[512,256]{1,0:T(8,128)(2,1)}, bf16[512,256]{1,0:T(8,128)(2,1)S(1)}, u32[]{:S(2)}, u32[]{:S(2)}) %collective-permute-start.11) | collective-permute-done | bytes 262176 | tf_op jit(solution)/shard_map/ppermute | solution.py:264
  57.7 5.2 %collective-permute-done.7.refs_9_ = bf16[512,256]{1,0:T(8,128)(2,1)} collective-permute-done((bf16[512,256]{1,0:T(8,128)(2,1)}, bf16[512,256]{1,0:T(8,128)(2,1)}, u32[]{:S(2)}, u32[]{:S(2)}) %collective-permute-start.7) | collective-permute-done | bytes 262176 | tf_op jit(solution)/shard_map/ppermute | solution.py:264
  62.9 5.7 %product.4 = (bf16[2,1024,256]{2,1,0:T(8,128)(2,1)}, bf16[2,1024,256]{2,1,0:T(8,128)(2,1)}) custom-call(s32[4]{0:T(128)S(1)} %pad_add_fusion.2.order, bf16[256,1024]{1,0:T(8,128)(2,1)S(1)} %halves.1.refs_0_, bf16[256,1024]{1,0:T(8,128)(2,1)S(1)} %collective-permute-done.refs_1_, bf16[256,1024]{1,0:T(8,128)(2,1)S(1)} %collective-permute-done.1.refs_2_, ...), custom_call_target="tpu_custom_call" | custom-call | flops 2147483648 | bytes 6291456 | tf_op jit(solution)/shard_map/product/pallas_call | solution.py:142
  69.2 3.0 %collective-permute-done.12.refs_14_ = bf16[2,1024,256]{2,1,0:T(8,128)(2,1)} collective-permute-done((bf16[2,1024,256]{2,1,0:T(8,128)(2,1)}, bf16[2,1024,256]{2,1,0:T(8,128)(2,1)}, u32[]{:S(2)}, u32[]{:S(2)}) %collective-permute-start.12) | collective-permute-done | bytes 1048608 | tf_op jit(solution)/shard_map/ppermute | solution.py:310
  72.2 2.6 %product.6 = (bf16[512,256]{1,0:T(8,128)(2,1)}, bf16[512,256]{1,0:T(8,128)(2,1)}) custom-call(s32[1]{0:T(128)} %bitcast.18.order, bf16[256,1024]{1,0:T(8,128)(2,1)S(1)} %halves.1.refs_0_, bf16[256,1024]{1,0:T(8,128)(2,1)S(1)} %collective-permute-done.refs_1_, bf16[256,1024]{1,0:T(8,128)(2,1)S(1)} %collective-permute-done.1.refs_2_, ...), custom_call_target="tpu_custom_call" | custom-call | flops 536870912 | bytes 3145728 | tf_op jit(solution)/shard_map/product/pallas_call | solution.py:142
  74.8 1.4 collective-permute-start.14
  77.0 6.6 %collective-permute-done.14.refs_16_ = bf16[512,256]{1,0:T(8,128)(2,1)} collective-permute-done((bf16[512,256]{1,0:T(8,128)(2,1)}, bf16[512,256]{1,0:T(8,128)(2,1)}, u32[]{:S(2)}, u32[]{:S(2)}) %collective-permute-start.14) | collective-permute-done | bytes 262176 | tf_op jit(solution)/shard_map/ppermute | solution.py:264
  84.6 4.2 %product.7 = (bf16[1024,256]{1,0:T(8,128)(2,1)}, bf16[1024,256]{1,0:T(8,128)(2,1)}) custom-call(s32[2]{0:T(128)S(1)} %pad_add_fusion.3.order, bf16[256,1024]{1,0:T(8,128)(2,1)S(1)} %halves.1.refs_0_, bf16[256,1024]{1,0:T(8,128)(2,1)S(1)} %collective-permute-done.refs_1_, bf16[256,1024]{1,0:T(8,128)(2,1)S(1)} %collective-permute-done.1.refs_2_, ...), custom_call_target="tpu_custom_call" | custom-call | flops 1073741824 | bytes 4194304 | tf_op jit(solution)/shard_map/product/pallas_call | solution.py:142
  88.8 1.7 %collective-permute-start.16 = (bf16[1024,256]{1,0:T(8,128)(2,1)}, bf16[1024,256]{1,0:T(8,128)(2,1)S(1)}, u32[]{:S(2)}, u32[]{:S(2)}) collective-permute-start(bf16[1024,256]{1,0:T(8,128)(2,1)} %get-tuple-element.15), channel_id=1, source_target_pairs={{0,2},{2,4},{4,6},{6,0},{1,3},{3,5},{5,7},{7,1},{8,10},{10,12},{12... | collective-permute-start | bytes 1572872 | tf_op jit(solution)/shard_map/ppermute | solution.py:264
  91.0 1.9 %product.5.refs_0_ = bf16[1024,256]{1,0:T(8,128)(2,1)S(1)} custom-call(s32[1]{0:T(128)} %bitcast.5.order, bf16[256,1024]{1,0:T(8,128)(2,1)S(1)} %halves.1.refs_0_, bf16[256,1024]{1,0:T(8,128)(2,1)S(1)} %collective-permute-done.refs_1_, bf16[256,1024]{1,0:T(8,128)(2,1)S(1)} %collective-permute-done.1.refs_2_, ...), custom_call_target="tpu_custom_call" | custom-call | flops 536870912 | bytes 3145728 | tf_op jit(solution)/shard_map/product/pallas_call | solution.py:142
  93.0 8.9 %collective-permute-done.16.refs_1_ = bf16[1024,256]{1,0:T(8,128)(2,1)S(1)} collective-permute-done((bf16[1024,256]{1,0:T(8,128)(2,1)}, bf16[1024,256]{1,0:T(8,128)(2,1)S(1)}, u32[]{:S(2)}, u32[]{:S(2)}) %collective-permute-start.16) | collective-permute-done | bytes 524320 | tf_op jit(solution)/shard_map/ppermute | solution.py:264
  101.9 1.5 %collective-permute-done.17.refs_2_ = bf16[1024,256]{1,0:T(8,128)(2,1)S(1)} collective-permute-done((bf16[1024,256]{1,0:T(8,128)(2,1)}, bf16[1024,256]{1,0:T(8,128)(2,1)S(1)}, u32[]{:S(2)}, u32[]{:S(2)}) %collective-permute-start.17) | collective-permute-done | bytes 524320 | tf_op jit(solution)/shard_map/ppermute | solution.py:264
  103.4 3.0 %place.1 = bf16[32,8,8,256]{3,2,1,0:T(8,128)(2,1)S(1)} custom-call(s32[128]{0:T(128)S(1)} %pad_add_fusion.dests, bf16[1024,256]{1,0:T(8,128)(2,1)S(1)} %product.5.refs_0_, bf16[1024,256]{1,0:T(8,128)(2,1)S(1)} %collective-permute-done.16.refs_1_, bf16[1024,256]{1,0:T(8,128)(2,1)S(1)} %collective-permute-done.17.refs_2_), custom_call_target="tpu_custom_call" | custom-call | flops 2097152 | bytes 3145728 | tf_op jit(solution)/shard_map/place/pallas_call | solution.py:206
  106.4 34.3 %all_to_all.10.part = bf16[32,8,8,256]{3,2,1,0:T(8,128)(2,1)S(1)} all-to-all(bf16[32,8,8,256]{3,2,1,0:T(8,128)(2,1)S(1)} %place.1), channel_id=1, replica_groups=mesh['z'=8,'x'=4,'y'=4,'core'=2] {'z','x'}, dimensions={0} | all-to-all | bytes 2097152 | tf_op jit(solution)/shard_map/all_to_all | solution.py:341
  (45 shorter events, 13.9 us)
Async XLA Ops:
  0.0 21.2 %collective-permute-start.8 = (bf16[1024,256]{1,0:T(8,128)(2,1)}, bf16[1024,256]{1,0:T(8,128)(2,1)S(1)}, u32[]{:S(2)}, u32[]{:S(2)}) collective-permute-start(bf16[1024,256]{1,0:T(8,128)(2,1)} %refs_5_.7), channel_id=1, source_target_pairs={{0,224},{32,0},{64,32},{96,64},{128,96},{160,128},{192,160},{224,1... | collective-permute-start | bytes 1572872 | tf_op jit(solution)/shard_map/ppermute | solution.py:264
  5.9 19.8 %collective-permute-start.4 = (bf16[1024,256]{1,0:T(8,128)(2,1)}, bf16[1024,256]{1,0:T(8,128)(2,1)S(1)}, u32[]{:S(2)}, u32[]{:S(2)}) collective-permute-start(bf16[1024,256]{1,0:T(8,128)(2,1)} %refs_5_.7), channel_id=1, source_target_pairs={{0,32},{32,64},{64,96},{96,128},{128,160},{160,192},{192,224},{224... | collective-permute-start | bytes 1572872 | tf_op jit(solution)/shard_map/ppermute | solution.py:264
  8.0 22.1 %all-to-all-start = ((bf16[32,8,640]{2,1,0:T(8,128)(2,1)}), bf16[32,8,640]{2,1,0:T(8,128)(2,1)S(1)}, u32[]{:S(2)}, u32[]{:S(2)}) async-start(bf16[32,8,640]{2,1,0:T(8,128)(2,1)} %broadcast_in_dim.10), calls=%async_computation | async-start | bytes 655360 | tf_op jit(solution)/shard_map/all_to_all | solution.py:276
  21.2 16.1 %copy-start.2 = (bf16[1024,256]{1,0:T(8,128)(2,1)}, bf16[1024,256]{1,0:T(8,128)(2,1)S(1)}, u32[]{:S(2)}) copy-start(bf16[1024,256]{1,0:T(8,128)(2,1)S(1)} %collective-permute-done.8.refs_13_) | copy-start | bytes 1572868
  21.2 16.1 %collective-permute-start.9 = (bf16[1024,256]{1,0:T(8,128)(2,1)S(1)}, bf16[1024,256]{1,0:T(8,128)(2,1)}, u32[]{:S(2)}, u32[]{:S(2)}) collective-permute-start(bf16[1024,256]{1,0:T(8,128)(2,1)S(1)} %collective-permute-done.8.refs_13_), channel_id=1, source_target_pairs={{0,224},{32,0},{64,32},{96,64},{128,96},{160,128},{192,160},{224,1... | collective-permute-start | bytes 1572872 | tf_op jit(solution)/shard_map/ppermute | solution.py:264
  25.6 20.8 %copy-start.3 = (bf16[1024,256]{1,0:T(8,128)(2,1)}, bf16[1024,256]{1,0:T(8,128)(2,1)S(1)}, u32[]{:S(2)}) copy-start(bf16[1024,256]{1,0:T(8,128)(2,1)S(1)} %collective-permute-done.4.refs_6_) | copy-start | bytes 1572868
  25.6 13.7 %collective-permute-start.5 = (bf16[1024,256]{1,0:T(8,128)(2,1)S(1)}, bf16[1024,256]{1,0:T(8,128)(2,1)}, u32[]{:S(2)}, u32[]{:S(2)}) collective-permute-start(bf16[1024,256]{1,0:T(8,128)(2,1)S(1)} %collective-permute-done.4.refs_6_), channel_id=1, source_target_pairs={{0,32},{32,64},{64,96},{96,128},{128,160},{160,192},{192,224},{224... | collective-permute-start | bytes 1572872 | tf_op jit(solution)/shard_map/ppermute | solution.py:264
  35.2 11.2 %collective-permute-start.1 = (bf16[256,1024]{1,0:T(8,128)(2,1)S(1)}, bf16[256,1024]{1,0:T(8,128)(2,1)S(1)}, u32[]{:S(2)}, u32[]{:S(2)}) collective-permute-start(bf16[256,1024]{1,0:T(8,128)(2,1)S(1)} %halves.1.refs_0_), channel_id=1, source_target_pairs={{0,24},{8,0},{16,8},{24,16},{1,25},{9,1},{17,9},{25,17},{2,26},{10... | collective-permute-start | bytes 1572872 | tf_op jit(solution)/shard_map/ppermute | solution.py:264
  36.2 11.9 %collective-permute-start = (bf16[256,1024]{1,0:T(8,128)(2,1)S(1)}, bf16[256,1024]{1,0:T(8,128)(2,1)S(1)}, u32[]{:S(2)}, u32[]{:S(2)}) collective-permute-start(bf16[256,1024]{1,0:T(8,128)(2,1)S(1)} %halves.1.refs_0_), channel_id=1, source_target_pairs={{0,8},{8,16},{16,24},{24,0},{1,9},{9,17},{17,25},{25,1},{2,10},{10... | collective-permute-start | bytes 1572872 | tf_op jit(solution)/shard_map/ppermute | solution.py:264
  37.3 12.6 %collective-permute-start.10 = (bf16[1024,256]{1,0:T(8,128)(2,1)}, bf16[1024,256]{1,0:T(8,128)(2,1)S(1)}, u32[]{:S(2)}, u32[]{:S(2)}) collective-permute-start(bf16[1024,256]{1,0:T(8,128)(2,1)} %collective-permute-done.9.refs_12_), channel_id=1, source_target_pairs={{0,224},{32,0},{64,32},{96,64},{128,96},{160,128},{192,160},{224,1... | collective-permute-start | bytes 1572872 | tf_op jit(solution)/shard_map/ppermute | solution.py:264
  39.3 14.2 %collective-permute-start.6 = (bf16[1024,256]{1,0:T(8,128)(2,1)}, bf16[1024,256]{1,0:T(8,128)(2,1)S(1)}, u32[]{:S(2)}, u32[]{:S(2)}) collective-permute-start(bf16[1024,256]{1,0:T(8,128)(2,1)} %collective-permute-done.5.refs_7_), channel_id=1, source_target_pairs={{0,32},{32,64},{64,96},{96,128},{128,160},{160,192},{192,224},{224... | collective-permute-start | bytes 1572872 | tf_op jit(solution)/shard_map/ppermute | solution.py:264
  47.2 7.9 %collective-permute-start.3 = (bf16[128,1024]{1,0:T(8,128)(2,1)}, bf16[128,1024]{1,0:T(8,128)(2,1)S(1)}, u32[]{:S(2)}, u32[]{:S(2)}) collective-permute-start(bf16[128,1024]{1,0:T(8,128)(2,1)} %slice.22), channel_id=1, source_target_pairs={{0,24},{8,0},{16,8},{24,16},{1,25},{9,1},{17,9},{25,17},{2,26},{10... | collective-permute-start | bytes 786440 | tf_op jit(solution)/shard_map/ppermute | solution.py:264
  48.8 6.6 %collective-permute-start.2 = (bf16[128,1024]{1,0:T(8,128)(2,1)}, bf16[128,1024]{1,0:T(8,128)(2,1)S(1)}, u32[]{:S(2)}, u32[]{:S(2)}) collective-permute-start(bf16[128,1024]{1,0:T(8,128)(2,1)} %slice.21), channel_id=1, source_target_pairs={{0,8},{8,16},{16,24},{24,0},{1,9},{9,17},{17,25},{25,1},{2,10},{10... | collective-permute-start | bytes 786440 | tf_op jit(solution)/shard_map/ppermute | solution.py:264
  49.9 12.9 %copy-start = (bf16[1024,256]{1,0:T(8,128)(2,1)}, bf16[1024,256]{1,0:T(8,128)(2,1)S(1)}, u32[]{:S(2)}) copy-start(bf16[1024,256]{1,0:T(8,128)(2,1)S(1)} %collective-permute-done.10.refs_11_) | copy-start | bytes 1572868
  50.7 7.0 %collective-permute-start.11 = (bf16[512,256]{1,0:T(8,128)(2,1)}, bf16[512,256]{1,0:T(8,128)(2,1)S(1)}, u32[]{:S(2)}, u32[]{:S(2)}) collective-permute-start(bf16[512,256]{1,0:T(8,128)(2,1)} %slice.24), channel_id=1, source_target_pairs={{0,224},{32,0},{64,32},{96,64},{128,96},{160,128},{192,160},{224,1... | collective-permute-start | bytes 786440 | tf_op jit(solution)/shard_map/ppermute | solution.py:264
  53.5 0.8 copy-start.1
  55.0 7.9 %collective-permute-start.7 = (bf16[512,256]{1,0:T(8,128)(2,1)}, bf16[512,256]{1,0:T(8,128)(2,1)}, u32[]{:S(2)}, u32[]{:S(2)}) collective-permute-start(bf16[512,256]{1,0:T(8,128)(2,1)} %slice.23), channel_id=1, source_target_pairs={{0,32},{32,64},{64,96},{96,128},{128,160},{160,192},{192,224},{224... | collective-permute-start | bytes 786440 | tf_op jit(solution)/shard_map/ppermute | solution.py:264
  57.7 5.2 %copy-start.4 = (bf16[512,256]{1,0:T(8,128)(2,1)}, bf16[512,256]{1,0:T(8,128)(2,1)S(1)}, u32[]{:S(2)}) copy-start(bf16[512,256]{1,0:T(8,128)(2,1)S(1)} %collective-permute-done.11.refs_10_) | copy-start | bytes 786436
  68.6 3.6 %collective-permute-start.12 = (bf16[2,1024,256]{2,1,0:T(8,128)(2,1)}, bf16[2,1024,256]{2,1,0:T(8,128)(2,1)}, u32[]{:S(2)}, u32[]{:S(2)}) collective-permute-start(bf16[2,1024,256]{2,1,0:T(8,128)(2,1)} %get-tuple-element.11), channel_id=1, source_target_pairs={{0,1},{1,0},{2,3},{3,2},{4,5},{5,4},{6,7},{7,6},{8,9},{9,8},{10,11... | collective-permute-start | bytes 3145736 | tf_op jit(solution)/shard_map/ppermute | solution.py:310
  68.7 8.3 %collective-permute-start.13 = (bf16[2,1024,256]{2,1,0:T(8,128)(2,1)}, bf16[2,1024,256]{2,1,0:T(8,128)(2,1)S(1)}, u32[]{:S(2)}, u32[]{:S(2)}) collective-permute-start(bf16[2,1024,256]{2,1,0:T(8,128)(2,1)} %get-tuple-element.12), channel_id=1, source_target_pairs={{0,1},{1,0},{2,3},{3,2},{4,5},{5,4},{6,7},{7,6},{8,9},{9,8},{10,11... | collective-permute-start | bytes 3145736 | tf_op jit(solution)/shard_map/ppermute | solution.py:311
  74.8 8.7 %collective-permute-start.14 = (bf16[512,256]{1,0:T(8,128)(2,1)}, bf16[512,256]{1,0:T(8,128)(2,1)}, u32[]{:S(2)}, u32[]{:S(2)}) collective-permute-start(bf16[512,256]{1,0:T(8,128)(2,1)} %get-tuple-element.13), channel_id=1, source_target_pairs={{0,2},{2,4},{4,6},{6,0},{1,3},{3,5},{5,7},{7,1},{8,10},{10,12},{12... | collective-permute-start | bytes 786440 | tf_op jit(solution)/shard_map/ppermute | solution.py:264
  76.2 8.4 %collective-permute-start.15 = (bf16[512,256]{1,0:T(8,128)(2,1)}, bf16[512,256]{1,0:T(8,128)(2,1)}, u32[]{:S(2)}, u32[]{:S(2)}) collective-permute-start(bf16[512,256]{1,0:T(8,128)(2,1)} %get-tuple-element.14), channel_id=1, source_target_pairs={{0,6},{2,0},{4,2},{6,4},{1,7},{3,1},{5,3},{7,5},{8,14},{10,8},{12,... | collective-permute-start | bytes 786440 | tf_op jit(solution)/shard_map/ppermute | solution.py:264
  88.8 13.1 %collective-permute-start.16 = (bf16[1024,256]{1,0:T(8,128)(2,1)}, bf16[1024,256]{1,0:T(8,128)(2,1)S(1)}, u32[]{:S(2)}, u32[]{:S(2)}) collective-permute-start(bf16[1024,256]{1,0:T(8,128)(2,1)} %get-tuple-element.15), channel_id=1, source_target_pairs={{0,2},{2,4},{4,6},{6,0},{1,3},{3,5},{5,7},{7,1},{8,10},{10,12},{12... | collective-permute-start | bytes 1572872 | tf_op jit(solution)/shard_map/ppermute | solution.py:264
  90.4 12.9 %collective-permute-start.17 = (bf16[1024,256]{1,0:T(8,128)(2,1)}, bf16[1024,256]{1,0:T(8,128)(2,1)S(1)}, u32[]{:S(2)}, u32[]{:S(2)}) collective-permute-start(bf16[1024,256]{1,0:T(8,128)(2,1)} %get-tuple-element.16), channel_id=1, source_target_pairs={{0,6},{2,0},{4,2},{6,4},{1,7},{3,1},{5,3},{7,5},{8,14},{10,8},{12,... | collective-permute-start | bytes 1572872 | tf_op jit(solution)/shard_map/ppermute | solution.py:264

commit v4 on v3

--- a/solution.py
+++ b/solution.py
@@ -112,6 +112,13 @@
         at = 0
         for piece in rows:
             count = piece.shape[0]
+            if not any(
+                wanted == step and first <= at < first + ref.shape[-2]
+                for ref, places in zip(results, outs)
+                for wanted, _, first in places
+            ):
+                at += count
+                continue
             value = jnp.dot(piece[...], held[step], preferred_element_type=F32)
             for slot, (_, wanted, first) in enumerate(adds):
                 size = terms[slot].shape[-2]
@@ -169,18 +176,24 @@
     )(order, *items, *flat, *[term[0] for term in terms])
 
 
-def place_kernel(dests, *refs, sources, count, cap):
-    *terms, out, total, used, held, sems = refs
-    copies = [
-        pltpu.make_async_copy(term, held.at[at], sems.at[at]) for at, term in enumerate(terms)
-    ]
+def place_kernel(dests, *refs, sources, count, cap, parts):
+    refs = list(refs)
+    terms = [[refs.pop(0) for _ in range(n)] for n in parts]
+    out, total, used, held, sems = refs
+    copies = []
+    for at, term in enumerate(terms):
+        row = 0
+        for part, ref in enumerate(term):
+            spot = held.at[at, pl.ds(row, ref.shape[0])]
+            copies.append(pltpu.make_async_copy(ref, spot, sems.at[at, part]))
+            row += ref.shape[0]
     for copy in copies:
         copy.start()
     out[...] = jnp.zeros_like(out)
     for copy in copies:
         copy.wait()
     value = held[0].astype(F32)
-    for at in range(1, len(terms)):
+    for at in range(1, len(parts)):
         value = value + held[at].astype(F32)
     total[...] = value
     peers = out.shape[0]
@@ -201,29 +214,37 @@
 
 
 def place(dests, terms, peers, sources, count, cap, rows):
-    q = terms[0].shape[1]
+    flat = [part for term in terms for part in term]
+    q = flat[0].shape[1]
     shape = (peers, sources * cap, rows, q)
+    size = sources * count * rows
     return pl.pallas_call(
-        functools.partial(place_kernel, sources=sources, count=count, cap=cap),
+        functools.partial(
+            place_kernel,
+            sources=sources,
+            count=count,
+            cap=cap,
+            parts=tuple(len(term) for term in terms),
+        ),
         grid_spec=pltpu.PrefetchScalarGridSpec(
             num_scalar_prefetch=1,
             grid=(1,),
-            in_specs=[pl.BlockSpec(memory_space=pltpu.HBM)] * len(terms),
+            in_specs=[pl.BlockSpec(memory_space=pltpu.HBM)] * len(flat),
             out_specs=pl.BlockSpec(shape, lambda s, o: (0, 0, 0, 0)),
             scratch_shapes=[
-                pltpu.VMEM(terms[0].shape, F32),
+                pltpu.VMEM((size, q), F32),
                 pltpu.SMEM((peers,), jnp.int32),
-                pltpu.VMEM((len(terms),) + terms[0].shape, BF),
-                pltpu.SemaphoreType.DMA((len(terms),)),
+                pltpu.VMEM((len(terms), size, q), BF),
+                pltpu.SemaphoreType.DMA((len(terms), 2)),
             ],
         ),
         out_shape=jax.ShapeDtypeStruct(shape, BF),
         compiler_params=params(SMALL_LIMIT),
         cost_estimate=pl.CostEstimate(
-            flops=8 * terms[0].size, bytes_accessed=2 * (4 * terms[0].size + 2 * terms[0].size), transcendentals=0
+            flops=4 * size * q, bytes_accessed=10 * size * q, transcendentals=0
         ),
         name="place",
-    )(dests, *terms)
+    )(dests, *flat)
 
 
 def final_kernel(part, out, *, offsets, nx, cap):
@@ -317,14 +338,23 @@
         ((near, q), (near, q)),
         (((0, None, 0),), ((0, None, near),)),
     )
+    made = low
     low, high = hop(low, "y", ny, -1), hop(high, "y", ny, 1)
-    right, left = product(
+    right_low, left_high = product(
+        lax.optimization_barrier((order_of((1, 3), core), made))[0],
+        items,
+        pieces,
+        ((second, 0, 0, 0), (second, 1, 1, 0)),
+        ((near, q), (near, q)),
+        (((0, None, 0),), ((1, None, near),)),
+    )
+    right_high, left_low = product(
         order_of((1, 3), core),
         items,
         pieces,
         ((second, 0, 0, 0), (second, 1, 1, 0), (high, None, 0, near), (low, None, 1, 0)),
-        ((rows, q), (rows, q)),
-        (((0, None, 0),), ((1, None, 0),)),
+        ((near, q), (near, q)),
+        (((0, None, near),), ((1, None, 0),)),
     )
     (kept,) = product(
         order_of((0,), core),
@@ -334,7 +364,11 @@
         ((rows, q),),
         (((0, None, 0),),),
     )
-    terms = [kept, hop(right, "y", ny, 1), hop(left, "y", ny, -1)]
+    terms = [
+        (kept,),
+        (hop(right_low, "y", ny, 1), hop(right_high, "y", ny, 1)),
+        (hop(left_low, "y", ny, -1), hop(left_high, "y", ny, -1)),
+    ]
     outgoing = place(
         rows_of, terms, peers, len(offsets), count, cap, item_rows
     )

time: 143 us -> 133 us (0.930)
  waiting for transfers between devices: 44.9 us -> 34 us
  starting transfers between devices: 31.2 us -> 33.3 us
    ppermute x16 -> x18, waiting for transfers between devices: 38.9 us -> 28.1 us  [hop(): return lax.ppermute(value, axis, shift(size, step))]
    ppermute x16 -> x18, starting transfers between devices: 22.9 us -> 25 us  [hop(): return lax.ppermute(value, axis, shift(size, step))]
    pallas_call x4 -> x5, Pallas kernels: 14.5 us -> 14.8 us  [product(): pl.pallas_call(functools.partial(product_kernel, items=len(items), pieces...]
  transfers between devices with their start and end apart: 19 -> 21, of which waited for: 12 -> 12; matrix products, arithmetic and copies ran while one was open for 4% -> 4% of each run, Pallas kernels for 7% -> 11%
where the time goes in v4:
time: 133 us
  blocking collectives  34.5 us (26%)
  waiting for transfers between devices  34 us (26%)
  starting transfers between devices  33.3 us (25%)
  Pallas kernels  23.9 us (18%)
  local copies, waits for them, and re-layouts  3.76 us (3%)
  other arithmetic  1.7 us (1%)
  between operations  1.45 us (1%)
    all_to_all x1, blocking collectives, per_device(): arrived = lax.all_to_all(outgoing, ('z', 'x'), 0, 0, tiled=True)  34.5 us
    ppermute x18, waiting for transfers between devices, hop(): return lax.ppermute(value, axis, shift(size, step))  28.1 us
    ppermute x18, starting transfers between devices, hop(): return lax.ppermute(value, axis, shift(size, step))  25 us
    pallas_call x5, Pallas kernels, product(): pl.pallas_call(functools.partial(product_kernel, items=len(items), pieces...  14.8 us
    all_to_all x1, starting transfers between devices, per_device(): lax.all_to_all(jnp.broadcast_to(packed[None], (peers,) + packed.shape), (...  7.78 us
    pallas_call x1, Pallas kernels, half_transform(): pl.pallas_call(functools.partial(halves_kernel, orbitals=orbitals), grid_...  5.14 us
    all_to_all x1, waiting for transfers between devices, per_device(): lax.all_to_all(jnp.broadcast_to(packed[None], (peers,) + packed.shape), (...  3.03 us
    pallas_call x1, Pallas kernels, place(): pl.pallas_call(functools.partial(place_kernel, sources=sources, count=cou...  2.99 us
  transfers between devices with their start and end apart: 21, of which 12 were waited for; matrix products, arithmetic and copies ran while one was open for 4% of the time, Pallas kernels for 11%

profile of v4, /device:TPU:18, one launch (start us, length us, event | category | flops | bytes accessed | tf_op | source)
XLA Modules:
  0.0 132.7 jit_solution(10753520766385077696)
XLA Ops:
  0.0 5.9 %collective-permute-start.8 = (bf16[1024,256]{1,0:T(8,128)(2,1)}, bf16[1024,256]{1,0:T(8,128)(2,1)S(1)}, u32[]{:S(2)}, u32[]{:S(2)}) collective-permute-start(bf16[1024,256]{1,0:T(8,128)(2,1)} %refs_5_.9), channel_id=1, source_target_pairs={{0,224},{32,0},{64,32},{96,64},{128,96},{160,128},{192,160},{224,1... | collective-permute-start | bytes 1572872 | tf_op jit(solution)/shard_map/ppermute | solution.py:285
  8.0 7.8 %all-to-all-start = ((bf16[32,8,640]{2,1,0:T(8,128)(2,1)}), bf16[32,8,640]{2,1,0:T(8,128)(2,1)S(1)}, u32[]{:S(2)}, u32[]{:S(2)}) async-start(bf16[32,8,640]{2,1,0:T(8,128)(2,1)} %broadcast_in_dim.10), calls=%async_computation | async-start | bytes 655360 | tf_op jit(solution)/shard_map/all_to_all | solution.py:297
  15.8 5.4 %collective-permute-done.8.refs_13_ = bf16[1024,256]{1,0:T(8,128)(2,1)S(1)} collective-permute-done((bf16[1024,256]{1,0:T(8,128)(2,1)}, bf16[1024,256]{1,0:T(8,128)(2,1)S(1)}, u32[]{:S(2)}, u32[]{:S(2)}) %collective-permute-start.8) | collective-permute-done | bytes 524320 | tf_op jit(solution)/shard_map/ppermute | solution.py:285
  21.2 3.9 %collective-permute-start.9 = (bf16[1024,256]{1,0:T(8,128)(2,1)S(1)}, bf16[1024,256]{1,0:T(8,128)(2,1)}, u32[]{:S(2)}, u32[]{:S(2)}) collective-permute-start(bf16[1024,256]{1,0:T(8,128)(2,1)S(1)} %collective-permute-done.8.refs_13_), channel_id=1, source_target_pairs={{0,224},{32,0},{64,32},{96,64},{128,96},{160,128},{192,160},{224,1... | collective-permute-start | bytes 1572872 | tf_op jit(solution)/shard_map/ppermute | solution.py:285
  27.0 3.0 %all-to-all-done.packed_ref = bf16[32,8,640]{2,1,0:T(8,128)(2,1)S(1)} async-done(((bf16[32,8,640]{2,1,0:T(8,128)(2,1)}), bf16[32,8,640]{2,1,0:T(8,128)(2,1)S(1)}, u32[]{:S(2)}, u32[]{:S(2)}) %all-to-all-start) | async-done | bytes 327712 | tf_op jit(solution)/shard_map/all_to_all | solution.py:297
  30.1 5.1 %halves.1.refs_0_ = bf16[256,1024]{1,0:T(8,128)(2,1)S(1)} custom-call(s32[3]{0:T(128)S(1)} %pad_add_fusion.1.where, bf16[32,8,640]{2,1,0:T(8,128)(2,1)S(1)} %all-to-all-done.packed_ref, bf16[64,64,1024]{2,1,0:T(8,128)(2,1)} %bitcast.24), custom_call_target="tpu_custom_call" | custom-call | flops 1073741824 | bytes 8388608 | tf_op jit(solution)/shard_map/halves/pallas_call | solution.py:52
  37.3 2.0 %collective-permute-start.10 = (bf16[1024,256]{1,0:T(8,128)(2,1)}, bf16[1024,256]{1,0:T(8,128)(2,1)S(1)}, u32[]{:S(2)}, u32[]{:S(2)}) collective-permute-start(bf16[1024,256]{1,0:T(8,128)(2,1)} %collective-permute-done.9.refs_12_), channel_id=1, source_target_pairs={{0,224},{32,0},{64,32},{96,64},{128,96},{160,128},{192,160},{224,1... | collective-permute-start | bytes 1572872 | tf_op jit(solution)/shard_map/ppermute | solution.py:285
  39.4 7.1 %collective-permute-done.1.refs_2_ = bf16[256,1024]{1,0:T(8,128)(2,1)S(1)} collective-permute-done((bf16[256,1024]{1,0:T(8,128)(2,1)S(1)}, bf16[256,1024]{1,0:T(8,128)(2,1)S(1)}, u32[]{:S(2)}, u32[]{:S(2)}) %collective-permute-start.1) | collective-permute-done | bytes 524320 | tf_op jit(solution)/shard_map/ppermute | solution.py:285
  50.7 2.8 %collective-permute-start.11 = (bf16[512,256]{1,0:T(8,128)(2,1)}, bf16[512,256]{1,0:T(8,128)(2,1)}, u32[]{:S(2)}, u32[]{:S(2)}) collective-permute-start(bf16[512,256]{1,0:T(8,128)(2,1)} %slice.24), channel_id=1, source_target_pairs={{0,224},{32,0},{64,32},{96,64},{128,96},{160,128},{192,160},{224,1... | collective-permute-start | bytes 786440 | tf_op jit(solution)/shard_map/ppermute | solution.py:285
  55.4 2.3 %collective-permute-done.11.refs_10_ = bf16[512,256]{1,0:T(8,128)(2,1)} collective-permute-done((bf16[512,256]{1,0:T(8,128)(2,1)}, bf16[512,256]{1,0:T(8,128)(2,1)}, u32[]{:S(2)}, u32[]{:S(2)}) %collective-permute-start.11) | collective-permute-done | bytes 262176 | tf_op jit(solution)/shard_map/ppermute | solution.py:285
  57.7 4.5 %collective-permute-done.7.refs_9_ = bf16[512,256]{1,0:T(8,128)(2,1)} collective-permute-done((bf16[512,256]{1,0:T(8,128)(2,1)}, bf16[512,256]{1,0:T(8,128)(2,1)}, u32[]{:S(2)}, u32[]{:S(2)}) %collective-permute-start.7) | collective-permute-done | bytes 262176 | tf_op jit(solution)/shard_map/ppermute | solution.py:285
  62.2 5.8 %product.5 = (bf16[2,1024,256]{2,1,0:T(8,128)(2,1)}, bf16[2,1024,256]{2,1,0:T(8,128)(2,1)}) custom-call(s32[4]{0:T(128)S(1)} %pad_add_fusion.2.order, bf16[256,1024]{1,0:T(8,128)(2,1)S(1)} %halves.1.refs_0_, bf16[256,1024]{1,0:T(8,128)(2,1)S(1)} %collective-permute-done.refs_1_, bf16[256,1024]{1,0:T(8,128)(2,1)S(1)} %collective-permute-done.1.refs_2_, ...), custom_call_target="tpu_custom_call" | custom-call | flops 2147483648 | bytes 6291456 | tf_op jit(solution)/shard_map/product/pallas_call | solution.py:149
  68.6 2.9 %collective-permute-done.12.refs_14_ = bf16[2,1024,256]{2,1,0:T(8,128)(2,1)} collective-permute-done((bf16[2,1024,256]{2,1,0:T(8,128)(2,1)}, bf16[2,1024,256]{2,1,0:T(8,128)(2,1)}, u32[]{:S(2)}, u32[]{:S(2)}) %collective-permute-start.12) | collective-permute-done | bytes 1048608 | tf_op jit(solution)/shard_map/ppermute | solution.py:331
  71.5 1.9 %product.7 = (bf16[512,256]{1,0:T(8,128)(2,1)S(1)}, bf16[512,256]{1,0:T(8,128)(2,1)S(1)}) custom-call(s32[1]{0:T(128)} %bitcast.18.order, bf16[256,1024]{1,0:T(8,128)(2,1)S(1)} %halves.1.refs_0_, bf16[256,1024]{1,0:T(8,128)(2,1)S(1)} %collective-permute-done.refs_1_, bf16[256,1024]{1,0:T(8,128)(2,1)S(1)} %collective-permute-done.1.refs_2_, ...), custom_call_target="tpu_custom_call" | custom-call | flops 536870912 | bytes 3145728 | tf_op jit(solution)/shard_map/product/pallas_call | solution.py:149
  73.4 1.4 %collective-permute-start.15 = (bf16[512,256]{1,0:T(8,128)(2,1)S(1)}, bf16[512,256]{1,0:T(8,128)(2,1)S(1)}, u32[]{:S(2)}, u32[]{:S(2)}) collective-permute-start(bf16[512,256]{1,0:T(8,128)(2,1)S(1)} %get-tuple-element.19), channel_id=1, source_target_pairs={{0,2},{2,4},{4,6},{6,0},{1,3},{3,5},{5,7},{7,1},{8,10},{10,12},{12... | collective-permute-start | bytes 786440 | tf_op jit(solution)/shard_map/ppermute | solution.py:285
  75.6 2.6 %product.8 = (bf16[512,256]{1,0:T(8,128)(2,1)S(1)}, bf16[512,256]{1,0:T(8,128)(2,1)S(1)}) custom-call(s32[2]{0:T(128)S(1)} %pad_add_fusion.3.order, bf16[256,1024]{1,0:T(8,128)(2,1)S(1)} %halves.1.refs_0_, bf16[256,1024]{1,0:T(8,128)(2,1)S(1)} %collective-permute-done.refs_1_, bf16[256,1024]{1,0:T(8,128)(2,1)S(1)} %collective-permute-done.1.refs_2_, ...), custom_call_target="tpu_custom_call" | custom-call | flops 1073741824 | bytes 4194304 | tf_op jit(solution)/shard_map/product/pallas_call | solution.py:149
  78.2 1.4 %collective-permute-start.14 = (bf16[512,256]{1,0:T(8,128)(2,1)S(1)}, bf16[512,256]{1,0:T(8,128)(2,1)S(1)}, u32[]{:S(2)}, u32[]{:S(2)}) collective-permute-start(bf16[512,256]{1,0:T(8,128)(2,1)S(1)} %get-tuple-element.18), channel_id=1, source_target_pairs={{0,2},{2,4},{4,6},{6,0},{1,3},{3,5},{5,7},{7,1},{8,10},{10,12},{12... | collective-permute-start | bytes 786440 | tf_op jit(solution)/shard_map/ppermute | solution.py:285
  80.3 2.4 %collective-permute-done.15.refs_16_ = bf16[512,256]{1,0:T(8,128)(2,1)S(1)} collective-permute-done((bf16[512,256]{1,0:T(8,128)(2,1)S(1)}, bf16[512,256]{1,0:T(8,128)(2,1)S(1)}, u32[]{:S(2)}, u32[]{:S(2)}) %collective-permute-start.15) | collective-permute-done | bytes 262176 | tf_op jit(solution)/shard_map/ppermute | solution.py:285
  84.0 2.6 %product.9 = (bf16[512,256]{1,0:T(8,128)(2,1)S(1)}, bf16[512,256]{1,0:T(8,128)(2,1)S(1)}) custom-call(s32[2]{0:T(128)S(1)} %pad_add_fusion.3.order, bf16[256,1024]{1,0:T(8,128)(2,1)S(1)} %halves.1.refs_0_, bf16[256,1024]{1,0:T(8,128)(2,1)S(1)} %collective-permute-done.refs_1_, bf16[256,1024]{1,0:T(8,128)(2,1)S(1)} %collective-permute-done.1.refs_2_, ...), custom_call_target="tpu_custom_call" | custom-call | flops 1073741824 | bytes 4194304 | tf_op jit(solution)/shard_map/product/pallas_call | solution.py:149
  87.3 1.4 %collective-permute-start.18 = (bf16[512,256]{1,0:T(8,128)(2,1)S(1)}, bf16[512,256]{1,0:T(8,128)(2,1)S(1)}, u32[]{:S(2)}, u32[]{:S(2)}) collective-permute-start(bf16[512,256]{1,0:T(8,128)(2,1)S(1)} %get-tuple-element.21), channel_id=1, source_target_pairs={{0,6},{2,0},{4,2},{6,4},{1,7},{3,1},{5,3},{7,5},{8,14},{10,8},{12,... | collective-permute-start | bytes 786440 | tf_op jit(solution)/shard_map/ppermute | solution.py:285
  88.8 1.9 %product.6.refs_0_ = bf16[1024,256]{1,0:T(8,128)(2,1)S(1)} custom-call(s32[1]{0:T(128)} %bitcast.5.order, bf16[256,1024]{1,0:T(8,128)(2,1)S(1)} %halves.1.refs_0_, bf16[256,1024]{1,0:T(8,128)(2,1)S(1)} %collective-permute-done.refs_1_, bf16[256,1024]{1,0:T(8,128)(2,1)S(1)} %collective-permute-done.1.refs_2_, ...), custom_call_target="tpu_custom_call" | custom-call | flops 536870912 | bytes 3145728 | tf_op jit(solution)/shard_map/product/pallas_call | solution.py:149
  90.7 2.4 %collective-permute-done.17.refs_2_ = bf16[512,256]{1,0:T(8,128)(2,1)S(1)} collective-permute-done((bf16[512,256]{1,0:T(8,128)(2,1)S(1)}, bf16[512,256]{1,0:T(8,128)(2,1)S(1)}, u32[]{:S(2)}, u32[]{:S(2)}) %collective-permute-start.17) | collective-permute-done | bytes 262176 | tf_op jit(solution)/shard_map/ppermute | solution.py:285
  94.2 3.0 %place.1 = bf16[32,8,8,256]{3,2,1,0:T(8,128)(2,1)S(1)} custom-call(s32[128]{0:T(128)S(1)} %pad_add_fusion.dests, bf16[1024,256]{1,0:T(8,128)(2,1)S(1)} %product.6.refs_0_, bf16[512,256]{1,0:T(8,128)(2,1)S(1)} %collective-permute-done.14.refs_1_, bf16[512,256]{1,0:T(8,128)(2,1)S(1)} %collective-permute-done.17.refs_2_, ...), custom_call_target="tpu_custom_call" | custom-call | flops 1048576 | bytes 2621440 | tf_op jit(solution)/shard_map/place/pallas_call | solution.py:221
  97.2 34.5 %all_to_all.10.part = bf16[32,8,8,256]{3,2,1,0:T(8,128)(2,1)S(1)} all-to-all(bf16[32,8,8,256]{3,2,1,0:T(8,128)(2,1)S(1)} %place.1), channel_id=1, replica_groups=mesh['z'=8,'x'=4,'y'=4,'core'=2] {'z','x'}, dimensions={0} | all-to-all | bytes 2097152 | tf_op jit(solution)/shard_map/all_to_all | solution.py:375
  (48 shorter events, 17.5 us)
Async XLA Ops:
  0.0 21.2 %collective-permute-start.8 = (bf16[1024,256]{1,0:T(8,128)(2,1)}, bf16[1024,256]{1,0:T(8,128)(2,1)S(1)}, u32[]{:S(2)}, u32[]{:S(2)}) collective-permute-start(bf16[1024,256]{1,0:T(8,128)(2,1)} %refs_5_.9), channel_id=1, source_target_pairs={{0,224},{32,0},{64,32},{96,64},{128,96},{160,128},{192,160},{224,1... | collective-permute-start | bytes 1572872 | tf_op jit(solution)/shard_map/ppermute | solution.py:285
  5.9 19.8 %collective-permute-start.4 = (bf16[1024,256]{1,0:T(8,128)(2,1)}, bf16[1024,256]{1,0:T(8,128)(2,1)S(1)}, u32[]{:S(2)}, u32[]{:S(2)}) collective-permute-start(bf16[1024,256]{1,0:T(8,128)(2,1)} %refs_5_.9), channel_id=1, source_target_pairs={{0,32},{32,64},{64,96},{96,128},{128,160},{160,192},{192,224},{224... | collective-permute-start | bytes 1572872 | tf_op jit(solution)/shard_map/ppermute | solution.py:285
  8.0 22.1 %all-to-all-start = ((bf16[32,8,640]{2,1,0:T(8,128)(2,1)}), bf16[32,8,640]{2,1,0:T(8,128)(2,1)S(1)}, u32[]{:S(2)}, u32[]{:S(2)}) async-start(bf16[32,8,640]{2,1,0:T(8,128)(2,1)} %broadcast_in_dim.10), calls=%async_computation | async-start | bytes 655360 | tf_op jit(solution)/shard_map/all_to_all | solution.py:297
  21.2 25.3 %copy-start.2 = (bf16[1024,256]{1,0:T(8,128)(2,1)}, bf16[1024,256]{1,0:T(8,128)(2,1)S(1)}, u32[]{:S(2)}) copy-start(bf16[1024,256]{1,0:T(8,128)(2,1)S(1)} %collective-permute-done.8.refs_13_) | copy-start | bytes 1572868
  21.2 16.1 %collective-permute-start.9 = (bf16[1024,256]{1,0:T(8,128)(2,1)S(1)}, bf16[1024,256]{1,0:T(8,128)(2,1)}, u32[]{:S(2)}, u32[]{:S(2)}) collective-permute-start(bf16[1024,256]{1,0:T(8,128)(2,1)S(1)} %collective-permute-done.8.refs_13_), channel_id=1, source_target_pairs={{0,224},{32,0},{64,32},{96,64},{128,96},{160,128},{192,160},{224,1... | collective-permute-start | bytes 1572872 | tf_op jit(solution)/shard_map/ppermute | solution.py:285
  25.6 13.7 %copy-start.3 = (bf16[1024,256]{1,0:T(8,128)(2,1)}, bf16[1024,256]{1,0:T(8,128)(2,1)S(1)}, u32[]{:S(2)}) copy-start(bf16[1024,256]{1,0:T(8,128)(2,1)S(1)} %collective-permute-done.4.refs_6_) | copy-start | bytes 1572868
  25.6 13.7 %collective-permute-start.5 = (bf16[1024,256]{1,0:T(8,128)(2,1)S(1)}, bf16[1024,256]{1,0:T(8,128)(2,1)}, u32[]{:S(2)}, u32[]{:S(2)}) collective-permute-start(bf16[1024,256]{1,0:T(8,128)(2,1)S(1)} %collective-permute-done.4.refs_6_), channel_id=1, source_target_pairs={{0,32},{32,64},{64,96},{96,128},{128,160},{160,192},{192,224},{224... | collective-permute-start | bytes 1572872 | tf_op jit(solution)/shard_map/ppermute | solution.py:285
  35.2 11.2 %collective-permute-start.1 = (bf16[256,1024]{1,0:T(8,128)(2,1)S(1)}, bf16[256,1024]{1,0:T(8,128)(2,1)S(1)}, u32[]{:S(2)}, u32[]{:S(2)}) collective-permute-start(bf16[256,1024]{1,0:T(8,128)(2,1)S(1)} %halves.1.refs_0_), channel_id=1, source_target_pairs={{0,24},{8,0},{16,8},{24,16},{1,25},{9,1},{17,9},{25,17},{2,26},{10... | collective-permute-start | bytes 1572872 | tf_op jit(solution)/shard_map/ppermute | solution.py:285
  36.2 11.9 %collective-permute-start = (bf16[256,1024]{1,0:T(8,128)(2,1)S(1)}, bf16[256,1024]{1,0:T(8,128)(2,1)S(1)}, u32[]{:S(2)}, u32[]{:S(2)}) collective-permute-start(bf16[256,1024]{1,0:T(8,128)(2,1)S(1)} %halves.1.refs_0_), channel_id=1, source_target_pairs={{0,8},{8,16},{16,24},{24,0},{1,9},{9,17},{17,25},{25,1},{2,10},{10... | collective-permute-start | bytes 1572872 | tf_op jit(solution)/shard_map/ppermute | solution.py:285
  37.3 12.6 %collective-permute-start.10 = (bf16[1024,256]{1,0:T(8,128)(2,1)}, bf16[1024,256]{1,0:T(8,128)(2,1)S(1)}, u32[]{:S(2)}, u32[]{:S(2)}) collective-permute-start(bf16[1024,256]{1,0:T(8,128)(2,1)} %collective-permute-done.9.refs_12_), channel_id=1, source_target_pairs={{0,224},{32,0},{64,32},{96,64},{128,96},{160,128},{192,160},{224,1... | collective-permute-start | bytes 1572872 | tf_op jit(solution)/shard_map/ppermute | solution.py:285
  39.3 14.2 %collective-permute-start.6 = (bf16[1024,256]{1,0:T(8,128)(2,1)}, bf16[1024,256]{1,0:T(8,128)(2,1)S(1)}, u32[]{:S(2)}, u32[]{:S(2)}) collective-permute-start(bf16[1024,256]{1,0:T(8,128)(2,1)} %collective-permute-done.5.refs_7_), channel_id=1, source_target_pairs={{0,32},{32,64},{64,96},{96,128},{128,160},{160,192},{192,224},{224... | collective-permute-start | bytes 1572872 | tf_op jit(solution)/shard_map/ppermute | solution.py:285
  47.2 7.2 %collective-permute-start.3 = (bf16[128,1024]{1,0:T(8,128)(2,1)}, bf16[128,1024]{1,0:T(8,128)(2,1)S(1)}, u32[]{:S(2)}, u32[]{:S(2)}) collective-permute-start(bf16[128,1024]{1,0:T(8,128)(2,1)} %slice.22), channel_id=1, source_target_pairs={{0,24},{8,0},{16,8},{24,16},{1,25},{9,1},{17,9},{25,17},{2,26},{10... | collective-permute-start | bytes 786440 | tf_op jit(solution)/shard_map/ppermute | solution.py:285
  48.8 6.6 %collective-permute-start.2 = (bf16[128,1024]{1,0:T(8,128)(2,1)}, bf16[128,1024]{1,0:T(8,128)(2,1)S(1)}, u32[]{:S(2)}, u32[]{:S(2)}) collective-permute-start(bf16[128,1024]{1,0:T(8,128)(2,1)} %slice.21), channel_id=1, source_target_pairs={{0,8},{8,16},{16,24},{24,0},{1,9},{9,17},{17,25},{25,1},{2,10},{10... | collective-permute-start | bytes 786440 | tf_op jit(solution)/shard_map/ppermute | solution.py:285
  49.9 12.2 %copy-start = (bf16[1024,256]{1,0:T(8,128)(2,1)}, bf16[1024,256]{1,0:T(8,128)(2,1)S(1)}, u32[]{:S(2)}) copy-start(bf16[1024,256]{1,0:T(8,128)(2,1)S(1)} %collective-permute-done.10.refs_11_) | copy-start | bytes 1572868
  50.7 7.0 %collective-permute-start.11 = (bf16[512,256]{1,0:T(8,128)(2,1)}, bf16[512,256]{1,0:T(8,128)(2,1)}, u32[]{:S(2)}, u32[]{:S(2)}) collective-permute-start(bf16[512,256]{1,0:T(8,128)(2,1)} %slice.24), channel_id=1, source_target_pairs={{0,224},{32,0},{64,32},{96,64},{128,96},{160,128},{192,160},{224,1... | collective-permute-start | bytes 786440 | tf_op jit(solution)/shard_map/ppermute | solution.py:285
  54.3 7.9 %collective-permute-start.7 = (bf16[512,256]{1,0:T(8,128)(2,1)}, bf16[512,256]{1,0:T(8,128)(2,1)}, u32[]{:S(2)}, u32[]{:S(2)}) collective-permute-start(bf16[512,256]{1,0:T(8,128)(2,1)} %slice.23), channel_id=1, source_target_pairs={{0,32},{32,64},{64,96},{96,128},{128,160},{160,192},{192,224},{224... | collective-permute-start | bytes 786440 | tf_op jit(solution)/shard_map/ppermute | solution.py:285
  67.9 3.6 %collective-permute-start.12 = (bf16[2,1024,256]{2,1,0:T(8,128)(2,1)}, bf16[2,1024,256]{2,1,0:T(8,128)(2,1)}, u32[]{:S(2)}, u32[]{:S(2)}) collective-permute-start(bf16[2,1024,256]{2,1,0:T(8,128)(2,1)} %get-tuple-element.14), channel_id=1, source_target_pairs={{0,1},{1,0},{2,3},{3,2},{4,5},{5,4},{6,7},{7,6},{8,9},{9,8},{10,11... | collective-permute-start | bytes 3145736 | tf_op jit(solution)/shard_map/ppermute | solution.py:331
  68.0 7.6 %collective-permute-start.13 = (bf16[2,1024,256]{2,1,0:T(8,128)(2,1)}, bf16[2,1024,256]{2,1,0:T(8,128)(2,1)S(1)}, u32[]{:S(2)}, u32[]{:S(2)}) collective-permute-start(bf16[2,1024,256]{2,1,0:T(8,128)(2,1)} %get-tuple-element.17), channel_id=1, source_target_pairs={{0,1},{1,0},{2,3},{3,2},{4,5},{5,4},{6,7},{7,6},{8,9},{9,8},{10,11... | collective-permute-start | bytes 3145736 | tf_op jit(solution)/shard_map/ppermute | solution.py:332
  73.4 9.2 %collective-permute-start.15 = (bf16[512,256]{1,0:T(8,128)(2,1)S(1)}, bf16[512,256]{1,0:T(8,128)(2,1)S(1)}, u32[]{:S(2)}, u32[]{:S(2)}) collective-permute-start(bf16[512,256]{1,0:T(8,128)(2,1)S(1)} %get-tuple-element.19), channel_id=1, source_target_pairs={{0,2},{2,4},{4,6},{6,0},{1,3},{3,5},{5,7},{7,1},{8,10},{10,12},{12... | collective-permute-start | bytes 786440 | tf_op jit(solution)/shard_map/ppermute | solution.py:285
  74.8 9.2 %collective-permute-start.16 = (bf16[512,256]{1,0:T(8,128)(2,1)S(1)}, bf16[512,256]{1,0:T(8,128)(2,1)S(1)}, u32[]{:S(2)}, u32[]{:S(2)}) collective-permute-start(bf16[512,256]{1,0:T(8,128)(2,1)S(1)} %get-tuple-element.15), channel_id=1, source_target_pairs={{0,6},{2,0},{4,2},{6,4},{1,7},{3,1},{5,3},{7,5},{8,14},{10,8},{12,... | collective-permute-start | bytes 786440 | tf_op jit(solution)/shard_map/ppermute | solution.py:285
  78.2 12.6 %collective-permute-start.14 = (bf16[512,256]{1,0:T(8,128)(2,1)S(1)}, bf16[512,256]{1,0:T(8,128)(2,1)S(1)}, u32[]{:S(2)}, u32[]{:S(2)}) collective-permute-start(bf16[512,256]{1,0:T(8,128)(2,1)S(1)} %get-tuple-element.18), channel_id=1, source_target_pairs={{0,2},{2,4},{4,6},{6,0},{1,3},{3,5},{5,7},{7,1},{8,10},{10,12},{12... | collective-permute-start | bytes 786440 | tf_op jit(solution)/shard_map/ppermute | solution.py:285
  79.5 11.2 %collective-permute-start.19 = (bf16[512,256]{1,0:T(8,128)(2,1)S(1)}, bf16[512,256]{1,0:T(8,128)(2,1)S(1)}, u32[]{:S(2)}, u32[]{:S(2)}) collective-permute-start(bf16[512,256]{1,0:T(8,128)(2,1)S(1)} %get-tuple-element.22), channel_id=1, source_target_pairs={{0,6},{2,0},{4,2},{6,4},{1,7},{3,1},{5,3},{7,5},{8,14},{10,8},{12,... | collective-permute-start | bytes 786440 | tf_op jit(solution)/shard_map/ppermute | solution.py:285
  86.6 6.5 %collective-permute-start.17 = (bf16[512,256]{1,0:T(8,128)(2,1)S(1)}, bf16[512,256]{1,0:T(8,128)(2,1)S(1)}, u32[]{:S(2)}, u32[]{:S(2)}) collective-permute-start(bf16[512,256]{1,0:T(8,128)(2,1)S(1)} %get-tuple-element.20), channel_id=1, source_target_pairs={{0,2},{2,4},{4,6},{6,0},{1,3},{3,5},{5,7},{7,1},{8,10},{10,12},{12... | collective-permute-start | bytes 786440 | tf_op jit(solution)/shard_map/ppermute | solution.py:285
  87.3 6.9 %collective-permute-start.18 = (bf16[512,256]{1,0:T(8,128)(2,1)S(1)}, bf16[512,256]{1,0:T(8,128)(2,1)S(1)}, u32[]{:S(2)}, u32[]{:S(2)}) collective-permute-start(bf16[512,256]{1,0:T(8,128)(2,1)S(1)} %get-tuple-element.21), channel_id=1, source_target_pairs={{0,6},{2,0},{4,2},{6,4},{1,7},{3,1},{5,3},{7,5},{8,14},{10,8},{12,... | collective-permute-start | bytes 786440 | tf_op jit(solution)/shard_map/ppermute | solution.py:285
  (1 other events, 8.7 us)

commit v5 on v4

--- a/solution.py
+++ b/solution.py
@@ -200,11 +200,11 @@
     rows = out.shape[2]
     for s in range(sources):
 
-        @pl.loop(0, peers)
+        @pl.loop(0, peers, unroll=8)
         def _(d):
             used[d] = 0
 
-        @pl.loop(0, count)
+        @pl.loop(0, count, unroll=8)
         def _(j, s=s):
             d = dests[s * count + j]
             rank = used[d]

time: 133 us -> 132 us (level)
  no operation moved by 1% of the time
where the time goes in v5:
time: 132 us; the launch traced here: 131 us
  blocking collectives  34.5 us (26%)
  waiting for transfers between devices  34 us (26%)
  starting transfers between devices  33.3 us (25%)
  Pallas kernels  22.6 us (17%)
  local copies, waits for them, and re-layouts  3.76 us (3%)
  other arithmetic  1.7 us (1%)
  between operations  1.45 us (1%)
    all_to_all x1, blocking collectives, per_device(): arrived = lax.all_to_all(outgoing, ('z', 'x'), 0, 0, tiled=True)  34.5 us
    ppermute x18, waiting for transfers between devices, hop(): return lax.ppermute(value, axis, shift(size, step))  28.1 us
    ppermute x18, starting transfers between devices, hop(): return lax.ppermute(value, axis, shift(size, step))  25 us
    pallas_call x5, Pallas kernels, product(): pl.pallas_call(functools.partial(product_kernel, items=len(items), pieces...  14.8 us
    all_to_all x1, starting transfers between devices, per_device(): lax.all_to_all(jnp.broadcast_to(packed[None], (peers,) + packed.shape), (...  7.78 us
    pallas_call x1, Pallas kernels, half_transform(): pl.pallas_call(functools.partial(halves_kernel, orbitals=orbitals), grid_...  5.14 us
    all_to_all x1, waiting for transfers between devices, per_device(): lax.all_to_all(jnp.broadcast_to(packed[None], (peers,) + packed.shape), (...  3.03 us
    ppermute x1, waiting for transfers between devices, per_device(): first = lax.ppermute(first, 'core', swap)  2.89 us
  transfers between devices with their start and end apart: 21, of which 12 were waited for; matrix products, arithmetic and copies ran while one was open for 4% of the time, Pallas kernels for 11%

profile of v5, /device:TPU:18, one launch (start us, length us, event | category | flops | bytes accessed | tf_op | source)
XLA Modules:
  0.0 131.4 jit_solution(5875703894141665481)
XLA Ops:
  0.0 5.9 %collective-permute-start.8 = (bf16[1024,256]{1,0:T(8,128)(2,1)}, bf16[1024,256]{1,0:T(8,128)(2,1)S(1)}, u32[]{:S(2)}, u32[]{:S(2)}) collective-permute-start(bf16[1024,256]{1,0:T(8,128)(2,1)} %refs_5_.9), channel_id=1, source_target_pairs={{0,224},{32,0},{64,32},{96,64},{128,96},{160,128},{192,160},{224,1... | collective-permute-start | bytes 1572872 | tf_op jit(solution)/shard_map/ppermute | solution.py:285
  8.0 7.8 %all-to-all-start = ((bf16[32,8,640]{2,1,0:T(8,128)(2,1)}), bf16[32,8,640]{2,1,0:T(8,128)(2,1)S(1)}, u32[]{:S(2)}, u32[]{:S(2)}) async-start(bf16[32,8,640]{2,1,0:T(8,128)(2,1)} %broadcast_in_dim.10), calls=%async_computation | async-start | bytes 655360 | tf_op jit(solution)/shard_map/all_to_all | solution.py:297
  15.8 5.4 %collective-permute-done.8.refs_13_ = bf16[1024,256]{1,0:T(8,128)(2,1)S(1)} collective-permute-done((bf16[1024,256]{1,0:T(8,128)(2,1)}, bf16[1024,256]{1,0:T(8,128)(2,1)S(1)}, u32[]{:S(2)}, u32[]{:S(2)}) %collective-permute-start.8) | collective-permute-done | bytes 524320 | tf_op jit(solution)/shard_map/ppermute | solution.py:285
  21.2 3.9 %collective-permute-start.9 = (bf16[1024,256]{1,0:T(8,128)(2,1)S(1)}, bf16[1024,256]{1,0:T(8,128)(2,1)}, u32[]{:S(2)}, u32[]{:S(2)}) collective-permute-start(bf16[1024,256]{1,0:T(8,128)(2,1)S(1)} %collective-permute-done.8.refs_13_), channel_id=1, source_target_pairs={{0,224},{32,0},{64,32},{96,64},{128,96},{160,128},{192,160},{224,1... | collective-permute-start | bytes 1572872 | tf_op jit(solution)/shard_map/ppermute | solution.py:285
  27.0 3.0 %all-to-all-done.packed_ref = bf16[32,8,640]{2,1,0:T(8,128)(2,1)S(1)} async-done(((bf16[32,8,640]{2,1,0:T(8,128)(2,1)}), bf16[32,8,640]{2,1,0:T(8,128)(2,1)S(1)}, u32[]{:S(2)}, u32[]{:S(2)}) %all-to-all-start) | async-done | bytes 327712 | tf_op jit(solution)/shard_map/all_to_all | solution.py:297
  30.1 5.1 %halves.1.refs_0_ = bf16[256,1024]{1,0:T(8,128)(2,1)S(1)} custom-call(s32[3]{0:T(128)S(1)} %pad_add_fusion.1.where, bf16[32,8,640]{2,1,0:T(8,128)(2,1)S(1)} %all-to-all-done.packed_ref, bf16[64,64,1024]{2,1,0:T(8,128)(2,1)} %bitcast.24), custom_call_target="tpu_custom_call" | custom-call | flops 1073741824 | bytes 8388608 | tf_op jit(solution)/shard_map/halves/pallas_call | solution.py:52
  37.3 2.0 %collective-permute-start.10 = (bf16[1024,256]{1,0:T(8,128)(2,1)}, bf16[1024,256]{1,0:T(8,128)(2,1)S(1)}, u32[]{:S(2)}, u32[]{:S(2)}) collective-permute-start(bf16[1024,256]{1,0:T(8,128)(2,1)} %collective-permute-done.9.refs_12_), channel_id=1, source_target_pairs={{0,224},{32,0},{64,32},{96,64},{128,96},{160,128},{192,160},{224,1... | collective-permute-start | bytes 1572872 | tf_op jit(solution)/shard_map/ppermute | solution.py:285
  39.4 7.1 %collective-permute-done.1.refs_2_ = bf16[256,1024]{1,0:T(8,128)(2,1)S(1)} collective-permute-done((bf16[256,1024]{1,0:T(8,128)(2,1)S(1)}, bf16[256,1024]{1,0:T(8,128)(2,1)S(1)}, u32[]{:S(2)}, u32[]{:S(2)}) %collective-permute-start.1) | collective-permute-done | bytes 524320 | tf_op jit(solution)/shard_map/ppermute | solution.py:285
  50.7 2.8 %collective-permute-start.11 = (bf16[512,256]{1,0:T(8,128)(2,1)}, bf16[512,256]{1,0:T(8,128)(2,1)}, u32[]{:S(2)}, u32[]{:S(2)}) collective-permute-start(bf16[512,256]{1,0:T(8,128)(2,1)} %slice.24), channel_id=1, source_target_pairs={{0,224},{32,0},{64,32},{96,64},{128,96},{160,128},{192,160},{224,1... | collective-permute-start | bytes 786440 | tf_op jit(solution)/shard_map/ppermute | solution.py:285
  55.4 2.3 %collective-permute-done.11.refs_10_ = bf16[512,256]{1,0:T(8,128)(2,1)} collective-permute-done((bf16[512,256]{1,0:T(8,128)(2,1)}, bf16[512,256]{1,0:T(8,128)(2,1)}, u32[]{:S(2)}, u32[]{:S(2)}) %collective-permute-start.11) | collective-permute-done | bytes 262176 | tf_op jit(solution)/shard_map/ppermute | solution.py:285
  57.7 4.5 %collective-permute-done.7.refs_9_ = bf16[512,256]{1,0:T(8,128)(2,1)} collective-permute-done((bf16[512,256]{1,0:T(8,128)(2,1)}, bf16[512,256]{1,0:T(8,128)(2,1)}, u32[]{:S(2)}, u32[]{:S(2)}) %collective-permute-start.7) | collective-permute-done | bytes 262176 | tf_op jit(solution)/shard_map/ppermute | solution.py:285
  62.2 5.8 %product.5 = (bf16[2,1024,256]{2,1,0:T(8,128)(2,1)}, bf16[2,1024,256]{2,1,0:T(8,128)(2,1)}) custom-call(s32[4]{0:T(128)S(1)} %pad_add_fusion.2.order, bf16[256,1024]{1,0:T(8,128)(2,1)S(1)} %halves.1.refs_0_, bf16[256,1024]{1,0:T(8,128)(2,1)S(1)} %collective-permute-done.refs_1_, bf16[256,1024]{1,0:T(8,128)(2,1)S(1)} %collective-permute-done.1.refs_2_, ...), custom_call_target="tpu_custom_call" | custom-call | flops 2147483648 | bytes 6291456 | tf_op jit(solution)/shard_map/product/pallas_call | solution.py:149
  68.6 2.9 %collective-permute-done.12.refs_14_ = bf16[2,1024,256]{2,1,0:T(8,128)(2,1)} collective-permute-done((bf16[2,1024,256]{2,1,0:T(8,128)(2,1)}, bf16[2,1024,256]{2,1,0:T(8,128)(2,1)}, u32[]{:S(2)}, u32[]{:S(2)}) %collective-permute-start.12) | collective-permute-done | bytes 1048608 | tf_op jit(solution)/shard_map/ppermute | solution.py:331
  71.5 1.9 %product.7 = (bf16[512,256]{1,0:T(8,128)(2,1)S(1)}, bf16[512,256]{1,0:T(8,128)(2,1)S(1)}) custom-call(s32[1]{0:T(128)} %bitcast.18.order, bf16[256,1024]{1,0:T(8,128)(2,1)S(1)} %halves.1.refs_0_, bf16[256,1024]{1,0:T(8,128)(2,1)S(1)} %collective-permute-done.refs_1_, bf16[256,1024]{1,0:T(8,128)(2,1)S(1)} %collective-permute-done.1.refs_2_, ...), custom_call_target="tpu_custom_call" | custom-call | flops 536870912 | bytes 3145728 | tf_op jit(solution)/shard_map/product/pallas_call | solution.py:149
  73.4 1.4 %collective-permute-start.15 = (bf16[512,256]{1,0:T(8,128)(2,1)S(1)}, bf16[512,256]{1,0:T(8,128)(2,1)S(1)}, u32[]{:S(2)}, u32[]{:S(2)}) collective-permute-start(bf16[512,256]{1,0:T(8,128)(2,1)S(1)} %get-tuple-element.19), channel_id=1, source_target_pairs={{0,2},{2,4},{4,6},{6,0},{1,3},{3,5},{5,7},{7,1},{8,10},{10,12},{12... | collective-permute-start | bytes 786440 | tf_op jit(solution)/shard_map/ppermute | solution.py:285
  75.6 2.6 %product.8 = (bf16[512,256]{1,0:T(8,128)(2,1)S(1)}, bf16[512,256]{1,0:T(8,128)(2,1)S(1)}) custom-call(s32[2]{0:T(128)S(1)} %pad_add_fusion.3.order, bf16[256,1024]{1,0:T(8,128)(2,1)S(1)} %halves.1.refs_0_, bf16[256,1024]{1,0:T(8,128)(2,1)S(1)} %collective-permute-done.refs_1_, bf16[256,1024]{1,0:T(8,128)(2,1)S(1)} %collective-permute-done.1.refs_2_, ...), custom_call_target="tpu_custom_call" | custom-call | flops 1073741824 | bytes 4194304 | tf_op jit(solution)/shard_map/product/pallas_call | solution.py:149
  78.2 1.4 %collective-permute-start.14 = (bf16[512,256]{1,0:T(8,128)(2,1)S(1)}, bf16[512,256]{1,0:T(8,128)(2,1)S(1)}, u32[]{:S(2)}, u32[]{:S(2)}) collective-permute-start(bf16[512,256]{1,0:T(8,128)(2,1)S(1)} %get-tuple-element.18), channel_id=1, source_target_pairs={{0,2},{2,4},{4,6},{6,0},{1,3},{3,5},{5,7},{7,1},{8,10},{10,12},{12... | collective-permute-start | bytes 786440 | tf_op jit(solution)/shard_map/ppermute | solution.py:285
  80.3 2.4 %collective-permute-done.15.refs_16_ = bf16[512,256]{1,0:T(8,128)(2,1)S(1)} collective-permute-done((bf16[512,256]{1,0:T(8,128)(2,1)S(1)}, bf16[512,256]{1,0:T(8,128)(2,1)S(1)}, u32[]{:S(2)}, u32[]{:S(2)}) %collective-permute-start.15) | collective-permute-done | bytes 262176 | tf_op jit(solution)/shard_map/ppermute | solution.py:285
  84.0 2.6 %product.9 = (bf16[512,256]{1,0:T(8,128)(2,1)S(1)}, bf16[512,256]{1,0:T(8,128)(2,1)S(1)}) custom-call(s32[2]{0:T(128)S(1)} %pad_add_fusion.3.order, bf16[256,1024]{1,0:T(8,128)(2,1)S(1)} %halves.1.refs_0_, bf16[256,1024]{1,0:T(8,128)(2,1)S(1)} %collective-permute-done.refs_1_, bf16[256,1024]{1,0:T(8,128)(2,1)S(1)} %collective-permute-done.1.refs_2_, ...), custom_call_target="tpu_custom_call" | custom-call | flops 1073741824 | bytes 4194304 | tf_op jit(solution)/shard_map/product/pallas_call | solution.py:149
  87.3 1.4 %collective-permute-start.18 = (bf16[512,256]{1,0:T(8,128)(2,1)S(1)}, bf16[512,256]{1,0:T(8,128)(2,1)S(1)}, u32[]{:S(2)}, u32[]{:S(2)}) collective-permute-start(bf16[512,256]{1,0:T(8,128)(2,1)S(1)} %get-tuple-element.21), channel_id=1, source_target_pairs={{0,6},{2,0},{4,2},{6,4},{1,7},{3,1},{5,3},{7,5},{8,14},{10,8},{12,... | collective-permute-start | bytes 786440 | tf_op jit(solution)/shard_map/ppermute | solution.py:285
  88.8 1.9 %product.6.refs_0_ = bf16[1024,256]{1,0:T(8,128)(2,1)S(1)} custom-call(s32[1]{0:T(128)} %bitcast.5.order, bf16[256,1024]{1,0:T(8,128)(2,1)S(1)} %halves.1.refs_0_, bf16[256,1024]{1,0:T(8,128)(2,1)S(1)} %collective-permute-done.refs_1_, bf16[256,1024]{1,0:T(8,128)(2,1)S(1)} %collective-permute-done.1.refs_2_, ...), custom_call_target="tpu_custom_call" | custom-call | flops 536870912 | bytes 3145728 | tf_op jit(solution)/shard_map/product/pallas_call | solution.py:149
  90.7 2.4 %collective-permute-done.17.refs_2_ = bf16[512,256]{1,0:T(8,128)(2,1)S(1)} collective-permute-done((bf16[512,256]{1,0:T(8,128)(2,1)S(1)}, bf16[512,256]{1,0:T(8,128)(2,1)S(1)}, u32[]{:S(2)}, u32[]{:S(2)}) %collective-permute-start.17) | collective-permute-done | bytes 262176 | tf_op jit(solution)/shard_map/ppermute | solution.py:285
  94.2 1.7 %place.1 = bf16[32,8,8,256]{3,2,1,0:T(8,128)(2,1)S(1)} custom-call(s32[128]{0:T(128)S(1)} %pad_add_fusion.dests, bf16[1024,256]{1,0:T(8,128)(2,1)S(1)} %product.6.refs_0_, bf16[512,256]{1,0:T(8,128)(2,1)S(1)} %collective-permute-done.14.refs_1_, bf16[512,256]{1,0:T(8,128)(2,1)S(1)} %collective-permute-done.17.refs_2_, ...), custom_call_target="tpu_custom_call" | custom-call | flops 1048576 | bytes 2621440 | tf_op jit(solution)/shard_map/place/pallas_call | solution.py:221
  95.9 34.5 %all_to_all.10.part = bf16[32,8,8,256]{3,2,1,0:T(8,128)(2,1)S(1)} all-to-all(bf16[32,8,8,256]{3,2,1,0:T(8,128)(2,1)S(1)} %place.1), channel_id=1, replica_groups=mesh['z'=8,'x'=4,'y'=4,'core'=2] {'z','x'}, dimensions={0} | all-to-all | bytes 2097152 | tf_op jit(solution)/shard_map/all_to_all | solution.py:375
  (48 shorter events, 17.5 us)
Async XLA Ops:
  0.0 21.2 %collective-permute-start.8 = (bf16[1024,256]{1,0:T(8,128)(2,1)}, bf16[1024,256]{1,0:T(8,128)(2,1)S(1)}, u32[]{:S(2)}, u32[]{:S(2)}) collective-permute-start(bf16[1024,256]{1,0:T(8,128)(2,1)} %refs_5_.9), channel_id=1, source_target_pairs={{0,224},{32,0},{64,32},{96,64},{128,96},{160,128},{192,160},{224,1... | collective-permute-start | bytes 1572872 | tf_op jit(solution)/shard_map/ppermute | solution.py:285
  5.9 19.8 %collective-permute-start.4 = (bf16[1024,256]{1,0:T(8,128)(2,1)}, bf16[1024,256]{1,0:T(8,128)(2,1)S(1)}, u32[]{:S(2)}, u32[]{:S(2)}) collective-permute-start(bf16[1024,256]{1,0:T(8,128)(2,1)} %refs_5_.9), channel_id=1, source_target_pairs={{0,32},{32,64},{64,96},{96,128},{128,160},{160,192},{192,224},{224... | collective-permute-start | bytes 1572872 | tf_op jit(solution)/shard_map/ppermute | solution.py:285
  8.0 22.1 %all-to-all-start = ((bf16[32,8,640]{2,1,0:T(8,128)(2,1)}), bf16[32,8,640]{2,1,0:T(8,128)(2,1)S(1)}, u32[]{:S(2)}, u32[]{:S(2)}) async-start(bf16[32,8,640]{2,1,0:T(8,128)(2,1)} %broadcast_in_dim.10), calls=%async_computation | async-start | bytes 655360 | tf_op jit(solution)/shard_map/all_to_all | solution.py:297
  21.2 25.3 %copy-start.2 = (bf16[1024,256]{1,0:T(8,128)(2,1)}, bf16[1024,256]{1,0:T(8,128)(2,1)S(1)}, u32[]{:S(2)}) copy-start(bf16[1024,256]{1,0:T(8,128)(2,1)S(1)} %collective-permute-done.8.refs_13_) | copy-start | bytes 1572868
  21.2 16.1 %collective-permute-start.9 = (bf16[1024,256]{1,0:T(8,128)(2,1)S(1)}, bf16[1024,256]{1,0:T(8,128)(2,1)}, u32[]{:S(2)}, u32[]{:S(2)}) collective-permute-start(bf16[1024,256]{1,0:T(8,128)(2,1)S(1)} %collective-permute-done.8.refs_13_), channel_id=1, source_target_pairs={{0,224},{32,0},{64,32},{96,64},{128,96},{160,128},{192,160},{224,1... | collective-permute-start | bytes 1572872 | tf_op jit(solution)/shard_map/ppermute | solution.py:285
  25.6 13.7 %copy-start.3 = (bf16[1024,256]{1,0:T(8,128)(2,1)}, bf16[1024,256]{1,0:T(8,128)(2,1)S(1)}, u32[]{:S(2)}) copy-start(bf16[1024,256]{1,0:T(8,128)(2,1)S(1)} %collective-permute-done.4.refs_6_) | copy-start | bytes 1572868
  25.6 13.7 %collective-permute-start.5 = (bf16[1024,256]{1,0:T(8,128)(2,1)S(1)}, bf16[1024,256]{1,0:T(8,128)(2,1)}, u32[]{:S(2)}, u32[]{:S(2)}) collective-permute-start(bf16[1024,256]{1,0:T(8,128)(2,1)S(1)} %collective-permute-done.4.refs_6_), channel_id=1, source_target_pairs={{0,32},{32,64},{64,96},{96,128},{128,160},{160,192},{192,224},{224... | collective-permute-start | bytes 1572872 | tf_op jit(solution)/shard_map/ppermute | solution.py:285
  35.2 11.2 %collective-permute-start.1 = (bf16[256,1024]{1,0:T(8,128)(2,1)S(1)}, bf16[256,1024]{1,0:T(8,128)(2,1)S(1)}, u32[]{:S(2)}, u32[]{:S(2)}) collective-permute-start(bf16[256,1024]{1,0:T(8,128)(2,1)S(1)} %halves.1.refs_0_), channel_id=1, source_target_pairs={{0,24},{8,0},{16,8},{24,16},{1,25},{9,1},{17,9},{25,17},{2,26},{10... | collective-permute-start | bytes 1572872 | tf_op jit(solution)/shard_map/ppermute | solution.py:285
  36.2 11.9 %collective-permute-start = (bf16[256,1024]{1,0:T(8,128)(2,1)S(1)}, bf16[256,1024]{1,0:T(8,128)(2,1)S(1)}, u32[]{:S(2)}, u32[]{:S(2)}) collective-permute-start(bf16[256,1024]{1,0:T(8,128)(2,1)S(1)} %halves.1.refs_0_), channel_id=1, source_target_pairs={{0,8},{8,16},{16,24},{24,0},{1,9},{9,17},{17,25},{25,1},{2,10},{10... | collective-permute-start | bytes 1572872 | tf_op jit(solution)/shard_map/ppermute | solution.py:285
  37.3 12.6 %collective-permute-start.10 = (bf16[1024,256]{1,0:T(8,128)(2,1)}, bf16[1024,256]{1,0:T(8,128)(2,1)S(1)}, u32[]{:S(2)}, u32[]{:S(2)}) collective-permute-start(bf16[1024,256]{1,0:T(8,128)(2,1)} %collective-permute-done.9.refs_12_), channel_id=1, source_target_pairs={{0,224},{32,0},{64,32},{96,64},{128,96},{160,128},{192,160},{224,1... | collective-permute-start | bytes 1572872 | tf_op jit(solution)/shard_map/ppermute | solution.py:285
  39.3 14.2 %collective-permute-start.6 = (bf16[1024,256]{1,0:T(8,128)(2,1)}, bf16[1024,256]{1,0:T(8,128)(2,1)S(1)}, u32[]{:S(2)}, u32[]{:S(2)}) collective-permute-start(bf16[1024,256]{1,0:T(8,128)(2,1)} %collective-permute-done.5.refs_7_), channel_id=1, source_target_pairs={{0,32},{32,64},{64,96},{96,128},{128,160},{160,192},{192,224},{224... | collective-permute-start | bytes 1572872 | tf_op jit(solution)/shard_map/ppermute | solution.py:285
  47.2 7.2 %collective-permute-start.3 = (bf16[128,1024]{1,0:T(8,128)(2,1)}, bf16[128,1024]{1,0:T(8,128)(2,1)S(1)}, u32[]{:S(2)}, u32[]{:S(2)}) collective-permute-start(bf16[128,1024]{1,0:T(8,128)(2,1)} %slice.22), channel_id=1, source_target_pairs={{0,24},{8,0},{16,8},{24,16},{1,25},{9,1},{17,9},{25,17},{2,26},{10... | collective-permute-start | bytes 786440 | tf_op jit(solution)/shard_map/ppermute | solution.py:285
  48.8 6.6 %collective-permute-start.2 = (bf16[128,1024]{1,0:T(8,128)(2,1)}, bf16[128,1024]{1,0:T(8,128)(2,1)S(1)}, u32[]{:S(2)}, u32[]{:S(2)}) collective-permute-start(bf16[128,1024]{1,0:T(8,128)(2,1)} %slice.21), channel_id=1, source_target_pairs={{0,8},{8,16},{16,24},{24,0},{1,9},{9,17},{17,25},{25,1},{2,10},{10... | collective-permute-start | bytes 786440 | tf_op jit(solution)/shard_map/ppermute | solution.py:285
  49.9 12.2 %copy-start = (bf16[1024,256]{1,0:T(8,128)(2,1)}, bf16[1024,256]{1,0:T(8,128)(2,1)S(1)}, u32[]{:S(2)}) copy-start(bf16[1024,256]{1,0:T(8,128)(2,1)S(1)} %collective-permute-done.10.refs_11_) | copy-start | bytes 1572868
  50.7 7.0 %collective-permute-start.11 = (bf16[512,256]{1,0:T(8,128)(2,1)}, bf16[512,256]{1,0:T(8,128)(2,1)}, u32[]{:S(2)}, u32[]{:S(2)}) collective-permute-start(bf16[512,256]{1,0:T(8,128)(2,1)} %slice.24), channel_id=1, source_target_pairs={{0,224},{32,0},{64,32},{96,64},{128,96},{160,128},{192,160},{224,1... | collective-permute-start | bytes 786440 | tf_op jit(solution)/shard_map/ppermute | solution.py:285
  54.3 7.9 %collective-permute-start.7 = (bf16[512,256]{1,0:T(8,128)(2,1)}, bf16[512,256]{1,0:T(8,128)(2,1)}, u32[]{:S(2)}, u32[]{:S(2)}) collective-permute-start(bf16[512,256]{1,0:T(8,128)(2,1)} %slice.23), channel_id=1, source_target_pairs={{0,32},{32,64},{64,96},{96,128},{128,160},{160,192},{192,224},{224... | collective-permute-start | bytes 786440 | tf_op jit(solution)/shard_map/ppermute | solution.py:285
  67.9 3.6 %collective-permute-start.12 = (bf16[2,1024,256]{2,1,0:T(8,128)(2,1)}, bf16[2,1024,256]{2,1,0:T(8,128)(2,1)}, u32[]{:S(2)}, u32[]{:S(2)}) collective-permute-start(bf16[2,1024,256]{2,1,0:T(8,128)(2,1)} %get-tuple-element.14), channel_id=1, source_target_pairs={{0,1},{1,0},{2,3},{3,2},{4,5},{5,4},{6,7},{7,6},{8,9},{9,8},{10,11... | collective-permute-start | bytes 3145736 | tf_op jit(solution)/shard_map/ppermute | solution.py:331
  68.0 7.6 %collective-permute-start.13 = (bf16[2,1024,256]{2,1,0:T(8,128)(2,1)}, bf16[2,1024,256]{2,1,0:T(8,128)(2,1)S(1)}, u32[]{:S(2)}, u32[]{:S(2)}) collective-permute-start(bf16[2,1024,256]{2,1,0:T(8,128)(2,1)} %get-tuple-element.17), channel_id=1, source_target_pairs={{0,1},{1,0},{2,3},{3,2},{4,5},{5,4},{6,7},{7,6},{8,9},{9,8},{10,11... | collective-permute-start | bytes 3145736 | tf_op jit(solution)/shard_map/ppermute | solution.py:332
  73.4 9.2 %collective-permute-start.15 = (bf16[512,256]{1,0:T(8,128)(2,1)S(1)}, bf16[512,256]{1,0:T(8,128)(2,1)S(1)}, u32[]{:S(2)}, u32[]{:S(2)}) collective-permute-start(bf16[512,256]{1,0:T(8,128)(2,1)S(1)} %get-tuple-element.19), channel_id=1, source_target_pairs={{0,2},{2,4},{4,6},{6,0},{1,3},{3,5},{5,7},{7,1},{8,10},{10,12},{12... | collective-permute-start | bytes 786440 | tf_op jit(solution)/shard_map/ppermute | solution.py:285
  74.8 9.2 %collective-permute-start.16 = (bf16[512,256]{1,0:T(8,128)(2,1)S(1)}, bf16[512,256]{1,0:T(8,128)(2,1)S(1)}, u32[]{:S(2)}, u32[]{:S(2)}) collective-permute-start(bf16[512,256]{1,0:T(8,128)(2,1)S(1)} %get-tuple-element.15), channel_id=1, source_target_pairs={{0,6},{2,0},{4,2},{6,4},{1,7},{3,1},{5,3},{7,5},{8,14},{10,8},{12,... | collective-permute-start | bytes 786440 | tf_op jit(solution)/shard_map/ppermute | solution.py:285
  78.2 12.6 %collective-permute-start.14 = (bf16[512,256]{1,0:T(8,128)(2,1)S(1)}, bf16[512,256]{1,0:T(8,128)(2,1)S(1)}, u32[]{:S(2)}, u32[]{:S(2)}) collective-permute-start(bf16[512,256]{1,0:T(8,128)(2,1)S(1)} %get-tuple-element.18), channel_id=1, source_target_pairs={{0,2},{2,4},{4,6},{6,0},{1,3},{3,5},{5,7},{7,1},{8,10},{10,12},{12... | collective-permute-start | bytes 786440 | tf_op jit(solution)/shard_map/ppermute | solution.py:285
  79.5 11.2 %collective-permute-start.19 = (bf16[512,256]{1,0:T(8,128)(2,1)S(1)}, bf16[512,256]{1,0:T(8,128)(2,1)S(1)}, u32[]{:S(2)}, u32[]{:S(2)}) collective-permute-start(bf16[512,256]{1,0:T(8,128)(2,1)S(1)} %get-tuple-element.22), channel_id=1, source_target_pairs={{0,6},{2,0},{4,2},{6,4},{1,7},{3,1},{5,3},{7,5},{8,14},{10,8},{12,... | collective-permute-start | bytes 786440 | tf_op jit(solution)/shard_map/ppermute | solution.py:285
  86.6 6.5 %collective-permute-start.17 = (bf16[512,256]{1,0:T(8,128)(2,1)S(1)}, bf16[512,256]{1,0:T(8,128)(2,1)S(1)}, u32[]{:S(2)}, u32[]{:S(2)}) collective-permute-start(bf16[512,256]{1,0:T(8,128)(2,1)S(1)} %get-tuple-element.20), channel_id=1, source_target_pairs={{0,2},{2,4},{4,6},{6,0},{1,3},{3,5},{5,7},{7,1},{8,10},{10,12},{12... | collective-permute-start | bytes 786440 | tf_op jit(solution)/shard_map/ppermute | solution.py:285
  87.3 6.9 %collective-permute-start.18 = (bf16[512,256]{1,0:T(8,128)(2,1)S(1)}, bf16[512,256]{1,0:T(8,128)(2,1)S(1)}, u32[]{:S(2)}, u32[]{:S(2)}) collective-permute-start(bf16[512,256]{1,0:T(8,128)(2,1)S(1)} %get-tuple-element.21), channel_id=1, source_target_pairs={{0,6},{2,0},{4,2},{6,4},{1,7},{3,1},{5,3},{7,5},{8,14},{10,8},{12,... | collective-permute-start | bytes 786440 | tf_op jit(solution)/shard_map/ppermute | solution.py:285
  (1 other events, 8.7 us)

commit v6 on v5

--- a/solution.py
+++ b/solution.py
@@ -204,7 +204,7 @@
         def _(d):
             used[d] = 0
 
-        @pl.loop(0, count, unroll=8)
+        @pl.loop(0, count, unroll=32)
         def _(j, s=s):
             d = dests[s * count + j]
             rank = used[d]

time: 132 us -> 132 us (level)
  no operation moved by 1% of the time
where the time goes in v6:
time: 132 us; the launch traced here: 131 us
  blocking collectives  34.5 us (26%)
  waiting for transfers between devices  34 us (26%)
  starting transfers between devices  33.3 us (25%)
  Pallas kernels  22.6 us (17%)
  local copies, waits for them, and re-layouts  3.76 us (3%)
  other arithmetic  1.7 us (1%)
  between operations  1.45 us (1%)
    all_to_all x1, blocking collectives, per_device(): arrived = lax.all_to_all(outgoing, ('z', 'x'), 0, 0, tiled=True)  34.5 us
    ppermute x18, waiting for transfers between devices, hop(): return lax.ppermute(value, axis, shift(size, step))  28.1 us
    ppermute x18, starting transfers between devices, hop(): return lax.ppermute(value, axis, shift(size, step))  25 us
    pallas_call x5, Pallas kernels, product(): pl.pallas_call(functools.partial(product_kernel, items=len(items), pieces...  14.8 us
    all_to_all x1, starting transfers between devices, per_device(): lax.all_to_all(jnp.broadcast_to(packed[None], (peers,) + packed.shape), (...  7.78 us
    pallas_call x1, Pallas kernels, half_transform(): pl.pallas_call(functools.partial(halves_kernel, orbitals=orbitals), grid_...  5.14 us
    all_to_all x1, waiting for transfers between devices, per_device(): lax.all_to_all(jnp.broadcast_to(packed[None], (peers,) + packed.shape), (...  3.03 us
    ppermute x1, waiting for transfers between devices, per_device(): first = lax.ppermute(first, 'core', swap)  2.89 us
  transfers between devices with their start and end apart: 21, of which 12 were waited for; matrix products, arithmetic and copies ran while one was open for 4% of the time, Pallas kernels for 11%

profile of v6, /device:TPU:18, one launch (start us, length us, event | category | flops | bytes accessed | tf_op | source)
XLA Modules:
  0.0 131.3 jit_solution(11301559467258468392)
XLA Ops:
  0.0 5.9 %collective-permute-start.8 = (bf16[1024,256]{1,0:T(8,128)(2,1)}, bf16[1024,256]{1,0:T(8,128)(2,1)S(1)}, u32[]{:S(2)}, u32[]{:S(2)}) collective-permute-start(bf16[1024,256]{1,0:T(8,128)(2,1)} %refs_5_.9), channel_id=1, source_target_pairs={{0,224},{32,0},{64,32},{96,64},{128,96},{160,128},{192,160},{224,1... | collective-permute-start | bytes 1572872 | tf_op jit(solution)/shard_map/ppermute | solution.py:285
  8.0 7.8 %all-to-all-start = ((bf16[32,8,640]{2,1,0:T(8,128)(2,1)}), bf16[32,8,640]{2,1,0:T(8,128)(2,1)S(1)}, u32[]{:S(2)}, u32[]{:S(2)}) async-start(bf16[32,8,640]{2,1,0:T(8,128)(2,1)} %broadcast_in_dim.10), calls=%async_computation | async-start | bytes 655360 | tf_op jit(solution)/shard_map/all_to_all | solution.py:297
  15.8 5.4 %collective-permute-done.8.refs_13_ = bf16[1024,256]{1,0:T(8,128)(2,1)S(1)} collective-permute-done((bf16[1024,256]{1,0:T(8,128)(2,1)}, bf16[1024,256]{1,0:T(8,128)(2,1)S(1)}, u32[]{:S(2)}, u32[]{:S(2)}) %collective-permute-start.8) | collective-permute-done | bytes 524320 | tf_op jit(solution)/shard_map/ppermute | solution.py:285
  21.2 3.9 %collective-permute-start.9 = (bf16[1024,256]{1,0:T(8,128)(2,1)S(1)}, bf16[1024,256]{1,0:T(8,128)(2,1)}, u32[]{:S(2)}, u32[]{:S(2)}) collective-permute-start(bf16[1024,256]{1,0:T(8,128)(2,1)S(1)} %collective-permute-done.8.refs_13_), channel_id=1, source_target_pairs={{0,224},{32,0},{64,32},{96,64},{128,96},{160,128},{192,160},{224,1... | collective-permute-start | bytes 1572872 | tf_op jit(solution)/shard_map/ppermute | solution.py:285
  27.0 3.0 %all-to-all-done.packed_ref = bf16[32,8,640]{2,1,0:T(8,128)(2,1)S(1)} async-done(((bf16[32,8,640]{2,1,0:T(8,128)(2,1)}), bf16[32,8,640]{2,1,0:T(8,128)(2,1)S(1)}, u32[]{:S(2)}, u32[]{:S(2)}) %all-to-all-start) | async-done | bytes 327712 | tf_op jit(solution)/shard_map/all_to_all | solution.py:297
  30.1 5.1 %halves.1.refs_0_ = bf16[256,1024]{1,0:T(8,128)(2,1)S(1)} custom-call(s32[3]{0:T(128)S(1)} %pad_add_fusion.1.where, bf16[32,8,640]{2,1,0:T(8,128)(2,1)S(1)} %all-to-all-done.packed_ref, bf16[64,64,1024]{2,1,0:T(8,128)(2,1)} %bitcast.24), custom_call_target="tpu_custom_call" | custom-call | flops 1073741824 | bytes 8388608 | tf_op jit(solution)/shard_map/halves/pallas_call | solution.py:52
  37.3 2.0 %collective-permute-start.10 = (bf16[1024,256]{1,0:T(8,128)(2,1)}, bf16[1024,256]{1,0:T(8,128)(2,1)S(1)}, u32[]{:S(2)}, u32[]{:S(2)}) collective-permute-start(bf16[1024,256]{1,0:T(8,128)(2,1)} %collective-permute-done.9.refs_12_), channel_id=1, source_target_pairs={{0,224},{32,0},{64,32},{96,64},{128,96},{160,128},{192,160},{224,1... | collective-permute-start | bytes 1572872 | tf_op jit(solution)/shard_map/ppermute | solution.py:285
  39.4 7.1 %collective-permute-done.1.refs_2_ = bf16[256,1024]{1,0:T(8,128)(2,1)S(1)} collective-permute-done((bf16[256,1024]{1,0:T(8,128)(2,1)S(1)}, bf16[256,1024]{1,0:T(8,128)(2,1)S(1)}, u32[]{:S(2)}, u32[]{:S(2)}) %collective-permute-start.1) | collective-permute-done | bytes 524320 | tf_op jit(solution)/shard_map/ppermute | solution.py:285
  50.7 2.8 %collective-permute-start.11 = (bf16[512,256]{1,0:T(8,128)(2,1)}, bf16[512,256]{1,0:T(8,128)(2,1)}, u32[]{:S(2)}, u32[]{:S(2)}) collective-permute-start(bf16[512,256]{1,0:T(8,128)(2,1)} %slice.24), channel_id=1, source_target_pairs={{0,224},{32,0},{64,32},{96,64},{128,96},{160,128},{192,160},{224,1... | collective-permute-start | bytes 786440 | tf_op jit(solution)/shard_map/ppermute | solution.py:285
  55.4 2.3 %collective-permute-done.11.refs_10_ = bf16[512,256]{1,0:T(8,128)(2,1)} collective-permute-done((bf16[512,256]{1,0:T(8,128)(2,1)}, bf16[512,256]{1,0:T(8,128)(2,1)}, u32[]{:S(2)}, u32[]{:S(2)}) %collective-permute-start.11) | collective-permute-done | bytes 262176 | tf_op jit(solution)/shard_map/ppermute | solution.py:285
  57.7 4.5 %collective-permute-done.7.refs_9_ = bf16[512,256]{1,0:T(8,128)(2,1)} collective-permute-done((bf16[512,256]{1,0:T(8,128)(2,1)}, bf16[512,256]{1,0:T(8,128)(2,1)}, u32[]{:S(2)}, u32[]{:S(2)}) %collective-permute-start.7) | collective-permute-done | bytes 262176 | tf_op jit(solution)/shard_map/ppermute | solution.py:285
  62.2 5.8 %product.5 = (bf16[2,1024,256]{2,1,0:T(8,128)(2,1)}, bf16[2,1024,256]{2,1,0:T(8,128)(2,1)}) custom-call(s32[4]{0:T(128)S(1)} %pad_add_fusion.2.order, bf16[256,1024]{1,0:T(8,128)(2,1)S(1)} %halves.1.refs_0_, bf16[256,1024]{1,0:T(8,128)(2,1)S(1)} %collective-permute-done.refs_1_, bf16[256,1024]{1,0:T(8,128)(2,1)S(1)} %collective-permute-done.1.refs_2_, ...), custom_call_target="tpu_custom_call" | custom-call | flops 2147483648 | bytes 6291456 | tf_op jit(solution)/shard_map/product/pallas_call | solution.py:149
  68.6 2.9 %collective-permute-done.12.refs_14_ = bf16[2,1024,256]{2,1,0:T(8,128)(2,1)} collective-permute-done((bf16[2,1024,256]{2,1,0:T(8,128)(2,1)}, bf16[2,1024,256]{2,1,0:T(8,128)(2,1)}, u32[]{:S(2)}, u32[]{:S(2)}) %collective-permute-start.12) | collective-permute-done | bytes 1048608 | tf_op jit(solution)/shard_map/ppermute | solution.py:331
  71.5 1.9 %product.7 = (bf16[512,256]{1,0:T(8,128)(2,1)S(1)}, bf16[512,256]{1,0:T(8,128)(2,1)S(1)}) custom-call(s32[1]{0:T(128)} %bitcast.18.order, bf16[256,1024]{1,0:T(8,128)(2,1)S(1)} %halves.1.refs_0_, bf16[256,1024]{1,0:T(8,128)(2,1)S(1)} %collective-permute-done.refs_1_, bf16[256,1024]{1,0:T(8,128)(2,1)S(1)} %collective-permute-done.1.refs_2_, ...), custom_call_target="tpu_custom_call" | custom-call | flops 536870912 | bytes 3145728 | tf_op jit(solution)/shard_map/product/pallas_call | solution.py:149
  73.4 1.4 %collective-permute-start.15 = (bf16[512,256]{1,0:T(8,128)(2,1)S(1)}, bf16[512,256]{1,0:T(8,128)(2,1)S(1)}, u32[]{:S(2)}, u32[]{:S(2)}) collective-permute-start(bf16[512,256]{1,0:T(8,128)(2,1)S(1)} %get-tuple-element.19), channel_id=1, source_target_pairs={{0,2},{2,4},{4,6},{6,0},{1,3},{3,5},{5,7},{7,1},{8,10},{10,12},{12... | collective-permute-start | bytes 786440 | tf_op jit(solution)/shard_map/ppermute | solution.py:285
  75.6 2.6 %product.8 = (bf16[512,256]{1,0:T(8,128)(2,1)S(1)}, bf16[512,256]{1,0:T(8,128)(2,1)S(1)}) custom-call(s32[2]{0:T(128)S(1)} %pad_add_fusion.3.order, bf16[256,1024]{1,0:T(8,128)(2,1)S(1)} %halves.1.refs_0_, bf16[256,1024]{1,0:T(8,128)(2,1)S(1)} %collective-permute-done.refs_1_, bf16[256,1024]{1,0:T(8,128)(2,1)S(1)} %collective-permute-done.1.refs_2_, ...), custom_call_target="tpu_custom_call" | custom-call | flops 1073741824 | bytes 4194304 | tf_op jit(solution)/shard_map/product/pallas_call | solution.py:149
  78.2 1.4 %collective-permute-start.14 = (bf16[512,256]{1,0:T(8,128)(2,1)S(1)}, bf16[512,256]{1,0:T(8,128)(2,1)S(1)}, u32[]{:S(2)}, u32[]{:S(2)}) collective-permute-start(bf16[512,256]{1,0:T(8,128)(2,1)S(1)} %get-tuple-element.18), channel_id=1, source_target_pairs={{0,2},{2,4},{4,6},{6,0},{1,3},{3,5},{5,7},{7,1},{8,10},{10,12},{12... | collective-permute-start | bytes 786440 | tf_op jit(solution)/shard_map/ppermute | solution.py:285
  80.3 2.4 %collective-permute-done.15.refs_16_ = bf16[512,256]{1,0:T(8,128)(2,1)S(1)} collective-permute-done((bf16[512,256]{1,0:T(8,128)(2,1)S(1)}, bf16[512,256]{1,0:T(8,128)(2,1)S(1)}, u32[]{:S(2)}, u32[]{:S(2)}) %collective-permute-start.15) | collective-permute-done | bytes 262176 | tf_op jit(solution)/shard_map/ppermute | solution.py:285
  84.0 2.6 %product.9 = (bf16[512,256]{1,0:T(8,128)(2,1)S(1)}, bf16[512,256]{1,0:T(8,128)(2,1)S(1)}) custom-call(s32[2]{0:T(128)S(1)} %pad_add_fusion.3.order, bf16[256,1024]{1,0:T(8,128)(2,1)S(1)} %halves.1.refs_0_, bf16[256,1024]{1,0:T(8,128)(2,1)S(1)} %collective-permute-done.refs_1_, bf16[256,1024]{1,0:T(8,128)(2,1)S(1)} %collective-permute-done.1.refs_2_, ...), custom_call_target="tpu_custom_call" | custom-call | flops 1073741824 | bytes 4194304 | tf_op jit(solution)/shard_map/product/pallas_call | solution.py:149
  87.3 1.4 %collective-permute-start.18 = (bf16[512,256]{1,0:T(8,128)(2,1)S(1)}, bf16[512,256]{1,0:T(8,128)(2,1)S(1)}, u32[]{:S(2)}, u32[]{:S(2)}) collective-permute-start(bf16[512,256]{1,0:T(8,128)(2,1)S(1)} %get-tuple-element.21), channel_id=1, source_target_pairs={{0,6},{2,0},{4,2},{6,4},{1,7},{3,1},{5,3},{7,5},{8,14},{10,8},{12,... | collective-permute-start | bytes 786440 | tf_op jit(solution)/shard_map/ppermute | solution.py:285
  88.8 1.9 %product.6.refs_0_ = bf16[1024,256]{1,0:T(8,128)(2,1)S(1)} custom-call(s32[1]{0:T(128)} %bitcast.5.order, bf16[256,1024]{1,0:T(8,128)(2,1)S(1)} %halves.1.refs_0_, bf16[256,1024]{1,0:T(8,128)(2,1)S(1)} %collective-permute-done.refs_1_, bf16[256,1024]{1,0:T(8,128)(2,1)S(1)} %collective-permute-done.1.refs_2_, ...), custom_call_target="tpu_custom_call" | custom-call | flops 536870912 | bytes 3145728 | tf_op jit(solution)/shard_map/product/pallas_call | solution.py:149
  90.7 2.4 %collective-permute-done.17.refs_2_ = bf16[512,256]{1,0:T(8,128)(2,1)S(1)} collective-permute-done((bf16[512,256]{1,0:T(8,128)(2,1)S(1)}, bf16[512,256]{1,0:T(8,128)(2,1)S(1)}, u32[]{:S(2)}, u32[]{:S(2)}) %collective-permute-start.17) | collective-permute-done | bytes 262176 | tf_op jit(solution)/shard_map/ppermute | solution.py:285
  94.2 1.6 %place.1 = bf16[32,8,8,256]{3,2,1,0:T(8,128)(2,1)S(1)} custom-call(s32[128]{0:T(128)S(1)} %pad_add_fusion.dests, bf16[1024,256]{1,0:T(8,128)(2,1)S(1)} %product.6.refs_0_, bf16[512,256]{1,0:T(8,128)(2,1)S(1)} %collective-permute-done.14.refs_1_, bf16[512,256]{1,0:T(8,128)(2,1)S(1)} %collective-permute-done.17.refs_2_, ...), custom_call_target="tpu_custom_call" | custom-call | flops 1048576 | bytes 2621440 | tf_op jit(solution)/shard_map/place/pallas_call | solution.py:221
  95.9 34.5 %all_to_all.10.part = bf16[32,8,8,256]{3,2,1,0:T(8,128)(2,1)S(1)} all-to-all(bf16[32,8,8,256]{3,2,1,0:T(8,128)(2,1)S(1)} %place.1), channel_id=1, replica_groups=mesh['z'=8,'x'=4,'y'=4,'core'=2] {'z','x'}, dimensions={0} | all-to-all | bytes 2097152 | tf_op jit(solution)/shard_map/all_to_all | solution.py:375
  (48 shorter events, 17.5 us)
Async XLA Ops:
  0.0 21.2 %collective-permute-start.8 = (bf16[1024,256]{1,0:T(8,128)(2,1)}, bf16[1024,256]{1,0:T(8,128)(2,1)S(1)}, u32[]{:S(2)}, u32[]{:S(2)}) collective-permute-start(bf16[1024,256]{1,0:T(8,128)(2,1)} %refs_5_.9), channel_id=1, source_target_pairs={{0,224},{32,0},{64,32},{96,64},{128,96},{160,128},{192,160},{224,1... | collective-permute-start | bytes 1572872 | tf_op jit(solution)/shard_map/ppermute | solution.py:285
  5.9 19.8 %collective-permute-start.4 = (bf16[1024,256]{1,0:T(8,128)(2,1)}, bf16[1024,256]{1,0:T(8,128)(2,1)S(1)}, u32[]{:S(2)}, u32[]{:S(2)}) collective-permute-start(bf16[1024,256]{1,0:T(8,128)(2,1)} %refs_5_.9), channel_id=1, source_target_pairs={{0,32},{32,64},{64,96},{96,128},{128,160},{160,192},{192,224},{224... | collective-permute-start | bytes 1572872 | tf_op jit(solution)/shard_map/ppermute | solution.py:285
  8.0 22.1 %all-to-all-start = ((bf16[32,8,640]{2,1,0:T(8,128)(2,1)}), bf16[32,8,640]{2,1,0:T(8,128)(2,1)S(1)}, u32[]{:S(2)}, u32[]{:S(2)}) async-start(bf16[32,8,640]{2,1,0:T(8,128)(2,1)} %broadcast_in_dim.10), calls=%async_computation | async-start | bytes 655360 | tf_op jit(solution)/shard_map/all_to_all | solution.py:297
  21.2 25.3 %copy-start.2 = (bf16[1024,256]{1,0:T(8,128)(2,1)}, bf16[1024,256]{1,0:T(8,128)(2,1)S(1)}, u32[]{:S(2)}) copy-start(bf16[1024,256]{1,0:T(8,128)(2,1)S(1)} %collective-permute-done.8.refs_13_) | copy-start | bytes 1572868
  21.2 16.1 %collective-permute-start.9 = (bf16[1024,256]{1,0:T(8,128)(2,1)S(1)}, bf16[1024,256]{1,0:T(8,128)(2,1)}, u32[]{:S(2)}, u32[]{:S(2)}) collective-permute-start(bf16[1024,256]{1,0:T(8,128)(2,1)S(1)} %collective-permute-done.8.refs_13_), channel_id=1, source_target_pairs={{0,224},{32,0},{64,32},{96,64},{128,96},{160,128},{192,160},{224,1... | collective-permute-start | bytes 1572872 | tf_op jit(solution)/shard_map/ppermute | solution.py:285
  25.6 13.7 %copy-start.3 = (bf16[1024,256]{1,0:T(8,128)(2,1)}, bf16[1024,256]{1,0:T(8,128)(2,1)S(1)}, u32[]{:S(2)}) copy-start(bf16[1024,256]{1,0:T(8,128)(2,1)S(1)} %collective-permute-done.4.refs_6_) | copy-start | bytes 1572868
  25.6 13.7 %collective-permute-start.5 = (bf16[1024,256]{1,0:T(8,128)(2,1)S(1)}, bf16[1024,256]{1,0:T(8,128)(2,1)}, u32[]{:S(2)}, u32[]{:S(2)}) collective-permute-start(bf16[1024,256]{1,0:T(8,128)(2,1)S(1)} %collective-permute-done.4.refs_6_), channel_id=1, source_target_pairs={{0,32},{32,64},{64,96},{96,128},{128,160},{160,192},{192,224},{224... | collective-permute-start | bytes 1572872 | tf_op jit(solution)/shard_map/ppermute | solution.py:285
  35.2 11.2 %collective-permute-start.1 = (bf16[256,1024]{1,0:T(8,128)(2,1)S(1)}, bf16[256,1024]{1,0:T(8,128)(2,1)S(1)}, u32[]{:S(2)}, u32[]{:S(2)}) collective-permute-start(bf16[256,1024]{1,0:T(8,128)(2,1)S(1)} %halves.1.refs_0_), channel_id=1, source_target_pairs={{0,24},{8,0},{16,8},{24,16},{1,25},{9,1},{17,9},{25,17},{2,26},{10... | collective-permute-start | bytes 1572872 | tf_op jit(solution)/shard_map/ppermute | solution.py:285
  36.2 11.9 %collective-permute-start = (bf16[256,1024]{1,0:T(8,128)(2,1)S(1)}, bf16[256,1024]{1,0:T(8,128)(2,1)S(1)}, u32[]{:S(2)}, u32[]{:S(2)}) collective-permute-start(bf16[256,1024]{1,0:T(8,128)(2,1)S(1)} %halves.1.refs_0_), channel_id=1, source_target_pairs={{0,8},{8,16},{16,24},{24,0},{1,9},{9,17},{17,25},{25,1},{2,10},{10... | collective-permute-start | bytes 1572872 | tf_op jit(solution)/shard_map/ppermute | solution.py:285
  37.3 12.6 %collective-permute-start.10 = (bf16[1024,256]{1,0:T(8,128)(2,1)}, bf16[1024,256]{1,0:T(8,128)(2,1)S(1)}, u32[]{:S(2)}, u32[]{:S(2)}) collective-permute-start(bf16[1024,256]{1,0:T(8,128)(2,1)} %collective-permute-done.9.refs_12_), channel_id=1, source_target_pairs={{0,224},{32,0},{64,32},{96,64},{128,96},{160,128},{192,160},{224,1... | collective-permute-start | bytes 1572872 | tf_op jit(solution)/shard_map/ppermute | solution.py:285
  39.3 14.2 %collective-permute-start.6 = (bf16[1024,256]{1,0:T(8,128)(2,1)}, bf16[1024,256]{1,0:T(8,128)(2,1)S(1)}, u32[]{:S(2)}, u32[]{:S(2)}) collective-permute-start(bf16[1024,256]{1,0:T(8,128)(2,1)} %collective-permute-done.5.refs_7_), channel_id=1, source_target_pairs={{0,32},{32,64},{64,96},{96,128},{128,160},{160,192},{192,224},{224... | collective-permute-start | bytes 1572872 | tf_op jit(solution)/shard_map/ppermute | solution.py:285
  47.2 7.2 %collective-permute-start.3 = (bf16[128,1024]{1,0:T(8,128)(2,1)}, bf16[128,1024]{1,0:T(8,128)(2,1)S(1)}, u32[]{:S(2)}, u32[]{:S(2)}) collective-permute-start(bf16[128,1024]{1,0:T(8,128)(2,1)} %slice.22), channel_id=1, source_target_pairs={{0,24},{8,0},{16,8},{24,16},{1,25},{9,1},{17,9},{25,17},{2,26},{10... | collective-permute-start | bytes 786440 | tf_op jit(solution)/shard_map/ppermute | solution.py:285
  48.8 6.6 %collective-permute-start.2 = (bf16[128,1024]{1,0:T(8,128)(2,1)}, bf16[128,1024]{1,0:T(8,128)(2,1)S(1)}, u32[]{:S(2)}, u32[]{:S(2)}) collective-permute-start(bf16[128,1024]{1,0:T(8,128)(2,1)} %slice.21), channel_id=1, source_target_pairs={{0,8},{8,16},{16,24},{24,0},{1,9},{9,17},{17,25},{25,1},{2,10},{10... | collective-permute-start | bytes 786440 | tf_op jit(solution)/shard_map/ppermute | solution.py:285
  49.9 12.2 %copy-start = (bf16[1024,256]{1,0:T(8,128)(2,1)}, bf16[1024,256]{1,0:T(8,128)(2,1)S(1)}, u32[]{:S(2)}) copy-start(bf16[1024,256]{1,0:T(8,128)(2,1)S(1)} %collective-permute-done.10.refs_11_) | copy-start | bytes 1572868
  50.7 7.0 %collective-permute-start.11 = (bf16[512,256]{1,0:T(8,128)(2,1)}, bf16[512,256]{1,0:T(8,128)(2,1)}, u32[]{:S(2)}, u32[]{:S(2)}) collective-permute-start(bf16[512,256]{1,0:T(8,128)(2,1)} %slice.24), channel_id=1, source_target_pairs={{0,224},{32,0},{64,32},{96,64},{128,96},{160,128},{192,160},{224,1... | collective-permute-start | bytes 786440 | tf_op jit(solution)/shard_map/ppermute | solution.py:285
  54.3 7.9 %collective-permute-start.7 = (bf16[512,256]{1,0:T(8,128)(2,1)}, bf16[512,256]{1,0:T(8,128)(2,1)}, u32[]{:S(2)}, u32[]{:S(2)}) collective-permute-start(bf16[512,256]{1,0:T(8,128)(2,1)} %slice.23), channel_id=1, source_target_pairs={{0,32},{32,64},{64,96},{96,128},{128,160},{160,192},{192,224},{224... | collective-permute-start | bytes 786440 | tf_op jit(solution)/shard_map/ppermute | solution.py:285
  67.9 3.6 %collective-permute-start.12 = (bf16[2,1024,256]{2,1,0:T(8,128)(2,1)}, bf16[2,1024,256]{2,1,0:T(8,128)(2,1)}, u32[]{:S(2)}, u32[]{:S(2)}) collective-permute-start(bf16[2,1024,256]{2,1,0:T(8,128)(2,1)} %get-tuple-element.14), channel_id=1, source_target_pairs={{0,1},{1,0},{2,3},{3,2},{4,5},{5,4},{6,7},{7,6},{8,9},{9,8},{10,11... | collective-permute-start | bytes 3145736 | tf_op jit(solution)/shard_map/ppermute | solution.py:331
  68.0 7.6 %collective-permute-start.13 = (bf16[2,1024,256]{2,1,0:T(8,128)(2,1)}, bf16[2,1024,256]{2,1,0:T(8,128)(2,1)S(1)}, u32[]{:S(2)}, u32[]{:S(2)}) collective-permute-start(bf16[2,1024,256]{2,1,0:T(8,128)(2,1)} %get-tuple-element.17), channel_id=1, source_target_pairs={{0,1},{1,0},{2,3},{3,2},{4,5},{5,4},{6,7},{7,6},{8,9},{9,8},{10,11... | collective-permute-start | bytes 3145736 | tf_op jit(solution)/shard_map/ppermute | solution.py:332
  73.4 9.2 %collective-permute-start.15 = (bf16[512,256]{1,0:T(8,128)(2,1)S(1)}, bf16[512,256]{1,0:T(8,128)(2,1)S(1)}, u32[]{:S(2)}, u32[]{:S(2)}) collective-permute-start(bf16[512,256]{1,0:T(8,128)(2,1)S(1)} %get-tuple-element.19), channel_id=1, source_target_pairs={{0,2},{2,4},{4,6},{6,0},{1,3},{3,5},{5,7},{7,1},{8,10},{10,12},{12... | collective-permute-start | bytes 786440 | tf_op jit(solution)/shard_map/ppermute | solution.py:285
  74.8 9.2 %collective-permute-start.16 = (bf16[512,256]{1,0:T(8,128)(2,1)S(1)}, bf16[512,256]{1,0:T(8,128)(2,1)S(1)}, u32[]{:S(2)}, u32[]{:S(2)}) collective-permute-start(bf16[512,256]{1,0:T(8,128)(2,1)S(1)} %get-tuple-element.15), channel_id=1, source_target_pairs={{0,6},{2,0},{4,2},{6,4},{1,7},{3,1},{5,3},{7,5},{8,14},{10,8},{12,... | collective-permute-start | bytes 786440 | tf_op jit(solution)/shard_map/ppermute | solution.py:285
  78.2 12.6 %collective-permute-start.14 = (bf16[512,256]{1,0:T(8,128)(2,1)S(1)}, bf16[512,256]{1,0:T(8,128)(2,1)S(1)}, u32[]{:S(2)}, u32[]{:S(2)}) collective-permute-start(bf16[512,256]{1,0:T(8,128)(2,1)S(1)} %get-tuple-element.18), channel_id=1, source_target_pairs={{0,2},{2,4},{4,6},{6,0},{1,3},{3,5},{5,7},{7,1},{8,10},{10,12},{12... | collective-permute-start | bytes 786440 | tf_op jit(solution)/shard_map/ppermute | solution.py:285
  79.5 11.2 %collective-permute-start.19 = (bf16[512,256]{1,0:T(8,128)(2,1)S(1)}, bf16[512,256]{1,0:T(8,128)(2,1)S(1)}, u32[]{:S(2)}, u32[]{:S(2)}) collective-permute-start(bf16[512,256]{1,0:T(8,128)(2,1)S(1)} %get-tuple-element.22), channel_id=1, source_target_pairs={{0,6},{2,0},{4,2},{6,4},{1,7},{3,1},{5,3},{7,5},{8,14},{10,8},{12,... | collective-permute-start | bytes 786440 | tf_op jit(solution)/shard_map/ppermute | solution.py:285
  86.6 6.5 %collective-permute-start.17 = (bf16[512,256]{1,0:T(8,128)(2,1)S(1)}, bf16[512,256]{1,0:T(8,128)(2,1)S(1)}, u32[]{:S(2)}, u32[]{:S(2)}) collective-permute-start(bf16[512,256]{1,0:T(8,128)(2,1)S(1)} %get-tuple-element.20), channel_id=1, source_target_pairs={{0,2},{2,4},{4,6},{6,0},{1,3},{3,5},{5,7},{7,1},{8,10},{10,12},{12... | collective-permute-start | bytes 786440 | tf_op jit(solution)/shard_map/ppermute | solution.py:285
  87.3 6.9 %collective-permute-start.18 = (bf16[512,256]{1,0:T(8,128)(2,1)S(1)}, bf16[512,256]{1,0:T(8,128)(2,1)S(1)}, u32[]{:S(2)}, u32[]{:S(2)}) collective-permute-start(bf16[512,256]{1,0:T(8,128)(2,1)S(1)} %get-tuple-element.21), channel_id=1, source_target_pairs={{0,6},{2,0},{4,2},{6,4},{1,7},{3,1},{5,3},{7,5},{8,14},{10,8},{12,... | collective-permute-start | bytes 786440 | tf_op jit(solution)/shard_map/ppermute | solution.py:285
  (1 other events, 8.7 us)
